TPU v7x, 32 devices: a whole 2x2x4 slice. The times are simulated.
32 devices in a mesh: dp: 4 (over x, core), context: 2 (over y), tensor: 4 (over z).
Axes of the slice: x: 2, y: 2, z: 4, core: 2. Of those that a mesh axis runs over, the one named last changes fastest.
Arguments:
- grad_out: bfloat16 [4096, 8192], P(('dp', 'context', 'tensor')), may hold values from -6 to 6
- queries: bfloat16 [4096, 1024], P(('dp', 'context'), 'tensor'), may hold values from -6 to 6
- attended: bfloat16 [4096, 1024], P(('dp', 'context'), 'tensor'), may hold values from -6 to 6
- keys: bfloat16 [4096, 128], P(('dp', 'context')), may hold values from -6 to 6
- values: bfloat16 [4096, 128], P(('dp', 'context')), may hold values from -6 to 6
- log_sums: float32 [8, 4096], P('tensor', ('dp', 'context')), may hold values from 1 to 3
- segment_ids: int32 [4, 1024], P('dp'), may hold values from 0 to 7, as said below
- w_out: bfloat16 [8192, 1024], P(('dp', 'context'), 'tensor'), may hold values from -0.0625 to 0.0625
- w_query: bfloat16 [1024, 8192], P('tensor', ('dp', 'context')), may hold values from -0.1875 to 0.1875
- w_key: bfloat16 [128, 8192], replicated, may hold values from -0.5 to 0.5
- w_value: bfloat16 [128, 8192], replicated, may hold values from -0.5 to 0.5
Outputs:
- grad_input: bfloat16 [4096, 8192], P(('dp', 'context', 'tensor'))
- out_proj_grad: float32 [8192, 1024], P(('dp', 'context'), 'tensor')
Inputs may be any that keep to these rules, and one draw needn't show every extreme that they name: `segment_ids`: along the positions of a sequence the document number never falls; every sequence holds exactly 8 documents, numbered from 0.
All inputs are finite; a program needn't handle non-finite values.
Results may differ from a plain program's by a relative error of at most 0.02.
Values may be sent and summed in bfloat16 or wider, within the bound.
No kernel may reach another device: no remote copies, remote signals or barrier semaphores. Data moves between devices by JAX's collectives and lax.ppermute only.
A program may use at most 128 MiB of HBM per device.

v0:
```python
import math

import jax
import jax.numpy as jnp
from jax import lax
from jax.sharding import PartitionSpec as P


def extended_2(x, sides, width):
    for axis, dim in sides:
        peers, length = (lax.axis_size(axis), x.shape[dim])
        up = [(i, (i + 1) % peers) for i in range(peers - 1)]
        down = [(j, i) for i, j in up]
        last = lax.slice_in_dim(x, length - width, length, axis=dim)
        initial = lax.slice_in_dim(x, 0, width, axis=dim)
        before = lax.ppermute(last, axis, up)
        after = lax.ppermute(initial, axis, down)
        x = jnp.concatenate([before, x, after], axis=dim)
    return x


def on_device(
    grad_out, queries, attended, keys, values, log_sums, segment_ids, w_out, w_query, w_key, w_value
):
    token_grads = lax.all_gather(grad_out, "tensor", axis=0, tiled=True)
    out_full, query_full = (
        lax.all_gather(w_out, ("dp", "context"), axis=0, tiled=True),
        lax.all_gather(w_query, ("dp", "context"), axis=1, tiled=True),
    )
    attn_grads = jnp.dot(token_grads, out_full, preferred_element_type=jnp.float32).astype(
        jnp.bfloat16
    )
    out_proj_grad = lax.psum_scatter(
        lax.dot_general(
            token_grads, attended, (((0,), (0,)), ((), ())), preferred_element_type=jnp.float32
        ),
        ("dp", "context"),
        scatter_dimension=0,
        tiled=True,
    )
    span_len = queries.shape[0] // 2
    head_dim = keys.shape[1]
    heads_here = queries.shape[1] // head_dim
    inv_root = 1.0 / math.sqrt(head_dim)
    cycle_size = lax.axis_size("context")
    cycle_pos = lax.axis_index("context")
    high_span = 2 * cycle_size - 1 - cycle_pos
    last_rank = cycle_pos == cycle_size - 1
    kv_pair = jnp.concatenate([keys, values], axis=1)
    flipped = jnp.concatenate([kv_pair[span_len:], kv_pair[:span_len]], axis=0)
    extended = extended_2(flipped, (("context", 0),), span_len)
    left_low = extended[:span_len]
    right_high = extended[3 * span_len :]
    own_low = kv_pair[:span_len]
    own_high = kv_pair[span_len:]
    prev_high = jnp.where(last_rank, own_low, right_high)
    block_kv = jnp.stack(
        [
            jnp.concatenate([left_low, own_low], axis=0),
            jnp.concatenate([prev_high, own_high], axis=0),
        ]
    )
    key_blk = block_kv[:, :, :head_dim]
    value_blk = block_kv[:, :, head_dim:]
    offsets = jnp.arange(span_len, dtype=jnp.int32)
    query_spans = jnp.stack([cycle_pos, high_span])
    query_pos = query_spans[:, None] * span_len + offsets[None, :]
    key_pos = jnp.concatenate([query_pos - span_len, query_pos], axis=1)
    seg_row = segment_ids[0]

    def seg_slice(span_idx):
        return lax.dynamic_slice_in_dim(seg_row, jnp.maximum(span_idx, 0) * span_len, span_len)

    seg_query = jnp.stack([seg_slice(cycle_pos), seg_slice(high_span)])
    seg_key = jnp.stack(
        [
            jnp.concatenate([seg_slice(cycle_pos - 1), seg_query[0]]),
            jnp.concatenate([seg_slice(high_span - 1), seg_query[1]]),
        ]
    )
    allowed = (
        (key_pos[:, None, :] <= query_pos[:, :, None])
        & (key_pos[:, None, :] >= 0)
        & (seg_key[:, None, :] == seg_query[:, :, None])
    )
    query_blk = queries.reshape(2, span_len, heads_here, head_dim)
    dout_blk = attn_grads.reshape(2, span_len, heads_here, head_dim)
    log_rows = log_sums.reshape(heads_here, 2, span_len).transpose(1, 0, 2)
    row_delta = (
        (attn_grads.astype(jnp.float32) * attended.astype(jnp.float32))
        .reshape(2, span_len, heads_here, head_dim)
        .sum(axis=3)
    )
    row_delta = row_delta.transpose(0, 2, 1)
    scores = (
        jnp.einsum("bqhe,bke->bhqk", query_blk, key_blk, preferred_element_type=jnp.float32)
        * inv_root
    )
    prob_full = jnp.where(allowed[:, None], jnp.exp(scores - log_rows[..., None]), 0.0)
    prob_low = prob_full.astype(jnp.bfloat16)
    dprobs = jnp.einsum("bqhe,bke->bhqk", dout_blk, value_blk, preferred_element_type=jnp.float32)
    dscores = (prob_full * (dprobs - row_delta[..., None])).astype(jnp.bfloat16)
    dquery = (
        jnp.einsum("bhqk,bke->bqhe", dscores, key_blk, preferred_element_type=jnp.float32)
        * inv_root
    ).astype(jnp.bfloat16)
    key_grads = (
        jnp.einsum("bhqk,bqhe->bke", dscores, query_blk, preferred_element_type=jnp.float32)
        * inv_root
    )
    value_grads = jnp.einsum(
        "bhqk,bqhe->bke", prob_low, dout_blk, preferred_element_type=jnp.float32
    )
    kv_block_grads = jnp.concatenate([key_grads, value_grads], axis=2)
    to_left = kv_block_grads[0, :span_len]
    to_right = jnp.where(last_rank, 0.0, kv_block_grads[1, :span_len])
    own_low_grads = kv_block_grads[0, span_len:] + jnp.where(
        last_rank, kv_block_grads[1, :span_len], 0.0
    )
    returned = extended_2(
        jnp.concatenate([to_left, to_right], axis=0).astype(jnp.bfloat16),
        (("context", 0),),
        span_len,
    ).astype(jnp.float32)
    low_summed = own_low_grads + returned[3 * span_len :]
    high_summed = kv_block_grads[1, span_len:] + returned[:span_len]
    kv_grads = jnp.concatenate([low_summed, high_summed], axis=0).astype(jnp.bfloat16)
    query_grads = dquery.reshape(2 * span_len, heads_here * head_dim)
    summed = jnp.dot(query_grads, query_full, preferred_element_type=jnp.float32)
    summed = summed + jnp.dot(kv_grads[:, :head_dim], w_key, preferred_element_type=jnp.float32)
    summed = summed + jnp.dot(kv_grads[:, head_dim:], w_value, preferred_element_type=jnp.float32)
    grad_input = lax.psum_scatter(
        summed.astype(jnp.bfloat16), "tensor", scatter_dimension=0, tiled=True
    )
    return (grad_input, out_proj_grad)


def solution(mesh):
    placed = (
        P(("dp", "context", "tensor"), None),
        P(("dp", "context"), "tensor"),
        P(("dp", "context"), "tensor"),
        P(("dp", "context"), None),
        P(("dp", "context"), None),
        P("tensor", ("dp", "context")),
        P("dp", None),
        P(("dp", "context"), "tensor"),
        P("tensor", ("dp", "context")),
        P(),
        P(),
    )
    return jax.shard_map(
        on_device,
        mesh=mesh,
        in_specs=placed,
        out_specs=(P(("dp", "context", "tensor"), None), P(("dp", "context"), "tensor")),
        check_vma=False,
    )
```

profile of v0, /device:TPU:0, one launch (start us, length us, event | category | flops | bytes accessed | tf_op | source)
XLA Modules:
  0.0 470.3 jit_solution(14566120997354077468)
XLA Ops:
  7.2 0.0 copy-start
  7.2 0.0 all-gather.4.cloned.1.call-start
  7.2 0.7 all-gather.4.cloned.1.call-update
  7.9 0.0 all-gather.6.cloned.1.call-start
  8.0 0.7 all-gather.6.cloned.1.call-update
  8.7 0.0 all-gather.8.cloned.1.call-start
  8.7 0.7 all-gather.8.cloned.1.call-update
  9.4 0.0 reduce-scatter.5.cloned.1.call-start
  9.4 152.5 %all-gather.4.cloned.1.call-done = bf16[512,8192]{1,0:T(8,128)(2,1)} async-done(((bf16[128,8192]{1,0:T(8,128)(2,1)}), bf16[512,8192]{1,0:T(8,128)(2,1)}) %all-gather.4.cloned.1.call-update) | async-done | bytes 8388624 | tf_op jit(solution)/shard_map/all_gather | solution.py:25
  162.0 9.0 %fusion.40 = f32[8192,256]{1,0:T(8,128)} fusion(bf16[512,8192]{1,0:T(8,128)(2,1)} %all-gather.4.cloned.1.call-done, bf16[512,256]{1,0:T(8,128)(2,1)} %param.13), kind=kOutput, calls=%fused_computation.80 | convolution fusion | flops 2147483648 | bytes 17039360 | tf_op jit(solution)/shard_map/dot_general | solution.py:34
  171.0 0.0 copy-start.10
  171.0 0.0 reduce-scatter.5.cloned.1.call-update
  171.1 0.0 reduce-scatter.3.cloned.1.call-start
  171.1 0.8 copy-done.7
  171.9 0.0 copy-done.8
  172.0 1.3 collective-permute-start.1
  173.3 0.1 add_multiply_fusion
  173.5 0.1 broadcast_add_fusion
  173.5 7.5 %collective-permute-done.1 = bf16[256,256]{1,0:T(8,128)(2,1)S(1)} collective-permute-done((bf16[256,256]{1,0:T(8,128)(2,1)S(1)}, bf16[256,256]{1,0:T(8,128)(2,1)S(1)}, u32[]{:S(2)}, u32[]{:S(2)}) %collective-permute-start.1) | collective-permute-done | bytes 131104 | tf_op jit(solution)/shard_map/ppermute | solution.py:17
  181.0 1.5 collective-permute-start
  182.5 1.2 compare_and_fusion
  183.7 0.1 reshape.104
  183.8 0.1 copy.40
  184.0 1.3 collective-permute-done
  185.4 2.9 fusion.3
  188.3 13.3 %all-gather.6.cloned.1.call-done = bf16[8192,256]{1,0:T(8,128)(2,1)} async-done(((bf16[1024,256]{1,0:T(8,128)(2,1)}), bf16[8192,256]{1,0:T(8,128)(2,1)}) %all-gather.6.cloned.1.call-update) | async-done | bytes 4194320 | tf_op jit(solution)/shard_map/all_gather | solution.py:27
  201.6 7.9 %convert_multiply_fusion = (f32[512,256]{1,0:T(8,128)}, bf16[512,256]{1,0:T(8,128)(2,1)}) fusion(bf16[512,256]{1,0:T(8,128)(2,1)} %param.13, bf16[512,8192]{1,0:T(8,128)(2,1)} %all-gather.4.cloned.1.call-done, bf16[8192,256]{1,0:T(8,128)(2,1)} %all-gather.6.cloned.1.call-done), kind=kOutput, calls=%fused_computation.24 | convolution fusion | flops 2148007936 | bytes 13631488 | tf_op jit(solution)/shard_map/dot_general | solution.py:30
  209.5 1.3 reshape.107
  210.8 0.6 reduce_sum.9
  211.5 0.1 copy.35
  211.6 1.1 reshape.106
  212.6 0.1 copy.42
  212.8 2.2 convolution_bitcast_fusion
  215.0 0.4 fusion.1
  215.5 1.4 fusion.4
  216.9 0.7 fusion.26
  217.6 3.8 collective-permute-start.2
  221.4 1.5 collective-permute-start.3
  222.9 2.0 fusion.6
  224.9 1.2 copy.38
  226.1 5.5 %collective-permute-done.3 = bf16[256,256]{0,1:T(8,128)(2,1)} collective-permute-done((bf16[256,256]{0,1:T(8,128)(2,1)}, bf16[256,256]{0,1:T(8,128)(2,1)}, u32[]{:S(2)}, u32[]{:S(2)}) %collective-permute-start.3) | collective-permute-done | bytes 131104 | tf_op jit(solution)/shard_map/ppermute | solution.py:17
  231.6 1.1 fusion.16
  232.6 8.1 %fusion.30 = f32[512,8192]{1,0:T(8,128)} fusion(bf16[128,8192]{1,0:T(8,128)(2,1)S(1)} %copy-done, bf16[256,256]{0,1:T(8,128)(2,1)S(1)} %get-tuple-element.3, bf16[256,256]{0,1:T(8,128)(2,1)S(1)} %get-tuple-element.2), kind=kOutput, calls=%fused_computation.53 | convolution fusion | flops 1074003968 | bytes 19136512 | tf_op jit(solution)/shard_map/dot_general | solution.py:131
  240.7 8.1 %fusion.28 = f32[512,8192]{1,0:T(8,128)} fusion(bf16[128,8192]{1,0:T(8,128)(2,1)S(1)} %copy-done.4, bf16[256,256]{0,1:T(8,128)(2,1)S(1)} %get-tuple-element.2, bf16[256,256]{0,1:T(8,128)(2,1)S(1)} %get-tuple-element.3), kind=kOutput, calls=%fused_computation.51 | convolution fusion | flops 1074003968 | bytes 19136512 | tf_op jit(solution)/shard_map/dot_general | solution.py:130
  248.8 20.5 %add_convert_fusion = bf16[512,8192]{1,0:T(8,128)(2,1)} fusion(f32[512,8192]{1,0:T(8,128)} %fusion.30, f32[512,8192]{1,0:T(8,128)} %fusion.28, bf16[256,8192]{1,0:T(8,128)(2,1)} %all-gather.8.cloned.1.call-done, bf16[64,8,2,128]{3,2,1,0:T(2,128)(2,1)S(1)} %bitcast.86), kind=kOutput, calls=%fused_computation | convolution fusion | flops 2160066560 | bytes 46399488 | tf_op jit(solution)/shard_map/dot_general | solution.py:129
  269.4 0.0 reduce-scatter.3.cloned.1.call-update
  269.4 47.0 %reduce-scatter.5.cloned.1.call-done = f32[1024,256]{1,0:T(8,128)} async-done(((f32[8192,256]{1,0:T(8,128)}), f32[1024,256]{1,0:T(8,128)}) %reduce-scatter.5.cloned.1.call-update) | async-done | bytes 1048592 | tf_op jit(solution)/shard_map/reduce_scatter | solution.py:33
  316.4 147.4 %reduce-scatter.3.cloned.1.call-done = bf16[128,8192]{1,0:T(8,128)(2,1)} async-done(((bf16[512,8192]{1,0:T(8,128)(2,1)}), bf16[128,8192]{1,0:T(8,128)(2,1)}) %reduce-scatter.3.cloned.1.call-update) | async-done | bytes 2097168 | tf_op jit(solution)/shard_map/reduce_scatter | solution.py:132
  (32 shorter events, 0.2 us)
Async XLA Ops:
  7.2 225.5 %copy-start = (bf16[128,8192]{1,0:T(8,128)(2,1)S(1)}, bf16[128,8192]{1,0:T(8,128)(2,1)}, u32[]{:S(2)}) copy-start(bf16[128,8192]{1,0:T(8,128)(2,1)} %param.21) | copy-start | bytes 6291460
  7.2 154.8 %all-gather.4.cloned.1.call-start = ((), (), s32[]{:S(2)}) async-start(), calls=%async_computation.2 | async-start | bytes 10485760 | tf_op jit(solution)/shard_map/all_gather | solution.py:25
  7.9 193.7 %all-gather.6.cloned.1.call-start = ((), (), s32[]{:S(2)}) async-start(), calls=%async_computation.3 | async-start | bytes 4718592 | tf_op jit(solution)/shard_map/all_gather | solution.py:27
  8.7 240.2 %all-gather.8.cloned.1.call-start = ((), (), s32[]{:S(2)}) async-start(), calls=%async_computation.4 | async-start | bytes 4718592 | tf_op jit(solution)/shard_map/all_gather | solution.py:28
  9.4 307.0 %reduce-scatter.5.cloned.1.call-start = ((), (), s32[]{:S(2)}) async-start(), calls=%async_computation.6 | async-start | bytes 9437184 | tf_op jit(solution)/shard_map/reduce_scatter | solution.py:33
  171.0 0.9 copy-start.7
  171.0 1.0 copy-start.8
  171.0 2.4 copy-start.9
  171.0 12.7 %copy-start.6 = (bf16[512,256]{1,0:T(8,128)(2,1)S(1)}, bf16[512,256]{1,0:T(8,128)(2,1)}, u32[]{:S(2)}) copy-start(bf16[512,256]{1,0:T(8,128)(2,1)} %param.12) | copy-start | bytes 786436
  171.0 14.4 %copy-start.10 = (f32[2,512]{1,0:T(2,128)S(1)}, f32[2,512]{1,0:T(2,128)}, u32[]{:S(2)}) copy-start(f32[2,512]{1,0:T(2,128)} %param.16) | copy-start | bytes 12292
  171.1 292.7 %reduce-scatter.3.cloned.1.call-start = ((), (), s32[]{:S(2)}) async-start(), calls=%async_computation.5 | async-start | bytes 10485760 | tf_op jit(solution)/shard_map/reduce_scatter | solution.py:132
  172.0 9.0 %collective-permute-start.1 = (bf16[256,256]{1,0:T(8,128)(2,1)S(1)}, bf16[256,256]{1,0:T(8,128)(2,1)S(1)}, u32[]{:S(2)}, u32[]{:S(2)}) collective-permute-start(bf16[256,256]{1,0:T(8,128)(2,1)S(1)} %slice.55), channel_id=1, source_target_pairs={{4,0},{5,1},{6,2},{7,3},{12,8},{13,9},{14,10},{15,11},{20,16},{21,... | collective-permute-start | bytes 393224 | tf_op jit(solution)/shard_map/ppermute | solution.py:17
  181.0 4.3 collective-permute-start
  184.0 25.6 %copy-start.5 = (bf16[2,256,2,128]{1,3,2,0:T(8,128)(2,1)}, bf16[2,256,2,128]{1,3,2,0:T(8,128)(2,1)S(1)}, u32[]{:S(2)}) copy-start(bf16[2,256,2,128]{1,3,2,0:T(8,128)(2,1)S(1)} %copy.40) | copy-start | bytes 786436
  185.4 29.7 %copy-start.3 = (bf16[1,512,256]{2,1,0:T(8,128)(2,1)}, bf16[1,512,256]{2,1,0:T(8,128)(2,1)S(1)}, u32[]{:S(2)}) copy-start(bf16[1,512,256]{2,1,0:T(8,128)(2,1)S(1)} %maximum_bitcast_fusion) | copy-start | bytes 786436
  212.8 2.2 copy-start.2
  217.6 8.5 %collective-permute-start.2 = (bf16[256,256]{0,1:T(8,128)(2,1)S(1)}, bf16[256,256]{0,1:T(8,128)(2,1)}, u32[]{:S(2)}, u32[]{:S(2)}) collective-permute-start(bf16[256,256]{0,1:T(8,128)(2,1)S(1)} %get-tuple-element.4), channel_id=1, source_target_pairs={{0,4},{1,5},{2,6},{3,7},{8,12},{9,13},{10,14},{11,15},{16,20},{17,... | collective-permute-start | bytes 393224 | tf_op jit(solution)/shard_map/ppermute | solution.py:16
  221.4 10.1 %collective-permute-start.3 = (bf16[256,256]{0,1:T(8,128)(2,1)}, bf16[256,256]{0,1:T(8,128)(2,1)}, u32[]{:S(2)}, u32[]{:S(2)}) collective-permute-start(bf16[256,256]{0,1:T(8,128)(2,1)} %get-tuple-element.5), channel_id=1, source_target_pairs={{4,0},{5,1},{6,2},{7,3},{12,8},{13,9},{14,10},{15,11},{20,16},{21,... | collective-permute-start | bytes 393224 | tf_op jit(solution)/shard_map/ppermute | solution.py:17
  232.6 8.1 %copy-start.4 = (bf16[128,8192]{1,0:T(8,128)(2,1)S(1)}, bf16[128,8192]{1,0:T(8,128)(2,1)}, u32[]{:S(2)}) copy-start(bf16[128,8192]{1,0:T(8,128)(2,1)} %param.20) | copy-start | bytes 6291460
  269.4 194.4 %copy-start.1 = (bf16[128,8192]{1,0:T(8,128)(2,1)S(1)}, bf16[128,8192]{1,0:T(8,128)(2,1)}, u32[]{:S(2)}) copy-start(bf16[128,8192]{1,0:T(8,128)(2,1)} %param.21) | copy-start | bytes 6291460
Sparse Core Ops, SparseCore 0:
  9.6 152.3 all-gather.3
  163.8 37.7 all-gather.5
  203.5 38.2 all-gather.7
  245.7 70.5 reduce-scatter.4
  319.3 144.4 reduce-scatter.2
where the time goes:
time: 471 us; the launch traced here: 470 us
  waiting for transfers between devices  377 us (80%)
  matrix products  62.6 us (13%)
  between operations  14 us (3%)
  starting transfers between devices  8.23 us (2%)
  local copies, waits for them, and re-layouts  5.02 us (1%)
    all_gather x1, waiting for transfers between devices, on_device(): token_grads = lax.all_gather(grad_out, 'tensor', axis=0, tiled=True)  153 us
    reduce_scatter x1, waiting for transfers between devices, on_device(): lax.psum_scatter(summed.astype(jnp.bfloat16), 'tensor', scatter_dimension...  147 us
    reduce_scatter x1, waiting for transfers between devices, on_device(): lax.psum_scatter(lax.dot_general(token_grads, attended, (((0,), (0,)), ((...  47 us
    dot_general x1, matrix products, on_device(): jnp.dot(query_grads, query_full, preferred_element_type=jnp.float32)  20.5 us
    all_gather x1, waiting for transfers between devices, on_device(): lax.all_gather(w_out, ('dp', 'context'), axis=0, tiled=True)  13.3 us
    ppermute x2, waiting for transfers between devices, extended_2(): after = lax.ppermute(initial, axis, down)  12.9 us
  transfers between devices with their start and end apart: 9, of which 7 were waited for; matrix products, arithmetic and copies ran while one was open for 15% of the time, Pallas kernels for 0%

commit v1 on v0

v1 whole, which is shorter than its diff:
```python
import functools
import math

import jax
import jax.numpy as jnp
from jax import lax
from jax.experimental import pallas as pl
from jax.experimental.pallas import tpu as pltpu
from jax.sharding import PartitionSpec as P

PLANE = ("dp", "context")
BF16 = jnp.bfloat16
F32 = jnp.float32


def swapped(x, axes, bit):
    size = lax.axis_size(axes)
    return lax.ppermute(x, axes, [(i, i ^ bit) for i in range(size)])


def neighbours(to_left, to_right):
    size, rank = lax.axis_size("context"), lax.axis_index("context")
    if size == 2:
        got = swapped(jnp.where(rank == 0, to_right, to_left), "context", 1)
        none = jnp.zeros_like(got)
        return jnp.where(rank == 0, none, got), jnp.where(rank == 0, got, none)
    up = [(i, i + 1) for i in range(size - 1)]
    down = [(i + 1, i) for i in range(size - 1)]
    return lax.ppermute(to_right, "context", up), lax.ppermute(to_left, "context", down)


def plane_bits():
    low, size = lax.axis_size("context"), lax.axis_size(PLANE)
    bits = [1 << i for i in range(size.bit_length() - 1)]
    return [low] + [b for b in reversed(bits) if b != low]


def plane_order():
    order = [0]
    for bit in reversed(plane_bits()):
        order = order + [k ^ bit for k in order]
    return order


def plane_exchange(blocks):
    order = plane_order()
    if len(order) <= 8:
        return [b if k == 0 else swapped(b, PLANE, k) for k, b in zip(order, blocks)]
    rank = lax.axis_index(PLANE)
    places = jnp.array(order, jnp.int32)
    inverse = jnp.argsort(places)
    stacked = jnp.stack(blocks)[inverse[jnp.arange(len(order)) ^ rank]]
    got = lax.all_to_all(stacked, PLANE, 0, 0, tiled=True)[places ^ rank]
    return [got[p] for p in range(len(order))]


def halves_orders(bits):
    return [bits[1:], bits[:0:-1]]


def plane_sum(parts, rows):
    bits, order = plane_bits(), plane_order()
    half = parts.shape[0] // 2
    got = swapped(parts[half:].astype(BF16), PLANE, bits[0])
    parts = parts[:half] + got.astype(F32)
    columns = parts.shape[1] // 2
    sums = []
    for side, path in enumerate(halves_orders(bits)):
        now = {
            k: parts[p * rows : (p + 1) * rows, side * columns : (side + 1) * columns]
            for p, k in enumerate(order[: len(order) // 2])
        }
        for bit in path:
            away = [k for k in now if k & bit]
            got = swapped(
                jnp.concatenate([now[k].astype(BF16) for k in away], axis=0), PLANE, bit
            )
            for i, k in enumerate(away):
                now[k ^ bit] = now[k ^ bit] + got[i * rows : (i + 1) * rows].astype(F32)
                del now[k]
        sums.append(now[0])
    return jnp.concatenate(sums, axis=1)


def plane_gather(x):
    bits, order = plane_bits(), plane_order()
    columns = x.shape[1] // 2
    sides = []
    for side, path in enumerate(halves_orders(bits)):
        held = {0: x[:, side * columns : (side + 1) * columns]}
        for bit in path:
            keys = list(held)
            got = swapped(jnp.concatenate([held[k] for k in keys], axis=0), PLANE, bit)
            for i, k in enumerate(keys):
                held[k ^ bit] = got[i * x.shape[0] : (i + 1) * x.shape[0]]
        sides.append(
            jnp.concatenate([held[k] for k in order[: len(order) // 2]], axis=0)
        )
    first = jnp.concatenate(sides, axis=1)
    return first, swapped(first, PLANE, bits[0])


def attention_kernel(
    tensor_ref, seg_query_ref, seg_key_ref, query_ref, dout_ref, attended_ref, kv_ref, log_ref,
    dquery_ref, kv_grads_ref, *, head_dim, peers,
):
    rank = tensor_ref[0]
    span = query_ref.shape[0] // 2
    heads = query_ref.shape[1] // head_dim
    sub = 2 * span // peers
    inv_root = 1.0 / math.sqrt(head_dim)

    def place(a):
        return pl.ds(pl.multiple_of(lax.bitwise_xor(rank, a) * sub, sub), sub)

    def by_head(x):
        return jnp.concatenate(
            [x[:, h * head_dim : (h + 1) * head_dim] for h in range(heads)], axis=0
        )

    def contract(x, y, dims):
        return lax.dot_general(x, y, (dims, ((), ())), preferred_element_type=F32)

    for b in range(2):
        rows = slice(b * span, (b + 1) * span)
        subs = range(b * peers // 2, (b + 1) * peers // 2)
        query = by_head(query_ref[rows, :])
        dout = by_head(jnp.concatenate([dout_ref[place(a), :] for a in subs], axis=0))
        attended = by_head(attended_ref[rows, :])
        key = kv_ref[b, :, :head_dim]
        value = kv_ref[b, :, head_dim:]
        log_rows = jnp.concatenate([log_ref[rows, h : h + 1] for h in range(heads)], axis=0)
        query_at = lax.broadcasted_iota(jnp.int32, (span, 2 * span), 0)
        key_at = lax.broadcasted_iota(jnp.int32, (span, 2 * span), 1) - span
        allowed = (key_at <= query_at) & (seg_query_ref[rows, :] == seg_key_ref[b : b + 1, :])
        allowed = jnp.concatenate([allowed] * heads, axis=0)
        scores = contract(query, key, ((1,), (1,))) * inv_root
        prob = jnp.where(allowed, jnp.exp(scores - log_rows), 0.0)
        delta = jnp.sum(
            dout.astype(F32) * attended.astype(F32), axis=1, keepdims=True
        )
        dprob = contract(dout, value, ((1,), (1,)))
        dscore = (prob * (dprob - delta)).astype(BF16)
        dquery = (contract(dscore, key, ((1,), (0,))) * inv_root).astype(BF16)
        for i, a in enumerate(subs):
            for h in range(heads):
                dquery_ref[place(a), h * head_dim : (h + 1) * head_dim] = dquery[
                    h * span + i * sub : h * span + (i + 1) * sub
                ]
        kv_grads_ref[b, :, :head_dim] = contract(dscore, query, ((0,), (0,))) * inv_root
        kv_grads_ref[b, :, head_dim:] = contract(prob.astype(BF16), dout, ((0,), (0,)))


def attention(rank, seg_query, seg_key, queries, dout, attended, kv, log_sums, head_dim, peers):
    vmem = pl.BlockSpec(memory_space=pltpu.VMEM)
    span = queries.shape[0] // 2
    heads = queries.shape[1] // head_dim
    pairs = 2 * heads * span * 2 * span
    return pl.pallas_call(
        functools.partial(attention_kernel, head_dim=head_dim, peers=peers),
        out_shape=(
            jax.ShapeDtypeStruct(queries.shape, BF16),
            jax.ShapeDtypeStruct(kv.shape, F32),
        ),
        in_specs=[pl.BlockSpec(memory_space=pltpu.SMEM)] + [vmem] * 7,
        out_specs=(vmem, vmem),
        compiler_params=pltpu.CompilerParams(vmem_limit_bytes=32 * 2**20),
        cost_estimate=pl.CostEstimate(
            flops=10 * pairs * head_dim, bytes_accessed=3 * 2**20, transcendentals=pairs
        ),
        name="attention",
    )(rank, seg_query, seg_key, queries, dout, attended, kv, log_sums)


def on_device(
    grad_out, queries, attended, keys, values, log_sums, segment_ids, w_out, w_query, w_key, w_value
):
    peers = lax.axis_size("tensor")
    tensor_rank = lax.axis_index("tensor")
    plane_rank = lax.axis_index(PLANE)
    cycle_size, cycle_pos = lax.axis_size("context"), lax.axis_index("context")
    last_rank = cycle_pos == cycle_size - 1
    own_rows, features = grad_out.shape
    width = w_out.shape[0]
    cols = queries.shape[1]
    span = queries.shape[0] // 2
    head_dim = keys.shape[1]
    order = plane_order()

    def own_block(x, rank, size, axis):
        return lax.dynamic_slice_in_dim(x, rank * size, size, axis=axis)

    w_out_all = [w_out] + [swapped(w_out, "tensor", j) for j in range(1, peers)]
    tokens = plane_exchange([own_block(grad_out, plane_rank ^ k, width, 1) for k in order])
    tokens = jnp.concatenate(tokens, axis=0)

    kv_pair = jnp.concatenate([keys, values], axis=1)
    own_low, own_high = kv_pair[:span], kv_pair[span:]
    left_low, right_high = neighbours(own_high, own_low)
    kv = jnp.stack(
        [
            jnp.concatenate([left_low, own_low], axis=0),
            jnp.concatenate([jnp.where(last_rank, own_low, right_high), own_high], axis=0),
        ]
    )
    seg_row = segment_ids[0]
    high_span = 2 * cycle_size - 1 - cycle_pos

    def seg_slice(at):
        return lax.dynamic_slice_in_dim(seg_row, jnp.maximum(at, 0) * span, span)

    seg_low, seg_high = seg_slice(cycle_pos), seg_slice(high_span)
    seg_before = jnp.where(cycle_pos == 0, -1, seg_slice(cycle_pos - 1))
    seg_query = jnp.concatenate([seg_low, seg_high])[:, None]
    seg_key = jnp.stack(
        [
            jnp.concatenate([seg_before, seg_low]),
            jnp.concatenate([seg_slice(high_span - 1), seg_high]),
        ]
    )
    log_rows = log_sums.T

    partial_attn = jnp.dot(
        tokens, jnp.concatenate(w_out_all, axis=1), preferred_element_type=F32
    )
    attn_own = plane_sum(partial_attn, own_rows).astype(BF16)
    dout = jnp.concatenate(
        [attn_own[:, :cols]]
        + [swapped(attn_own[:, j * cols : (j + 1) * cols], "tensor", j) for j in range(1, peers)],
        axis=0,
    )
    dquery, kv_grads = attention(
        tensor_rank.reshape(1), seg_query, seg_key, queries, dout, attended, kv, log_rows,
        head_dim, peers,
    )

    before_low, before_high = kv_grads[0, :span], kv_grads[1, :span]
    from_left, from_right = neighbours(
        before_low.astype(BF16), jnp.where(last_rank, 0.0, before_high).astype(BF16)
    )
    low = kv_grads[0, span:] + jnp.where(last_rank, before_high, 0.0) + from_right.astype(F32)
    high = kv_grads[1, span:] + from_left.astype(F32)
    kv_grads = jnp.concatenate([low, high], axis=0).astype(BF16)

    sent = [
        jnp.concatenate(
            [
                dquery[j * own_rows : (j + 1) * own_rows],
                own_block(kv_grads, tensor_rank ^ j, own_rows, 0),
            ],
            axis=1,
        )
        for j in range(peers)
    ]
    got = [sent[0]] + [swapped(sent[j], "tensor", j) for j in range(1, peers)]
    kv_own = sum(g[:, cols:].astype(F32) for g in got).astype(BF16)
    inner_own = jnp.concatenate([g[:, :cols] for g in got] + [kv_own], axis=1)
    inner = plane_gather(inner_own)
    w_in = jnp.concatenate(
        [w_query]
        + [swapped(w_query, "tensor", j) for j in range(1, peers)]
        + [own_block(w_key, plane_rank, width, 1), own_block(w_value, plane_rank, width, 1)],
        axis=0,
    )
    grads = [jnp.dot(x, w_in, preferred_element_type=F32).astype(BF16) for x in inner]
    blocks = [g[i * own_rows : (i + 1) * own_rows] for g in grads for i in range(len(order) // 2)]
    blocks = plane_exchange(blocks)
    grad_input = jnp.zeros((own_rows, features), BF16)
    for k, block in zip(order, blocks):
        grad_input = lax.dynamic_update_slice_in_dim(
            grad_input, block, (plane_rank ^ k) * width, axis=1
        )

    attended_own = [own_block(attended, tensor_rank ^ j, own_rows, 0) for j in range(peers)]
    attended_own = jnp.concatenate(
        [attended_own[0]] + [swapped(attended_own[j], "tensor", j) for j in range(1, peers)],
        axis=1,
    )
    attended_all = jnp.concatenate(plane_gather(attended_own), axis=0)
    partial_out = lax.dot_general(
        tokens, attended_all, (((0,), (0,)), ((), ())), preferred_element_type=F32
    )
    out_proj_grad = partial_out[:, :cols]
    for j in range(1, peers):
        out_proj_grad = out_proj_grad + swapped(
            partial_out[:, j * cols : (j + 1) * cols].astype(BF16), "tensor", j
        ).astype(F32)
    return (grad_input, out_proj_grad)


def solution(mesh):
    placed = (
        P(("dp", "context", "tensor"), None),
        P(("dp", "context"), "tensor"),
        P(("dp", "context"), "tensor"),
        P(("dp", "context"), None),
        P(("dp", "context"), None),
        P("tensor", ("dp", "context")),
        P("dp", None),
        P(("dp", "context"), "tensor"),
        P("tensor", ("dp", "context")),
        P(),
        P(),
    )
    return jax.shard_map(
        on_device,
        mesh=mesh,
        in_specs=placed,
        out_specs=(P(("dp", "context", "tensor"), None), P(("dp", "context"), "tensor")),
        check_vma=False,
    )
```

time: 471 us -> 227 us (0.48)
  waiting for transfers between devices: 377 us -> 128 us
  matrix products: 62.6 us -> 9.34 us
  starting transfers between devices: 8.23 us -> 59.3 us
  local copies, waits for them, and re-layouts: 5.02 us -> 18.6 us
  between operations: 14 us -> 1.29 us
    reduce_scatter x2 -> x0, waiting for transfers between devices: 194 us -> none  [the longest x1 147 us: on_device(): lax.psum_scatter(summed.astype(jnp.bfloat16), 'tensor', scatter_dimension...]
    all_gather x3 -> x0, waiting for transfers between devices: 166 us -> none  [the longest x1 153 us: on_device(): token_grads = lax.all_gather(grad_out, 'tensor', axis=0, tiled=True)]
    ppermute x4 -> x49, waiting for transfers between devices: 14.3 us -> 128 us  [swapped(): return lax.ppermute(x, axes, [(i, i ^ bit) for i in range(size)])]
    dot_general x10 -> x4, matrix products: 62.6 us -> 9.34 us  [the longest x1 3.93 us: on_device(): jnp.dot(tokens, jnp.concatenate(w_out_all, axis=1), preferred_element_typ...]
    ppermute x4 -> x49, starting transfers between devices: 8.04 us -> 59.3 us  [swapped(): return lax.ppermute(x, axes, [(i, i ^ bit) for i in range(size)])]
    unnamed x23 -> x42, local copies, waits for them, and re-layouts: 0.92 us -> 12.5 us
  transfers between devices with their start and end apart: 9 -> 49, of which waited for: 7 -> 27; matrix products, arithmetic and copies ran while one was open for 15% -> 13% of each run, Pallas kernels for 0% -> 1%
where the time goes in v1:
time: 227 us; the launch traced here: 223 us
  waiting for transfers between devices  128 us (56%)
  starting transfers between devices  59.3 us (26%)
  local copies, waits for them, and re-layouts  18.6 us (8%)
  matrix products  9.34 us (4%)
  other arithmetic  3.96 us (2%)
  Pallas kernels  2.41 us (1%)
    ppermute x49, waiting for transfers between devices, swapped(): return lax.ppermute(x, axes, [(i, i ^ bit) for i in range(size)])  128 us
    ppermute x49, starting transfers between devices, swapped(): return lax.ppermute(x, axes, [(i, i ^ bit) for i in range(size)])  59.3 us
    unnamed x42, local copies, waits for them, and re-layouts  12.5 us
  transfers between devices with their start and end apart: 49, of which 27 were waited for; matrix products, arithmetic and copies ran while one was open for 13% of the time, Pallas kernels for 1%

profile of v1, /device:TPU:0, one launch (start us, length us, event | category | flops | bytes accessed | tf_op | source)
XLA Modules:
  0.0 222.9 jit_solution(18316703782824850938)
XLA Ops:
  0.7 2.6 %constant_dynamic-slice_fusion.4 = (bf16[128,1024]{1,0:T(8,128)(2,1)S(1)}, bf16[128,1024]{1,0:T(8,128)(2,1)S(1)}, bf16[128,1024]{1,0:T(8,128)(2,1)S(1)}, bf16[12...) fusion(bf16[128,8192]{1,0:T(8,128)(2,1)} %param.11, ...), kind=kLoop, calls=%fused_computation.116 | loop fusion | bytes 4194336 | tf_op jit(solution)/shard_map/dynamic_slice | solution.py:191
  3.3 3.0 %collective-permute-start = (bf16[128,1024]{1,0:T(8,128)(2,1)S(1)}, bf16[128,1024]{1,0:T(8,128)(2,1)}, u32[]{:S(2)}, u32[]{:S(2)}) collective-permute-start(bf16[128,1024]{1,0:T(8,128)(2,1)S(1)} %get-tuple-element.20), channel_id=1, source_target_pairs={{0,4},{4,0},{8,12},{12,8},{16,20},{20,16},{24,28},{28,24},{1,5},{5... | collective-permute-start | bytes 786440 | tf_op jit(solution)/shard_map/ppermute | solution.py:18
  7.8 2.1 collective-permute-start.4
  12.5 1.7 collective-permute-done
  14.2 2.8 %collective-permute-start.7 = (bf16[1024,256]{1,0:T(8,128)(2,1)}, bf16[1024,256]{1,0:T(8,128)(2,1)S(1)}, u32[]{:S(2)}, u32[]{:S(2)}) collective-permute-start(bf16[1024,256]{1,0:T(8,128)(2,1)} %param.18), channel_id=1, source_target_pairs={{0,1},{1,0},{2,3},{3,2},{4,5},{5,4},{6,7},{7,6},{8,9},{9,8},{10,11... | collective-permute-start | bytes 1572872 | tf_op jit(solution)/shard_map/ppermute | solution.py:18
  17.1 1.7 constant_dynamic-update-slice_fusion.6
  18.7 2.6 %collective-permute-start.8 = (bf16[1024,256]{1,0:T(8,128)(2,1)}, bf16[1024,256]{1,0:T(8,128)(2,1)S(1)}, u32[]{:S(2)}, u32[]{:S(2)}) collective-permute-start(bf16[1024,256]{1,0:T(8,128)(2,1)} %param.18), channel_id=1, source_target_pairs={{0,2},{1,3},{2,0},{3,1},{4,6},{5,7},{6,4},{7,5},{8,10},{9,11},{10,... | collective-permute-start | bytes 1572872 | tf_op jit(solution)/shard_map/ppermute | solution.py:18
  21.3 1.7 constant_dynamic-update-slice_fusion.5
  23.4 1.7 constant_dynamic-update-slice_fusion.4
  25.1 2.7 %collective-permute-start.6 = (bf16[128,1024]{1,0:T(8,128)(2,1)S(1)}, bf16[128,1024]{1,0:T(8,128)(2,1)S(1)}, u32[]{:S(2)}, u32[]{:S(2)}) collective-permute-start(bf16[128,1024]{1,0:T(8,128)(2,1)S(1)} %get-tuple-element.15), channel_id=1, source_target_pairs={{0,28},{4,24},{8,20},{12,16},{16,12},{20,8},{24,4},{28,0},{1,29},{... | collective-permute-start | bytes 786440 | tf_op jit(solution)/shard_map/ppermute | solution.py:18
  27.8 1.7 constant_dynamic-update-slice_fusion.3
  29.5 1.7 constant_dynamic-update-slice_fusion.2
  33.2 5.4 %collective-permute-done.6 = bf16[128,1024]{1,0:T(8,128)(2,1)S(1)} collective-permute-done((bf16[128,1024]{1,0:T(8,128)(2,1)S(1)}, bf16[128,1024]{1,0:T(8,128)(2,1)S(1)}, u32[]{:S(2)}, u32[]{:S(2)}) %collective-permute-start.6) | collective-permute-done | bytes 262176 | tf_op jit(solution)/shard_map/ppermute | solution.py:18
  42.2 15.0 %collective-permute-done.8 = bf16[1024,256]{1,0:T(8,128)(2,1)S(1)} collective-permute-done((bf16[1024,256]{1,0:T(8,128)(2,1)}, bf16[1024,256]{1,0:T(8,128)(2,1)S(1)}, u32[]{:S(2)}, u32[]{:S(2)}) %collective-permute-start.8) | collective-permute-done | bytes 524320 | tf_op jit(solution)/shard_map/ppermute | solution.py:18
  57.2 2.5 %collective-permute-start.42 = (bf16[128,256]{1,0:T(8,128)(2,1)S(1)}, bf16[128,256]{1,0:T(8,128)(2,1)S(1)}, u32[]{:S(2)}, u32[]{:S(2)}) collective-permute-start(bf16[128,256]{1,0:T(8,128)(2,1)S(1)} %copy-done.8), channel_id=1, source_target_pairs={{0,3},{1,2},{2,1},{3,0},{4,7},{5,6},{6,5},{7,4},{8,11},{9,10},{10,... | collective-permute-start | bytes 196616 | tf_op jit(solution)/shard_map/ppermute | solution.py:18
  59.7 3.9 %fusion = f32[1024,1024]{1,0:T(8,128)S(1)} fusion(bf16[1024,1024]{1,0:T(8,128)(2,1)} %constant_dynamic-update-slice_fusion, bf16[1024,256]{1,0:T(8,128)(2,1)S(1)} %collective-permute-done.9, bf16[1024,256]{1,0:T(8,128)(2,1)S(1)} %collective-permute-done.8, bf16[1024,256]{1,0:T(8,128)(2,1)S(1)} %collective-permute-done.7, bf16[1024,256]{1,0:T(8,128)(2,1)S(1)} %copy-done.13), kind=kOutput, calls=%fused_computation.2 | convolution fusion | flops 2155872256 | bytes 8388608 | tf_op jit(solution)/shard_map/dot_general | solution.py:223
  63.9 27.9 %collective-permute-done.41 = bf16[128,256]{1,0:T(8,128)(2,1)S(1)} collective-permute-done((bf16[128,256]{1,0:T(8,128)(2,1)S(1)}, bf16[128,256]{1,0:T(8,128)(2,1)S(1)}, u32[]{:S(2)}, u32[]{:S(2)}) %collective-permute-start.41) | collective-permute-done | bytes 65568 | tf_op jit(solution)/shard_map/ppermute | solution.py:18
  92.7 3.3 %collective-permute-done.38 = bf16[128,256]{1,0:T(8,128)(2,1)S(1)} collective-permute-done((bf16[128,256]{1,0:T(8,128)(2,1)S(1)}, bf16[128,256]{1,0:T(8,128)(2,1)S(1)}, u32[]{:S(2)}, u32[]{:S(2)}) %collective-permute-start.38) | collective-permute-done | bytes 65568 | tf_op jit(solution)/shard_map/ppermute | solution.py:18
  97.6 1.5 collective-permute-start.39
  99.3 4.2 %collective-permute-done.39 = bf16[128,512]{1,0:T(8,128)(2,1)S(1)} collective-permute-done((bf16[128,512]{1,0:T(8,128)(2,1)S(1)}, bf16[128,512]{1,0:T(8,128)(2,1)S(1)}, u32[]{:S(2)}, u32[]{:S(2)}) %collective-permute-start.39) | collective-permute-done | bytes 131104 | tf_op jit(solution)/shard_map/ppermute | solution.py:18
  104.5 1.7 collective-permute-start.14
  106.2 1.5 collective-permute-start.11
  107.8 2.1 collective-permute-done.40
  109.9 1.5 collective-permute-start.44
  111.4 2.5 %collective-permute-done.14 = bf16[256,512]{1,0:T(8,128)(2,1)S(1)} collective-permute-done((bf16[256,512]{1,0:T(8,128)(2,1)S(1)}, bf16[256,512]{1,0:T(8,128)(2,1)S(1)}, u32[]{:S(2)}, u32[]{:S(2)}) %collective-permute-start.14) | collective-permute-done | bytes 262176 | tf_op jit(solution)/shard_map/ppermute | solution.py:18
  113.9 2.7 %collective-permute-start.29 = (bf16[256,1024]{1,0:T(8,128)(2,1)S(1)}, bf16[256,1024]{1,0:T(8,128)(2,1)S(1)}, u32[]{:S(2)}, u32[]{:S(2)}) collective-permute-start(bf16[256,1024]{1,0:T(8,128)(2,1)S(1)} %copy-done.3), channel_id=1, source_target_pairs={{0,3},{1,2},{2,1},{3,0},{4,7},{5,6},{6,5},{7,4},{8,11},{9,10},{10,... | collective-permute-start | bytes 1572872 | tf_op jit(solution)/shard_map/ppermute | solution.py:18
  118.8 2.9 %collective-permute-done.12 = bf16[128,512]{1,0:T(8,128)(2,1)S(1)} collective-permute-done((bf16[128,512]{1,0:T(8,128)(2,1)S(1)}, bf16[128,512]{1,0:T(8,128)(2,1)S(1)}, u32[]{:S(2)}, u32[]{:S(2)}) %collective-permute-start.12) | collective-permute-done | bytes 131104 | tf_op jit(solution)/shard_map/ppermute | solution.py:18
  122.2 2.4 %collective-permute-start.13 = (bf16[128,256]{1,0:T(8,128)(2,1)S(1)}, bf16[128,256]{1,0:T(8,128)(2,1)S(1)}, u32[]{:S(2)}, u32[]{:S(2)}) collective-permute-start(bf16[128,256]{1,0:T(8,128)(2,1)S(1)} %get-tuple-element.55), channel_id=1, source_target_pairs={{0,1},{1,0},{2,3},{3,2},{4,5},{5,4},{6,7},{7,6},{8,9},{9,8},{10,11... | collective-permute-start | bytes 196616 | tf_op jit(solution)/shard_map/ppermute | solution.py:18
  125.7 1.5 collective-permute-start.17
  127.4 8.2 %collective-permute-done.16 = bf16[128,256]{1,0:T(8,128)(2,1)S(1)} collective-permute-done((bf16[128,256]{1,0:T(8,128)(2,1)S(1)}, bf16[128,256]{1,0:T(8,128)(2,1)S(1)}, u32[]{:S(2)}, u32[]{:S(2)}) %collective-permute-start.16) | collective-permute-done | bytes 65568 | tf_op jit(solution)/shard_map/ppermute | solution.py:18
  135.7 2.4 %attention.1 = (bf16[512,256]{1,0:T(8,128)(2,1)S(1)}, f32[2,512,256]{2,1,0:T(8,128)S(1)}) custom-call(s32[1]{0:T(128)} %bitcast.tensor_ref, s32[512,1]{1,0:T(8,128)S(1)} %copy.15.seg_query_ref, s32[2,512]{1,0:T(2,128)S(1)} %pad_add_fusion.seg_key_ref, bf16[512,256]{1,0:T(8,128)(2,1)S(1)} %copy-done.1, bf16[512,256]{1,0:T(8,128)(2,1)S(1)} %pad_maximum_fusion.4.dout_ref, ...), custom_call_target="tpu_custom_call" | custom-call | flops 671088640 | bytes 3145728 | tf_op jit(solution)/shard_map/attention/pallas_call | solution.py:159
  139.2 3.9 %collective-permute-done.19 = bf16[256,256]{1,0:T(8,128)(2,1)S(1)} collective-permute-done((bf16[256,256]{1,0:T(8,128)(2,1)S(1)}, bf16[256,256]{1,0:T(8,128)(2,1)S(1)}, u32[]{:S(2)}, u32[]{:S(2)}) %collective-permute-start.19) | collective-permute-done | bytes 131104 | tf_op jit(solution)/shard_map/ppermute | solution.py:18
  143.8 2.5 %collective-permute-start.24 = (bf16[128,512]{1,0:T(8,128)(2,1)S(1)}, bf16[128,512]{1,0:T(8,128)(2,1)S(1)}, u32[]{:S(2)}, u32[]{:S(2)}) collective-permute-start(bf16[128,512]{1,0:T(8,128)(2,1)S(1)} %pad_maximum_fusion.13), channel_id=1, source_target_pairs={{0,3},{1,2},{2,1},{3,0},{4,7},{5,6},{6,5},{7,4},{8,11},{9,10},{10,... | collective-permute-start | bytes 393224 | tf_op jit(solution)/shard_map/ppermute | solution.py:18
  146.8 1.6 collective-permute-start.21
  148.5 2.3 %collective-permute-done.24 = bf16[128,512]{1,0:T(8,128)(2,1)S(1)} collective-permute-done((bf16[128,512]{1,0:T(8,128)(2,1)S(1)}, bf16[128,512]{1,0:T(8,128)(2,1)S(1)}, u32[]{:S(2)}, u32[]{:S(2)}) %collective-permute-start.24) | collective-permute-done | bytes 131104 | tf_op jit(solution)/shard_map/ppermute | solution.py:18
  150.8 2.5 %collective-permute-done.20 = bf16[128,512]{1,0:T(8,128)(2,1)S(1)} collective-permute-done((bf16[128,512]{1,0:T(8,128)(2,1)S(1)}, bf16[128,512]{1,0:T(8,128)(2,1)S(1)}, u32[]{:S(2)}, u32[]{:S(2)}) %collective-permute-start.20) | collective-permute-done | bytes 131104 | tf_op jit(solution)/shard_map/ppermute | solution.py:18
  154.3 1.6 collective-permute-start.22
  156.9 2.4 %fusion.55 = (bf16[1024,1024]{1,0:T(8,128)(2,1)S(1)}, f32[1024,1024]{1,0:T(8,128)S(1)}) fusion(bf16[1024,1024]{1,0:T(8,128)(2,1)S(1)} %copy-done.10, bf16[512,1024]{1,0:T(8,128)(2,1)S(1)} %collective-permute-done.45, bf16[256,512]{1,0:T(8,128)(2,1)S(1)} %collective-permute-done.44, bf16[128,512]{1,0:T(8,128)(2,1)S(1)} %collective-permute-done.43, ...), kind=kOutput, calls=%fused_computation.145 | convolution fusion | flops 2167406592 | bytes 10485760 | tf_op jit(solution)/shard_map/dot_general | solution.py:280
  163.1 2.3 %collective-permute-start.47 = (bf16[1024,256]{1,0:T(8,128)(2,1)S(1)}, bf16[1024,256]{1,0:T(8,128)(2,1)S(1)}, u32[]{:S(2)}, u32[]{:S(2)}) collective-permute-start(bf16[1024,256]{1,0:T(8,128)(2,1)S(1)} %get-tuple-element.10), channel_id=1, source_target_pairs={{0,2},{1,3},{2,0},{3,1},{4,6},{5,7},{6,4},{7,5},{8,10},{9,11},{10,... | collective-permute-start | bytes 1572872 | tf_op jit(solution)/shard_map/ppermute | solution.py:18
  165.4 1.9 collective-permute-start.48
  171.0 10.4 %collective-permute-done.46 = bf16[1024,256]{1,0:T(8,128)(2,1)S(1)} collective-permute-done((bf16[1024,256]{1,0:T(8,128)(2,1)S(1)}, bf16[1024,256]{1,0:T(8,128)(2,1)S(1)}, u32[]{:S(2)}, u32[]{:S(2)}) %collective-permute-start.46) | collective-permute-done | bytes 524320 | tf_op jit(solution)/shard_map/ppermute | solution.py:18
  181.3 15.2 %collective-permute-done.47 = bf16[1024,256]{1,0:T(8,128)(2,1)S(1)} collective-permute-done((bf16[1024,256]{1,0:T(8,128)(2,1)S(1)}, bf16[1024,256]{1,0:T(8,128)(2,1)S(1)}, u32[]{:S(2)}, u32[]{:S(2)}) %collective-permute-start.47) | collective-permute-done | bytes 524320 | tf_op jit(solution)/shard_map/ppermute | solution.py:18
  197.8 1.5 convolution_convert_fusion.1
  201.4 1.8 collective-permute-start.32
  203.2 1.5 convolution_convert_fusion
  207.7 2.7 %collective-permute-done.32 = bf16[128,1024]{1,0:T(8,128)(2,1)S(1)} collective-permute-done((bf16[128,1024]{1,0:T(8,128)(2,1)S(1)}, bf16[128,1024]{1,0:T(8,128)(2,1)S(1)}, u32[]{:S(2)}, u32[]{:S(2)}) %collective-permute-start.32) | collective-permute-done | bytes 262176 | tf_op jit(solution)/shard_map/ppermute | solution.py:18
  210.6 5.4 %collective-permute-done.35 = bf16[128,1024]{1,0:T(8,128)(2,1)S(1)} collective-permute-done((bf16[128,1024]{1,0:T(8,128)(2,1)S(1)}, bf16[128,1024]{1,0:T(8,128)(2,1)S(1)}, u32[]{:S(2)}, u32[]{:S(2)}) %collective-permute-start.35) | collective-permute-done | bytes 262176 | tf_op jit(solution)/shard_map/ppermute | solution.py:18
  216.1 5.5 %collective-permute-done.37 = bf16[128,1024]{1,0:T(8,128)(2,1)S(1)} collective-permute-done((bf16[128,1024]{1,0:T(8,128)(2,1)S(1)}, bf16[128,1024]{1,0:T(8,128)(2,1)S(1)}, u32[]{:S(2)}, u32[]{:S(2)}) %collective-permute-start.37) | collective-permute-done | bytes 262176 | tf_op jit(solution)/shard_map/ppermute | solution.py:18
  (154 shorter events, 37.6 us)
Async XLA Ops:
  3.3 10.9 %collective-permute-start = (bf16[128,1024]{1,0:T(8,128)(2,1)S(1)}, bf16[128,1024]{1,0:T(8,128)(2,1)}, u32[]{:S(2)}, u32[]{:S(2)}) collective-permute-start(bf16[128,1024]{1,0:T(8,128)(2,1)S(1)} %get-tuple-element.20), channel_id=1, source_target_pairs={{0,4},{4,0},{8,12},{12,8},{16,20},{20,16},{24,28},{28,24},{1,5},{5... | collective-permute-start | bytes 786440 | tf_op jit(solution)/shard_map/ppermute | solution.py:18
  6.3 12.5 %collective-permute-start.1 = (bf16[128,1024]{1,0:T(8,128)(2,1)S(1)}, bf16[128,1024]{1,0:T(8,128)(2,1)}, u32[]{:S(2)}, u32[]{:S(2)}) collective-permute-start(bf16[128,1024]{1,0:T(8,128)(2,1)S(1)} %get-tuple-element.19), channel_id=1, source_target_pairs={{0,16},{4,20},{8,24},{12,28},{16,0},{20,4},{24,8},{28,12},{1,17},{... | collective-permute-start | bytes 786440 | tf_op jit(solution)/shard_map/ppermute | solution.py:18
  7.8 15.2 %collective-permute-start.2 = (bf16[128,1024]{1,0:T(8,128)(2,1)S(1)}, bf16[128,1024]{1,0:T(8,128)(2,1)}, u32[]{:S(2)}, u32[]{:S(2)}) collective-permute-start(bf16[128,1024]{1,0:T(8,128)(2,1)S(1)} %get-tuple-element.18), channel_id=1, source_target_pairs={{0,20},{4,16},{8,28},{12,24},{16,4},{20,0},{24,12},{28,8},{1,21},{... | collective-permute-start | bytes 786440 | tf_op jit(solution)/shard_map/ppermute | solution.py:18
  7.8 15.6 %collective-permute-start.3 = (bf16[128,1024]{1,0:T(8,128)(2,1)S(1)}, bf16[128,1024]{1,0:T(8,128)(2,1)}, u32[]{:S(2)}, u32[]{:S(2)}) collective-permute-start(bf16[128,1024]{1,0:T(8,128)(2,1)S(1)} %get-tuple-element.17), channel_id=1, source_target_pairs={{0,8},{4,12},{8,0},{12,4},{16,24},{20,28},{24,16},{28,20},{1,9},{5... | collective-permute-start | bytes 786440 | tf_op jit(solution)/shard_map/ppermute | solution.py:18
  7.8 17.3 %collective-permute-start.4 = (bf16[128,1024]{1,0:T(8,128)(2,1)S(1)}, bf16[128,1024]{1,0:T(8,128)(2,1)}, u32[]{:S(2)}, u32[]{:S(2)}) collective-permute-start(bf16[128,1024]{1,0:T(8,128)(2,1)S(1)} %get-tuple-element.16), channel_id=1, source_target_pairs={{0,12},{4,8},{8,4},{12,0},{16,28},{20,24},{24,20},{28,16},{1,13},{... | collective-permute-start | bytes 786440 | tf_op jit(solution)/shard_map/ppermute | solution.py:18
  14.2 26.5 %collective-permute-start.7 = (bf16[1024,256]{1,0:T(8,128)(2,1)}, bf16[1024,256]{1,0:T(8,128)(2,1)S(1)}, u32[]{:S(2)}, u32[]{:S(2)}) collective-permute-start(bf16[1024,256]{1,0:T(8,128)(2,1)} %param.18), channel_id=1, source_target_pairs={{0,1},{1,0},{2,3},{3,2},{4,5},{5,4},{6,7},{7,6},{8,9},{9,8},{10,11... | collective-permute-start | bytes 1572872 | tf_op jit(solution)/shard_map/ppermute | solution.py:18
  18.7 38.5 %collective-permute-start.8 = (bf16[1024,256]{1,0:T(8,128)(2,1)}, bf16[1024,256]{1,0:T(8,128)(2,1)S(1)}, u32[]{:S(2)}, u32[]{:S(2)}) collective-permute-start(bf16[1024,256]{1,0:T(8,128)(2,1)} %param.18), channel_id=1, source_target_pairs={{0,2},{1,3},{2,0},{3,1},{4,6},{5,7},{6,4},{7,5},{8,10},{9,11},{10,... | collective-permute-start | bytes 1572872 | tf_op jit(solution)/shard_map/ppermute | solution.py:18
  23.0 36.7 %collective-permute-start.9 = (bf16[1024,256]{1,0:T(8,128)(2,1)}, bf16[1024,256]{1,0:T(8,128)(2,1)S(1)}, u32[]{:S(2)}, u32[]{:S(2)}) collective-permute-start(bf16[1024,256]{1,0:T(8,128)(2,1)} %param.18), channel_id=1, source_target_pairs={{0,3},{1,2},{2,1},{3,0},{4,7},{5,6},{6,5},{7,4},{8,11},{9,10},{10,... | collective-permute-start | bytes 1572872 | tf_op jit(solution)/shard_map/ppermute | solution.py:18
  23.4 8.6 %collective-permute-start.5 = (bf16[128,1024]{1,0:T(8,128)(2,1)S(1)}, bf16[128,1024]{1,0:T(8,128)(2,1)S(1)}, u32[]{:S(2)}, u32[]{:S(2)}) collective-permute-start(bf16[128,1024]{1,0:T(8,128)(2,1)S(1)} %get-tuple-element.22), channel_id=1, source_target_pairs={{0,24},{4,28},{8,16},{12,20},{16,8},{20,12},{24,0},{28,4},{1,25},{... | collective-permute-start | bytes 786440 | tf_op jit(solution)/shard_map/ppermute | solution.py:18
  25.1 13.5 %collective-permute-start.6 = (bf16[128,1024]{1,0:T(8,128)(2,1)S(1)}, bf16[128,1024]{1,0:T(8,128)(2,1)S(1)}, u32[]{:S(2)}, u32[]{:S(2)}) collective-permute-start(bf16[128,1024]{1,0:T(8,128)(2,1)S(1)} %get-tuple-element.15), channel_id=1, source_target_pairs={{0,28},{4,24},{8,20},{12,16},{16,12},{20,8},{24,4},{28,0},{1,29},{... | collective-permute-start | bytes 786440 | tf_op jit(solution)/shard_map/ppermute | solution.py:18
  32.0 93.7 %collective-permute-start.27 = (bf16[256,1024]{1,0:T(8,128)(2,1)S(1)}, bf16[256,1024]{1,0:T(8,128)(2,1)S(1)}, u32[]{:S(2)}, u32[]{:S(2)}) collective-permute-start(bf16[256,1024]{1,0:T(8,128)(2,1)S(1)} %copy-done.3), channel_id=1, source_target_pairs={{0,1},{1,0},{2,3},{3,2},{4,5},{5,4},{6,7},{7,6},{8,9},{9,8},{10,11... | collective-permute-start | bytes 1572872 | tf_op jit(solution)/shard_map/ppermute | solution.py:18
  38.6 108.2 %collective-permute-start.28 = (bf16[256,1024]{1,0:T(8,128)(2,1)S(1)}, bf16[256,1024]{1,0:T(8,128)(2,1)S(1)}, u32[]{:S(2)}, u32[]{:S(2)}) collective-permute-start(bf16[256,1024]{1,0:T(8,128)(2,1)S(1)} %copy-done.3), channel_id=1, source_target_pairs={{0,2},{1,3},{2,0},{3,1},{4,6},{5,7},{6,4},{7,5},{8,10},{9,11},{10,... | collective-permute-start | bytes 1572872 | tf_op jit(solution)/shard_map/ppermute | solution.py:18
  40.8 51.0 %collective-permute-start.41 = (bf16[128,256]{1,0:T(8,128)(2,1)S(1)}, bf16[128,256]{1,0:T(8,128)(2,1)S(1)}, u32[]{:S(2)}, u32[]{:S(2)}) collective-permute-start(bf16[128,256]{1,0:T(8,128)(2,1)S(1)} %copy-done.9), channel_id=1, source_target_pairs={{0,2},{1,3},{2,0},{3,1},{4,6},{5,7},{6,4},{7,5},{8,10},{9,11},{10,... | collective-permute-start | bytes 196616 | tf_op jit(solution)/shard_map/ppermute | solution.py:18
  57.2 34.6 %collective-permute-start.42 = (bf16[128,256]{1,0:T(8,128)(2,1)S(1)}, bf16[128,256]{1,0:T(8,128)(2,1)S(1)}, u32[]{:S(2)}, u32[]{:S(2)}) collective-permute-start(bf16[128,256]{1,0:T(8,128)(2,1)S(1)} %copy-done.8), channel_id=1, source_target_pairs={{0,3},{1,2},{2,1},{3,0},{4,7},{5,6},{6,5},{7,4},{8,11},{9,10},{10,... | collective-permute-start | bytes 196616 | tf_op jit(solution)/shard_map/ppermute | solution.py:18
  63.8 40.1 %collective-permute-start.10 = (bf16[512,1024]{1,0:T(8,128)(2,1)S(1)}, bf16[512,1024]{1,0:T(8,128)(2,1)S(1)}, u32[]{:S(2)}, u32[]{:S(2)}) collective-permute-start(bf16[512,1024]{1,0:T(8,128)(2,1)S(1)} %slice.321), channel_id=1, source_target_pairs={{0,8},{4,12},{8,0},{12,4},{16,24},{20,28},{24,16},{28,20},{1,9},{5... | collective-permute-start | bytes 3145736 | tf_op jit(solution)/shard_map/ppermute | solution.py:18
  91.8 5.8 %collective-permute-start.18 = (bf16[256,256]{1,0:T(8,128)(2,1)S(1)}, bf16[256,256]{1,0:T(8,128)(2,1)S(1)}, u32[]{:S(2)}, u32[]{:S(2)}) collective-permute-start(bf16[256,256]{1,0:T(8,128)(2,1)S(1)} %copy-done.6), channel_id=1, source_target_pairs={{0,4},{4,0},{1,5},{5,1},{2,6},{6,2},{3,7},{7,3},{8,12},{12,8},{9,1... | collective-permute-start | bytes 393224 | tf_op jit(solution)/shard_map/ppermute | solution.py:18
  96.1 10.2 %collective-permute-start.43 = (bf16[128,512]{1,0:T(8,128)(2,1)S(1)}, bf16[128,512]{1,0:T(8,128)(2,1)S(1)}, u32[]{:S(2)}, u32[]{:S(2)}) collective-permute-start(bf16[128,512]{1,0:T(8,128)(2,1)S(1)} %constant_dynamic-update-slice_fusion.13), channel_id=1, source_target_pairs={{0,4},{4,0},{8,12},{12,8},{16,20},{20,16},{24,28},{28,24},{1,5},{5... | collective-permute-start | bytes 393224 | tf_op jit(solution)/shard_map/ppermute | solution.py:18
  97.6 5.8 %collective-permute-start.39 = (bf16[128,512]{1,0:T(8,128)(2,1)S(1)}, bf16[128,512]{1,0:T(8,128)(2,1)S(1)}, u32[]{:S(2)}, u32[]{:S(2)}) collective-permute-start(bf16[128,512]{1,0:T(8,128)(2,1)S(1)} %pad_maximum_fusion.14), channel_id=1, source_target_pairs={{0,16},{4,20},{8,24},{12,28},{16,0},{20,4},{24,8},{28,12},{1,17},{... | collective-permute-start | bytes 393224 | tf_op jit(solution)/shard_map/ppermute | solution.py:18
  103.5 6.4 %collective-permute-start.40 = (bf16[256,512]{1,0:T(8,128)(2,1)S(1)}, bf16[256,512]{1,0:T(8,128)(2,1)S(1)}, u32[]{:S(2)}, u32[]{:S(2)}) collective-permute-start(bf16[256,512]{1,0:T(8,128)(2,1)S(1)} %pad_maximum_fusion.5), channel_id=1, source_target_pairs={{0,4},{4,0},{8,12},{12,8},{16,20},{20,16},{24,28},{28,24},{1,5},{5... | collective-permute-start | bytes 786440 | tf_op jit(solution)/shard_map/ppermute | solution.py:18
  104.5 9.4 %collective-permute-start.14 = (bf16[256,512]{1,0:T(8,128)(2,1)S(1)}, bf16[256,512]{1,0:T(8,128)(2,1)S(1)}, u32[]{:S(2)}, u32[]{:S(2)}) collective-permute-start(bf16[256,512]{1,0:T(8,128)(2,1)S(1)} %pad_maximum_fusion.3), channel_id=1, source_target_pairs={{0,4},{4,0},{8,12},{12,8},{16,20},{20,16},{24,28},{28,24},{1,5},{5... | collective-permute-start | bytes 786440 | tf_op jit(solution)/shard_map/ppermute | solution.py:18
  106.2 10.3 %collective-permute-start.11 = (bf16[256,512]{1,0:T(8,128)(2,1)S(1)}, bf16[256,512]{1,0:T(8,128)(2,1)S(1)}, u32[]{:S(2)}, u32[]{:S(2)}) collective-permute-start(bf16[256,512]{1,0:T(8,128)(2,1)S(1)} %slice.237), channel_id=1, source_target_pairs={{0,16},{4,20},{8,24},{12,28},{16,0},{20,4},{24,8},{28,12},{1,17},{... | collective-permute-start | bytes 786440 | tf_op jit(solution)/shard_map/ppermute | solution.py:18
  109.9 7.2 %collective-permute-start.44 = (bf16[256,512]{1,0:T(8,128)(2,1)S(1)}, bf16[256,512]{1,0:T(8,128)(2,1)S(1)}, u32[]{:S(2)}, u32[]{:S(2)}) collective-permute-start(bf16[256,512]{1,0:T(8,128)(2,1)S(1)} %pad_maximum_fusion.6), channel_id=1, source_target_pairs={{0,16},{4,20},{8,24},{12,28},{16,0},{20,4},{24,8},{28,12},{1,17},{... | collective-permute-start | bytes 786440 | tf_op jit(solution)/shard_map/ppermute | solution.py:18
  113.9 34.5 %collective-permute-start.29 = (bf16[256,1024]{1,0:T(8,128)(2,1)S(1)}, bf16[256,1024]{1,0:T(8,128)(2,1)S(1)}, u32[]{:S(2)}, u32[]{:S(2)}) collective-permute-start(bf16[256,1024]{1,0:T(8,128)(2,1)S(1)} %copy-done.3), channel_id=1, source_target_pairs={{0,3},{1,2},{2,1},{3,0},{4,7},{5,6},{6,5},{7,4},{8,11},{9,10},{10,... | collective-permute-start | bytes 1572872 | tf_op jit(solution)/shard_map/ppermute | solution.py:18
  116.7 5.0 %collective-permute-start.12 = (bf16[128,512]{1,0:T(8,128)(2,1)S(1)}, bf16[128,512]{1,0:T(8,128)(2,1)S(1)}, u32[]{:S(2)}, u32[]{:S(2)}) collective-permute-start(bf16[128,512]{1,0:T(8,128)(2,1)S(1)} %get-tuple-element.13), channel_id=1, source_target_pairs={{0,4},{4,0},{8,12},{12,8},{16,20},{20,16},{24,28},{28,24},{1,5},{5... | collective-permute-start | bytes 393224 | tf_op jit(solution)/shard_map/ppermute | solution.py:18
  117.1 5.0 %collective-permute-start.15 = (bf16[128,512]{1,0:T(8,128)(2,1)S(1)}, bf16[128,512]{1,0:T(8,128)(2,1)S(1)}, u32[]{:S(2)}, u32[]{:S(2)}) collective-permute-start(bf16[128,512]{1,0:T(8,128)(2,1)S(1)} %get-tuple-element.14), channel_id=1, source_target_pairs={{0,16},{4,20},{8,24},{12,28},{16,0},{20,4},{24,8},{28,12},{1,17},{... | collective-permute-start | bytes 393224 | tf_op jit(solution)/shard_map/ppermute | solution.py:18
  122.2 5.1 %collective-permute-start.13 = (bf16[128,256]{1,0:T(8,128)(2,1)S(1)}, bf16[128,256]{1,0:T(8,128)(2,1)S(1)}, u32[]{:S(2)}, u32[]{:S(2)}) collective-permute-start(bf16[128,256]{1,0:T(8,128)(2,1)S(1)} %get-tuple-element.55), channel_id=1, source_target_pairs={{0,1},{1,0},{2,3},{3,2},{4,5},{5,4},{6,7},{7,6},{8,9},{9,8},{10,11... | collective-permute-start | bytes 196616 | tf_op jit(solution)/shard_map/ppermute | solution.py:18
  124.6 11.0 %collective-permute-start.16 = (bf16[128,256]{1,0:T(8,128)(2,1)S(1)}, bf16[128,256]{1,0:T(8,128)(2,1)S(1)}, u32[]{:S(2)}, u32[]{:S(2)}) collective-permute-start(bf16[128,256]{1,0:T(8,128)(2,1)S(1)} %get-tuple-element.56), channel_id=1, source_target_pairs={{0,2},{1,3},{2,0},{3,1},{4,6},{5,7},{6,4},{7,5},{8,10},{9,11},{10,... | collective-permute-start | bytes 196616 | tf_op jit(solution)/shard_map/ppermute | solution.py:18
  125.7 9.9 %collective-permute-start.17 = (bf16[128,256]{1,0:T(8,128)(2,1)S(1)}, bf16[128,256]{1,0:T(8,128)(2,1)S(1)}, u32[]{:S(2)}, u32[]{:S(2)}) collective-permute-start(bf16[128,256]{1,0:T(8,128)(2,1)S(1)} %get-tuple-element.57), channel_id=1, source_target_pairs={{0,3},{1,2},{2,1},{3,0},{4,7},{5,6},{6,5},{7,4},{8,11},{9,10},{10,... | collective-permute-start | bytes 196616 | tf_op jit(solution)/shard_map/ppermute | solution.py:18
  127.3 29.6 %collective-permute-start.45 = (bf16[512,1024]{1,0:T(8,128)(2,1)S(1)}, bf16[512,1024]{1,0:T(8,128)(2,1)S(1)}, u32[]{:S(2)}, u32[]{:S(2)}) collective-permute-start(bf16[512,1024]{1,0:T(8,128)(2,1)S(1)} %maximum_maximum_fusion.1), channel_id=1, source_target_pairs={{0,8},{4,12},{8,0},{12,4},{16,24},{20,28},{24,16},{28,20},{1,9},{5... | collective-permute-start | bytes 3145736 | tf_op jit(solution)/shard_map/ppermute | solution.py:18
  138.1 5.0 %collective-permute-start.19 = (bf16[256,256]{1,0:T(8,128)(2,1)S(1)}, bf16[256,256]{1,0:T(8,128)(2,1)S(1)}, u32[]{:S(2)}, u32[]{:S(2)}) collective-permute-start(bf16[256,256]{1,0:T(8,128)(2,1)S(1)} %fusion.37), channel_id=1, source_target_pairs={{0,4},{4,0},{1,5},{5,1},{2,6},{6,2},{3,7},{7,3},{8,12},{12,8},{9,1... | collective-permute-start | bytes 393224 | tf_op jit(solution)/shard_map/ppermute | solution.py:18
  143.8 7.0 %collective-permute-start.24 = (bf16[128,512]{1,0:T(8,128)(2,1)S(1)}, bf16[128,512]{1,0:T(8,128)(2,1)S(1)}, u32[]{:S(2)}, u32[]{:S(2)}) collective-permute-start(bf16[128,512]{1,0:T(8,128)(2,1)S(1)} %pad_maximum_fusion.13), channel_id=1, source_target_pairs={{0,3},{1,2},{2,1},{3,0},{4,7},{5,6},{6,5},{7,4},{8,11},{9,10},{10,... | collective-permute-start | bytes 393224 | tf_op jit(solution)/shard_map/ppermute | solution.py:18
  146.3 6.9 %collective-permute-start.20 = (bf16[128,512]{1,0:T(8,128)(2,1)S(1)}, bf16[128,512]{1,0:T(8,128)(2,1)S(1)}, u32[]{:S(2)}, u32[]{:S(2)}) collective-permute-start(bf16[128,512]{1,0:T(8,128)(2,1)S(1)} %pad_maximum_fusion.11), channel_id=1, source_target_pairs={{0,1},{1,0},{2,3},{3,2},{4,5},{5,4},{6,7},{7,6},{8,9},{9,8},{10,11... | collective-permute-start | bytes 393224 | tf_op jit(solution)/shard_map/ppermute | solution.py:18
  146.8 7.4 %collective-permute-start.21 = (bf16[128,512]{1,0:T(8,128)(2,1)S(1)}, bf16[128,512]{1,0:T(8,128)(2,1)S(1)}, u32[]{:S(2)}, u32[]{:S(2)}) collective-permute-start(bf16[128,512]{1,0:T(8,128)(2,1)S(1)} %pad_maximum_fusion.12), channel_id=1, source_target_pairs={{0,2},{1,3},{2,0},{3,1},{4,6},{5,7},{6,4},{7,5},{8,10},{9,11},{10,... | collective-permute-start | bytes 393224 | tf_op jit(solution)/shard_map/ppermute | solution.py:18
  154.3 5.8 %collective-permute-start.22 = (bf16[128,640]{1,0:T(8,128)(2,1)S(1)}, bf16[128,640]{1,0:T(8,128)(2,1)S(1)}, u32[]{:S(2)}, u32[]{:S(2)}) collective-permute-start(bf16[128,640]{1,0:T(8,128)(2,1)S(1)} %get-tuple-element.58), channel_id=1, source_target_pairs={{0,16},{4,20},{8,24},{12,28},{16,0},{20,4},{24,8},{28,12},{1,17},{... | collective-permute-start | bytes 491528 | tf_op jit(solution)/shard_map/ppermute | solution.py:18
  155.9 5.8 %collective-permute-start.25 = (bf16[128,640]{1,0:T(8,128)(2,1)S(1)}, bf16[128,640]{1,0:T(8,128)(2,1)S(1)}, u32[]{:S(2)}, u32[]{:S(2)}) collective-permute-start(bf16[128,640]{1,0:T(8,128)(2,1)S(1)} %get-tuple-element.59), channel_id=1, source_target_pairs={{0,4},{4,0},{8,12},{12,8},{16,20},{20,16},{24,28},{28,24},{1,5},{5... | collective-permute-start | bytes 491528 | tf_op jit(solution)/shard_map/ppermute | solution.py:18
  160.2 7.3 %collective-permute-start.23 = (bf16[256,640]{1,0:T(8,128)(2,1)S(1)}, bf16[256,640]{1,0:T(8,128)(2,1)S(1)}, u32[]{:S(2)}, u32[]{:S(2)}) collective-permute-start(bf16[256,640]{1,0:T(8,128)(2,1)S(1)} %pad_maximum_fusion.1), channel_id=1, source_target_pairs={{0,4},{4,0},{8,12},{12,8},{16,20},{20,16},{24,28},{28,24},{1,5},{5... | collective-permute-start | bytes 983048 | tf_op jit(solution)/shard_map/ppermute | solution.py:18
  161.7 7.1 %collective-permute-start.26 = (bf16[256,640]{1,0:T(8,128)(2,1)S(1)}, bf16[256,640]{1,0:T(8,128)(2,1)S(1)}, u32[]{:S(2)}, u32[]{:S(2)}) collective-permute-start(bf16[256,640]{1,0:T(8,128)(2,1)S(1)} %pad_maximum_fusion.2), channel_id=1, source_target_pairs={{0,16},{4,20},{8,24},{12,28},{16,0},{20,4},{24,8},{28,12},{1,17},{... | collective-permute-start | bytes 983048 | tf_op jit(solution)/shard_map/ppermute | solution.py:18
  162.8 18.5 %collective-permute-start.46 = (bf16[1024,256]{1,0:T(8,128)(2,1)S(1)}, bf16[1024,256]{1,0:T(8,128)(2,1)S(1)}, u32[]{:S(2)}, u32[]{:S(2)}) collective-permute-start(bf16[1024,256]{1,0:T(8,128)(2,1)S(1)} %get-tuple-element.8), channel_id=1, source_target_pairs={{0,1},{1,0},{2,3},{3,2},{4,5},{5,4},{6,7},{7,6},{8,9},{9,8},{10,11... | collective-permute-start | bytes 1572872 | tf_op jit(solution)/shard_map/ppermute | solution.py:18
  163.1 33.5 %collective-permute-start.47 = (bf16[1024,256]{1,0:T(8,128)(2,1)S(1)}, bf16[1024,256]{1,0:T(8,128)(2,1)S(1)}, u32[]{:S(2)}, u32[]{:S(2)}) collective-permute-start(bf16[1024,256]{1,0:T(8,128)(2,1)S(1)} %get-tuple-element.10), channel_id=1, source_target_pairs={{0,2},{1,3},{2,0},{3,1},{4,6},{5,7},{6,4},{7,5},{8,10},{9,11},{10,... | collective-permute-start | bytes 1572872 | tf_op jit(solution)/shard_map/ppermute | solution.py:18
  165.4 31.2 %collective-permute-start.48 = (bf16[1024,256]{1,0:T(8,128)(2,1)S(1)}, bf16[1024,256]{1,0:T(8,128)(2,1)S(1)}, u32[]{:S(2)}, u32[]{:S(2)}) collective-permute-start(bf16[1024,256]{1,0:T(8,128)(2,1)S(1)} %get-tuple-element.9), channel_id=1, source_target_pairs={{0,3},{1,2},{2,1},{3,0},{4,7},{5,6},{6,5},{7,4},{8,11},{9,10},{10,... | collective-permute-start | bytes 1572872 | tf_op jit(solution)/shard_map/ppermute | solution.py:18
  168.9 34.3 %collective-permute-start.33 = (bf16[512,1280]{1,0:T(8,128)(2,1)S(1)}, bf16[512,1280]{1,0:T(8,128)(2,1)S(1)}, u32[]{:S(2)}, u32[]{:S(2)}) collective-permute-start(bf16[512,1280]{1,0:T(8,128)(2,1)S(1)} %maximum_maximum_fusion), channel_id=1, source_target_pairs={{0,8},{4,12},{8,0},{12,4},{16,24},{20,28},{24,16},{28,20},{1,9},{5... | collective-permute-start | bytes 3932168 | tf_op jit(solution)/shard_map/ppermute | solution.py:18
  199.7 6.4 %collective-permute-start.30 = (bf16[128,1024]{1,0:T(8,128)(2,1)S(1)}, bf16[128,1024]{1,0:T(8,128)(2,1)S(1)}, u32[]{:S(2)}, u32[]{:S(2)}) collective-permute-start(bf16[128,1024]{1,0:T(8,128)(2,1)S(1)} %get-tuple-element.31), channel_id=1, source_target_pairs={{0,4},{4,0},{8,12},{12,8},{16,20},{20,16},{24,28},{28,24},{1,5},{5... | collective-permute-start | bytes 786440 | tf_op jit(solution)/shard_map/ppermute | solution.py:18
  200.1 6.4 %collective-permute-start.31 = (bf16[128,1024]{1,0:T(8,128)(2,1)S(1)}, bf16[128,1024]{1,0:T(8,128)(2,1)S(1)}, u32[]{:S(2)}, u32[]{:S(2)}) collective-permute-start(bf16[128,1024]{1,0:T(8,128)(2,1)S(1)} %get-tuple-element.30), channel_id=1, source_target_pairs={{0,16},{4,20},{8,24},{12,28},{16,0},{20,4},{24,8},{28,12},{1,17},{... | collective-permute-start | bytes 786440 | tf_op jit(solution)/shard_map/ppermute | solution.py:18
  201.4 9.0 %collective-permute-start.32 = (bf16[128,1024]{1,0:T(8,128)(2,1)S(1)}, bf16[128,1024]{1,0:T(8,128)(2,1)S(1)}, u32[]{:S(2)}, u32[]{:S(2)}) collective-permute-start(bf16[128,1024]{1,0:T(8,128)(2,1)S(1)} %get-tuple-element.29), channel_id=1, source_target_pairs={{0,20},{4,16},{8,28},{12,24},{16,4},{20,0},{24,12},{28,8},{1,21},{... | collective-permute-start | bytes 786440 | tf_op jit(solution)/shard_map/ppermute | solution.py:18
  204.8 5.8 %collective-permute-start.34 = (bf16[128,1024]{1,0:T(8,128)(2,1)S(1)}, bf16[128,1024]{1,0:T(8,128)(2,1)S(1)}, u32[]{:S(2)}, u32[]{:S(2)}) collective-permute-start(bf16[128,1024]{1,0:T(8,128)(2,1)S(1)} %get-tuple-element.28), channel_id=1, source_target_pairs={{0,8},{4,12},{8,0},{12,4},{16,24},{20,28},{24,16},{28,20},{1,9},{5... | collective-permute-start | bytes 786440 | tf_op jit(solution)/shard_map/ppermute | solution.py:18
  206.1 9.9 %collective-permute-start.35 = (bf16[128,1024]{1,0:T(8,128)(2,1)S(1)}, bf16[128,1024]{1,0:T(8,128)(2,1)S(1)}, u32[]{:S(2)}, u32[]{:S(2)}) collective-permute-start(bf16[128,1024]{1,0:T(8,128)(2,1)S(1)} %get-tuple-element.27), channel_id=1, source_target_pairs={{0,12},{4,8},{8,4},{12,0},{16,28},{20,24},{24,20},{28,16},{1,13},{... | collective-permute-start | bytes 786440 | tf_op jit(solution)/shard_map/ppermute | solution.py:18
  206.5 9.5 %collective-permute-start.36 = (bf16[128,1024]{1,0:T(8,128)(2,1)S(1)}, bf16[128,1024]{1,0:T(8,128)(2,1)S(1)}, u32[]{:S(2)}, u32[]{:S(2)}) collective-permute-start(bf16[128,1024]{1,0:T(8,128)(2,1)S(1)} %get-tuple-element.26), channel_id=1, source_target_pairs={{0,24},{4,28},{8,16},{12,20},{16,8},{20,12},{24,0},{28,4},{1,25},{... | collective-permute-start | bytes 786440 | tf_op jit(solution)/shard_map/ppermute | solution.py:18
  210.5 11.1 %collective-permute-start.37 = (bf16[128,1024]{1,0:T(8,128)(2,1)S(1)}, bf16[128,1024]{1,0:T(8,128)(2,1)S(1)}, u32[]{:S(2)}, u32[]{:S(2)}) collective-permute-start(bf16[128,1024]{1,0:T(8,128)(2,1)S(1)} %get-tuple-element.25), channel_id=1, source_target_pairs={{0,28},{4,24},{8,20},{12,16},{16,12},{20,8},{24,4},{28,0},{1,29},{... | collective-permute-start | bytes 786440 | tf_op jit(solution)/shard_map/ppermute | solution.py:18
  (15 other events, 249.3 us)

commit v2 on v1

v2 whole, which is shorter than its diff:
```python
import functools
import math

import jax
import jax.numpy as jnp
from jax import lax
from jax.experimental import pallas as pl
from jax.experimental.pallas import tpu as pltpu
from jax.sharding import PartitionSpec as P

PLANE = ("dp", "context")
BF16 = jnp.bfloat16
F32 = jnp.float32
TENSOR_ORDER = (0, 2, 1, 3)


def swapped(x, axes, bit):
    size = lax.axis_size(axes)
    return lax.ppermute(x, axes, [(i, i ^ bit) for i in range(size)])


def neighbours(to_left, to_right):
    size = lax.axis_size("context")
    up = [(i, i + 1) for i in range(size - 1)]
    down = [(i + 1, i) for i in range(size - 1)]
    return [lax.ppermute(to_right, "context", up), lax.ppermute(to_left, "context", down)]


def contract(x, y, dims):
    return lax.dot_general(x, y, (dims, ((), ())), preferred_element_type=F32)


VMEM = pl.BlockSpec(memory_space=pltpu.VMEM)
ANY = pl.BlockSpec(memory_space=pl.ANY)
SMALL = pl.CostEstimate(flops=0, bytes_accessed=0, transcendentals=0)


def cut_kernel(
    ranks_ref, x_ref, weight_ref, att_ref, *refs, parts, pair
):
    out_refs, (to_2_ref, to_1_ref, att_own_ref) = refs[:-3], refs[-3:]
    width = out_refs[0].shape[1] // 2
    for i, k in enumerate(parts):
        for half in range(2):
            owner = lax.bitwise_xor(ranks_ref[0], k ^ (half * pair))
            start = pl.multiple_of(owner * width, width)
            out_refs[i][:, half * width : (half + 1) * width] = x_ref[:, pl.ds(start, width)]
    rows, depth = att_own_ref.shape[0], weight_ref.shape[0]

    def att_of(j):
        owner = lax.bitwise_xor(ranks_ref[1], j)
        return att_ref[pl.ds(pl.multiple_of(owner * rows, rows), rows), :]

    att_own_ref[...] = att_of(0)
    to_2_ref[:rows, :] = att_of(2)
    to_2_ref[rows : rows + depth, :] = weight_ref[...]
    to_2_ref[rows + depth :, :] = att_of(3)
    to_1_ref[:depth, :] = weight_ref[...]
    to_1_ref[depth:, :] = att_of(1)


def cut(ranks, x, weight, att, parts, pair):
    rows, (depth, cols) = x.shape[0], weight.shape
    return pl.pallas_call(
        functools.partial(cut_kernel, parts=parts, pair=pair),
        out_shape=[jax.ShapeDtypeStruct((rows, 2 * depth), x.dtype) for _ in parts]
        + [
            jax.ShapeDtypeStruct((depth + 2 * rows, cols), x.dtype),
            jax.ShapeDtypeStruct((depth + rows, cols), x.dtype),
            jax.ShapeDtypeStruct((rows, cols), x.dtype),
        ],
        in_specs=[pl.BlockSpec(memory_space=pltpu.SMEM)] + [VMEM] * 3,
        out_specs=[VMEM] * (len(parts) + 3),
        compiler_params=pltpu.CompilerParams(vmem_limit_bytes=40 * 2**20),
        cost_estimate=SMALL,
        name="cut",
    )(ranks, x, weight, att)


def project_kernel(*refs, tokens, starts, width):
    pieces = len(starts)
    att_ref, token_refs, refs = refs[0], refs[1 : 1 + tokens], refs[1 + tokens :]
    own_refs, pair_refs = refs[:pieces], refs[pieces : 2 * pieces]
    out_refs, att_out_ref, held = refs[-2 - tokens : -2], refs[-2], refs[-1]
    rows = token_refs[0].shape[0]
    cols = own_refs[0].shape[1]
    for i, ref in enumerate(token_refs):
        held[i * rows : (i + 1) * rows, :] = ref[...]
    for j, start in enumerate(starts):
        at, used = slice(j * cols, (j + 1) * cols), slice(start, start + width)
        total = contract(held[:, :width], own_refs[j][used, :], ((1,), (0,)))
        total = total + contract(held[:, width:], pair_refs[j][used, :], ((1,), (0,)))
        for i, ref in enumerate(out_refs):
            ref[:, at] = total[i * rows : (i + 1) * rows].astype(ref.dtype)
        if j == 0:
            att_out_ref[:, at] = att_ref[...]
        else:
            beside = 0 if start else width
            att_out_ref[:, at] = own_refs[j][beside : beside + rows, :]


def project(att, tokens, own, pair, starts, width, behind):
    rows, cols = att.shape
    columns = len(own) * cols
    return pl.pallas_call(
        functools.partial(project_kernel, tokens=len(tokens), starts=starts, width=width),
        out_shape=[
            jax.ShapeDtypeStruct((rows, columns), BF16 if i else F32) for i in range(len(tokens))
        ]
        + [jax.ShapeDtypeStruct((rows, columns), BF16)],
        in_specs=[VMEM] * (1 + len(tokens) + 2 * len(own)) + [ANY] * len(behind),
        out_specs=[VMEM] * (len(tokens) + 1),
        scratch_shapes=[pltpu.VMEM((rows * len(tokens), 2 * width), BF16)],
        compiler_params=pltpu.CompilerParams(vmem_limit_bytes=40 * 2**20),
        cost_estimate=SMALL,
        name="project",
    )(att, *tokens, *own, *pair, *behind)


def hand_on_kernel(x_ref, *refs):
    refs[-1][...] = x_ref[-refs[-1].shape[0] :, :]


def hand_on(x, rows, behind):
    return pl.pallas_call(
        hand_on_kernel,
        out_shape=jax.ShapeDtypeStruct((rows, x.shape[1]), x.dtype),
        in_specs=[VMEM] + [ANY] * len(behind),
        out_specs=VMEM,
        compiler_params=pltpu.CompilerParams(vmem_limit_bytes=40 * 2**20),
        cost_estimate=SMALL,
        name="hand_on",
    )(x, *behind)


def add_kernel(own_ref, *refs, parts, pieces):
    part_refs, out_refs = refs[:parts], refs[parts:]
    cols = out_refs[0].shape[1]
    total = own_ref[...]
    for ref in part_refs:
        total = total + ref[...].astype(F32)
    for j, ref in enumerate(out_refs):
        ref[...] = total[:, j * cols : (j + 1) * cols].astype(BF16)


def add_up(own, parts, pieces):
    rows, columns = own.shape
    return pl.pallas_call(
        functools.partial(add_kernel, parts=len(parts), pieces=pieces),
        out_shape=[jax.ShapeDtypeStruct((rows, columns // pieces), BF16)] * pieces,
        in_specs=[VMEM] * (1 + len(parts)),
        out_specs=[VMEM] * pieces,
        compiler_params=pltpu.CompilerParams(vmem_limit_bytes=60 * 2**20),
        cost_estimate=SMALL,
        name="add_up",
    )(own, *parts)


def join_kernel(ranks_ref, kv_ref, *refs, pieces, backs, later):
    refs = refs[later:]
    query_refs, back_refs = refs[:pieces], refs[pieces : pieces + backs]
    (query_ref, away_ref, next_ref, own_ref), held = refs[pieces + backs :][:4], refs[-1]
    rows, cols = query_refs[0].shape
    span = kv_ref.shape[0] // 2
    for i, ref in enumerate(query_refs):
        query_ref[:, i * cols : (i + 1) * cols] = ref[...]
    held[...] = kv_ref[...]
    if backs == 1:
        at = pl.ds(pl.multiple_of(ranks_ref[2] * span, span), span)
        held[at, :] = held[at, :] + back_refs[0][...].astype(F32)
    else:
        held[span:, :] = held[span:, :] + back_refs[0][...].astype(F32)
        held[:span, :] = held[:span, :] + back_refs[1][...].astype(F32)

    def rank_rows(j):
        at = pl.ds(pl.multiple_of(lax.bitwise_xor(ranks_ref[1], j) * rows, rows), rows)
        return held[at, :]

    away_ref[:rows, :] = rank_rows(2).astype(BF16)
    away_ref[rows:, :] = rank_rows(3).astype(BF16)
    next_ref[...] = rank_rows(1)
    own_ref[...] = rank_rows(0)


def join(ranks, kv, back, queries, later):
    rows, cols = queries[0].shape
    width = kv.shape[1]
    return pl.pallas_call(
        functools.partial(
            join_kernel, pieces=len(queries), backs=len(back), later=len(later)
        ),
        out_shape=[
            jax.ShapeDtypeStruct((rows, cols * len(queries)), BF16),
            jax.ShapeDtypeStruct((2 * rows, width), BF16),
            jax.ShapeDtypeStruct((rows, width), F32),
            jax.ShapeDtypeStruct((rows, width), F32),
            *[jax.ShapeDtypeStruct(x.shape, x.dtype) for x in later],
        ],
        in_specs=[pl.BlockSpec(memory_space=pltpu.SMEM), VMEM]
        + [ANY] * len(later)
        + [VMEM] * (len(queries) + len(back)),
        out_specs=[VMEM] * 4 + [ANY] * len(later),
        scratch_shapes=[pltpu.VMEM(kv.shape, F32)],
        input_output_aliases={2 + i: 4 + i for i in range(len(later))},
        compiler_params=pltpu.CompilerParams(vmem_limit_bytes=60 * 2**20),
        cost_estimate=SMALL,
        name="join",
    )(ranks, kv, *later, *queries, *back)


def outer_kernel(*refs, tokens, atts, behind):
    (own_ref, pair_ref), (held, att_held) = refs[tokens + atts + behind :][:2], refs[-2:]
    for block_refs, whole in ((refs[:tokens], held), (refs[tokens : tokens + atts], att_held)):
        start = 0
        for ref in block_refs:
            whole[start : start + ref.shape[0], :] = ref[...]
            start += ref.shape[0]
    width = own_ref.shape[0]
    step = min(width, 256)
    for e in range(0, width, step):
        at = slice(e, e + step)
        own_ref[at, :] = contract(held[:, at], att_held[...], ((0,), (0,)))
        pair_at = slice(width + e, width + e + step)
        pair_ref[at, :] = contract(held[:, pair_at], att_held[...], ((0,), (0,))).astype(BF16)


def outer(tokens, atts, later, behind):
    width, columns = tokens[0].shape[1] // 2, atts[0].shape[1]
    depth = tokens[0].shape[0] * len(tokens)
    return pl.pallas_call(
        functools.partial(
            outer_kernel, tokens=len(tokens), atts=len(atts), behind=len(later) + len(behind)
        ),
        out_shape=[
            jax.ShapeDtypeStruct((width, columns), F32),
            jax.ShapeDtypeStruct((width, columns), BF16),
            *[jax.ShapeDtypeStruct(x.shape, x.dtype) for x in later],
        ],
        in_specs=[VMEM] * (len(tokens) + len(atts)) + [ANY] * (len(later) + len(behind)),
        out_specs=[VMEM] * 2 + [ANY] * len(later),
        input_output_aliases={len(tokens) + len(atts) + i: 2 + i for i in range(len(later))},
        scratch_shapes=[pltpu.VMEM((depth, 2 * width), BF16), pltpu.VMEM((depth, columns), BF16)],
        compiler_params=pltpu.CompilerParams(vmem_limit_bytes=40 * 2**20),
        cost_estimate=SMALL,
        name="outer",
    )(*tokens, *atts, *later, *behind)


def feed_kernel(*refs, tokens, sides):
    query_refs, kv_refs, refs = refs[:tokens], refs[tokens : 2 * tokens], refs[2 * tokens :]
    weights, refs = [refs[i * sides : (i + 1) * sides] for i in range(2)], refs[2 * sides :]
    w_kv_ref, out_refs, held = refs[0], refs[-1 - tokens : -1], refs[-1]
    rows, columns = query_refs[0].shape
    width = w_kv_ref.shape[1] // 2
    for i in range(tokens):
        held[i * rows : (i + 1) * rows, :columns] = query_refs[i][...]
        held[i * rows : (i + 1) * rows, columns:] = kv_refs[i][...]
    for half in range(2):
        at = slice(half * width, (half + 1) * width)
        total = contract(held[:, columns:], w_kv_ref[:, at], ((1,), (0,)))
        start = 0
        for w in weights[half]:
            depth = w.shape[0]
            total = total + contract(held[:, start : start + depth], w[...], ((1,), (0,)))
            start += depth
        for i, ref in enumerate(out_refs):
            ref[:, at] = total[i * rows : (i + 1) * rows].astype(BF16)


def feed(queries, kvs, own, pair, w_kv, behind):
    rows, columns = queries[0].shape
    width = w_kv.shape[1]
    depth = columns + w_kv.shape[0]
    return pl.pallas_call(
        functools.partial(feed_kernel, tokens=len(queries), sides=len(own)),
        out_shape=[jax.ShapeDtypeStruct((rows, width), BF16)] * len(queries),
        in_specs=[VMEM] * (2 * len(queries) + 2 * len(own) + 1) + [ANY] * len(behind),
        out_specs=[VMEM] * len(queries),
        scratch_shapes=[pltpu.VMEM((rows * len(queries), depth), BF16)],
        compiler_params=pltpu.CompilerParams(vmem_limit_bytes=60 * 2**20),
        cost_estimate=SMALL,
        name="feed",
    )(*queries, *kvs, *own, *pair, w_kv, *behind)


def attention_kernel(
    ranks_ref, seg_query_ref, seg_key_ref, query_ref, attended_ref, key_ref, value_ref, log_ref,
    *refs, peers, befores, cycle_size,
):
    dout_refs, before_refs = refs[:peers], refs[peers : peers + befores]
    dquery_refs, away_refs = refs[-3 - befores - peers : -3 - befores], refs[-3 - befores : -3]
    kv_grads_ref, dout_held, dquery_held = refs[-3:]
    rank, last_rank = ranks_ref[1], ranks_ref[2] == cycle_size - 1
    head_dim = key_ref.shape[1]
    span = query_ref.shape[0] // 2
    heads = query_ref.shape[1] // head_dim
    sub = 2 * span // peers
    inv_root = 1.0 / math.sqrt(head_dim)

    def place(a):
        return pl.ds(pl.multiple_of(a * sub, sub), sub)

    def by_head(x):
        return jnp.concatenate(
            [x[:, h * head_dim : (h + 1) * head_dim] for h in range(heads)], axis=0
        )

    for j, ref in zip(TENSOR_ORDER, dout_refs):
        dout_held[place(lax.bitwise_xor(rank, j)), :] = ref[...]
    before = []
    for b in range(2):
        rows = slice(b * span, (b + 1) * span)
        query = by_head(query_ref[rows, :])
        dout = by_head(dout_held[rows, :])
        attended = by_head(attended_ref[rows, :])
        key_before = before_refs[b % befores][:, :head_dim]
        value_before = before_refs[b % befores][:, head_dim:]
        if b == 1:
            key_before = jnp.where(last_rank, key_ref[:span, :], key_before)
            value_before = jnp.where(last_rank, value_ref[:span, :], value_before)
        key = jnp.concatenate([key_before, key_ref[rows, :]], axis=0)
        value = jnp.concatenate([value_before, value_ref[rows, :]], axis=0)
        log_rows = jnp.concatenate([log_ref[rows, h : h + 1] for h in range(heads)], axis=0)
        query_at = lax.broadcasted_iota(jnp.int32, (span, 2 * span), 0)
        key_at = lax.broadcasted_iota(jnp.int32, (span, 2 * span), 1) - span
        allowed = (key_at <= query_at) & (seg_query_ref[rows, :] == seg_key_ref[b : b + 1, :])
        allowed = jnp.concatenate([allowed] * heads, axis=0)
        scores = contract(query, key, ((1,), (1,))) * inv_root
        prob = jnp.where(allowed, jnp.exp(scores - log_rows), 0.0)
        delta = jnp.sum(dout.astype(F32) * attended.astype(F32), axis=1, keepdims=True)
        dprob = contract(dout, value, ((1,), (1,)))
        dscore = (prob * (dprob - delta)).astype(BF16)
        dquery = (contract(dscore, key, ((1,), (0,))) * inv_root).astype(BF16)
        for h in range(heads):
            dquery_held[rows, h * head_dim : (h + 1) * head_dim] = dquery[
                h * span : (h + 1) * span
            ]
        key_grads = contract(dscore, query, ((0,), (0,))) * inv_root
        value_grads = contract(prob.astype(BF16), dout, ((0,), (0,)))
        kv_grads_ref[rows, :head_dim] = key_grads[span:]
        kv_grads_ref[rows, head_dim:] = value_grads[span:]
        before.append((key_grads[:span], value_grads[:span]))
    for i, half in enumerate((slice(0, head_dim), slice(head_dim, 2 * head_dim))):
        low, high = before[0][i], before[1][i]
        kv_grads_ref[:span, half] = kv_grads_ref[:span, half] + jnp.where(last_rank, high, 0.0)
        if befores == 1:
            away_refs[0][:, half] = jnp.where(last_rank, low, high).astype(BF16)
        else:
            away_refs[0][:, half] = low.astype(BF16)
            away_refs[1][:, half] = jnp.where(last_rank, 0.0, high).astype(BF16)
    for j, ref in zip(TENSOR_ORDER, dquery_refs):
        ref[...] = dquery_held[place(lax.bitwise_xor(rank, j)), :]


def attention(
    ranks, seg_query, seg_key, queries, attended, keys, values, log_sums, dout, before, behind,
    cycle_size,
):
    kv_shape = (keys.shape[0], 2 * keys.shape[1])
    return pl.pallas_call(
        functools.partial(
            attention_kernel, peers=len(dout), befores=len(before), cycle_size=cycle_size
        ),
        out_shape=[jax.ShapeDtypeStruct(x.shape, BF16) for x in (*dout, *before)]
        + [jax.ShapeDtypeStruct(kv_shape, F32)],
        in_specs=[pl.BlockSpec(memory_space=pltpu.SMEM)]
        + [VMEM] * (7 + len(dout) + len(before))
        + [ANY] * len(behind),
        out_specs=[VMEM] * (len(dout) + len(before) + 1),
        scratch_shapes=[pltpu.VMEM(queries.shape, BF16)] * 2,
        compiler_params=pltpu.CompilerParams(vmem_limit_bytes=32 * 2**20),
        cost_estimate=SMALL,
        name="attention",
    )(ranks, seg_query, seg_key, queries, attended, keys, values, log_sums, *dout, *before, *behind)


def on_device(
    grad_out, queries, attended, keys, values, log_sums, segment_ids, w_out, w_query, w_key, w_value
):
    tensor_rank = lax.axis_index("tensor")
    plane_rank = lax.axis_index(PLANE)
    cycle_size, cycle_pos = lax.axis_size("context"), lax.axis_index("context")
    own_rows, features = grad_out.shape
    width = w_out.shape[0]
    cols = queries.shape[1]
    span = queries.shape[0] // 2
    head_dim = keys.shape[1]
    pair = cycle_size
    bits = [1 << i for i in range(lax.axis_size(PLANE).bit_length() - 1)]
    bits = [bit for bit in reversed(bits) if bit != pair]
    meets = [0]
    for bit in bits:
        meets += [k ^ bit for k in meets]
    meets = meets[1:]

    def own_block(x, rank, size, axis):
        return lax.dynamic_slice_in_dim(x, rank * size, size, axis=axis)

    def pair_blocks(x, k):
        return jnp.concatenate(
            [own_block(x, plane_rank ^ k, width, 1), own_block(x, plane_rank ^ k ^ pair, width, 1)],
            axis=1,
        )

    def plane_gather(x):
        return [x] + [swapped(x, PLANE, k) for k in meets]

    def along(x, j):
        return swapped(x, "tensor", j)

    ranks = jnp.stack([plane_rank, tensor_rank, cycle_pos])
    *tokens, to_2, to_1, att_own = cut(ranks, grad_out, w_out, attended, [0] + meets, pair)
    out_2, out_1 = along(to_2, 2), along(to_1, 1)
    tokens = tokens[:1] + [swapped(x, PLANE, k) for k, x in zip(meets, tokens[1:])]
    out_3 = along(hand_on(out_2, width + own_rows, tokens[1:]), 1)
    w_out_own = [w_out, out_2, out_1, out_3]
    w_out_pair = [swapped(w, PLANE, pair) for w in w_out_own]
    starts = (0, own_rows, 0, 0)

    query_2, query_1 = along(w_query, 2), along(w_query, 1)

    kv_pair = jnp.concatenate([keys, values], axis=1)
    if cycle_size == 2:
        before = [swapped(own_block(kv_pair, cycle_pos, span, 0), "context", 1)]
    else:
        before = neighbours(kv_pair[span:], kv_pair[:span])
    seg_row = segment_ids[0]
    high_span = 2 * cycle_size - 1 - cycle_pos

    def seg_slice(at):
        return lax.dynamic_slice_in_dim(seg_row, jnp.maximum(at, 0) * span, span)

    seg_low, seg_high = seg_slice(cycle_pos), seg_slice(high_span)
    seg_before = jnp.where(cycle_pos == 0, -1, seg_slice(cycle_pos - 1))
    seg_query = jnp.concatenate([seg_low, seg_high])[:, None]
    seg_key = jnp.stack(
        [
            jnp.concatenate([seg_before, seg_low]),
            jnp.concatenate([seg_slice(high_span - 1), seg_high]),
        ]
    )
    log_rows = log_sums.T

    *partial_attn, att_own = project(
        att_own, tokens, w_out_own, w_out_pair, starts, width, before
    )
    parts = [swapped(x, PLANE, k) for k, x in zip(meets, partial_attn[1:])]
    attn_own = list(add_up(partial_attn[0], parts, 4))
    dout = attn_own[:1] + [along(x, j) for x, j in zip(attn_own[1:], TENSOR_ORDER[1:])]
    *dquery, kv_grads = attention(
        ranks, seg_query, seg_key, queries, attended, keys, values, log_rows, dout, before,
        [query_2, query_1], cycle_size,
    )
    dquery, away = dquery[:4], dquery[4:]

    atts = [att_own]
    for bit in bits:
        atts.append(swapped(jnp.concatenate(atts, axis=0), PLANE, bit))

    dquery = dquery[:1] + [along(x, j) for x, j in zip(dquery[1:], TENSOR_ORDER[1:])]
    back = [swapped(away[0], "context", 1)] if cycle_size == 2 else neighbours(*away)
    dquery_own, kv_away, kv_next, kv_rest, query_2, query_1 = join(
        ranks, kv_grads, back, dquery, [query_2, query_1]
    )
    dquery_met = plane_gather(dquery_own)
    got = along(kv_away, 2)
    kv_next = along((kv_next + got[own_rows:].astype(F32)).astype(BF16), 1)
    kv_own = (kv_rest + got[:own_rows].astype(F32) + kv_next.astype(F32)).astype(BF16)
    kv_met = plane_gather(kv_own)

    query_3 = along(query_2, 1)

    out_own, out_pair, *w_query_own = outer(
        tokens, atts, [query_2, query_1, query_3], [dquery_met[1], got]
    )
    w_query_own = [w_query, *w_query_own]
    w_query_pair = [swapped(w, PLANE, pair) for w in w_query_own]
    got = swapped(out_pair, PLANE, pair)

    def out_block(i):
        at = slice(i * cols, (i + 1) * cols)
        return out_own[:, at] + got[:, at].astype(F32)

    to_3 = out_block(3).astype(BF16)
    from_3 = along(to_3, 1)
    from_1 = along(out_block(2).astype(BF16), 1)
    from_2 = along((out_block(1) + from_3.astype(F32)).astype(BF16), 2)
    out_proj_grad = out_block(0) + from_1.astype(F32) + from_2.astype(F32)

    w_kv = jnp.concatenate([pair_blocks(w_key, 0), pair_blocks(w_value, 0)], axis=0)
    blocks = feed(dquery_met, kv_met, w_query_own, w_query_pair, w_kv, [to_3])
    blocks = [(0, blocks[0])] + [(k, swapped(x, PLANE, k)) for k, x in zip(meets, blocks[1:])]
    grad_input = jnp.zeros((own_rows, features), BF16)
    for k, block in blocks:
        for i, owner in enumerate((plane_rank ^ k, plane_rank ^ k ^ pair)):
            grad_input = lax.dynamic_update_slice_in_dim(
                grad_input, block[:, i * width : (i + 1) * width], owner * width, axis=1
            )
    return (grad_input, out_proj_grad)


def solution(mesh):
    placed = (
        P(("dp", "context", "tensor"), None),
        P(("dp", "context"), "tensor"),
        P(("dp", "context"), "tensor"),
        P(("dp", "context"), None),
        P(("dp", "context"), None),
        P("tensor", ("dp", "context")),
        P("dp", None),
        P(("dp", "context"), "tensor"),
        P("tensor", ("dp", "context")),
        P(),
        P(),
    )
    return jax.shard_map(
        on_device,
        mesh=mesh,
        in_specs=placed,
        out_specs=(P(("dp", "context", "tensor"), None), P(("dp", "context"), "tensor")),
        check_vma=False,
    )
```

time: 227 us -> 206 us (0.907); the launches traced: 223 us -> 206 us
  Pallas kernels: 2.41 us -> 25.8 us
  waiting for transfers between devices: 128 us -> 106 us
  starting transfers between devices: 59.3 us -> 46.1 us
  matrix products: 9.34 us -> 0 us
  other arithmetic: 3.96 us -> 9.43 us
    pallas_call x1 -> x8, Pallas kernels: 2.41 us -> 25.8 us  [the longest x1 7.07 us: feed(): pl.pallas_call(functools.partial(feed_kernel, tokens=len(queries), sides=...]
    ppermute x49 -> x45, waiting for transfers between devices: 128 us -> 106 us  [swapped(): return lax.ppermute(x, axes, [(i, i ^ bit) for i in range(size)])]
    ppermute x49 -> x45, starting transfers between devices: 59.3 us -> 46.1 us  [swapped(): return lax.ppermute(x, axes, [(i, i ^ bit) for i in range(size)])]
    dot_general x4 -> x0, matrix products: 9.34 us -> none  [the longest x1 3.93 us: on_device(): jnp.dot(tokens, jnp.concatenate(w_out_all, axis=1), preferred_element_typ...]
    convert_element_type x2 -> x4, other arithmetic: 0.2 us -> 3.81 us  [the longest x1 2.29 us: on_device(): from_1 = along(out_block(2).astype(BF16), 1)]
    unnamed x42 -> x93, local copies, waits for them, and re-layouts: 12.5 us -> 15.6 us
  transfers between devices with their start and end apart: 49 -> 45, of which waited for: 27 -> 22; matrix products, arithmetic and copies ran while one was open for 13% -> 4% of each run, Pallas kernels for 1% -> 10%
where the time goes in v2:
time: 206 us
  waiting for transfers between devices  106 us (51%)
  starting transfers between devices  46.1 us (22%)
  Pallas kernels  25.8 us (13%)
  local copies, waits for them, and re-layouts  17.4 us (8%)
  other arithmetic  9.43 us (5%)
    ppermute x45, waiting for transfers between devices, swapped(): return lax.ppermute(x, axes, [(i, i ^ bit) for i in range(size)])  106 us
    ppermute x45, starting transfers between devices, swapped(): return lax.ppermute(x, axes, [(i, i ^ bit) for i in range(size)])  46.1 us
    unnamed x93, local copies, waits for them, and re-layouts  15.6 us
    pallas_call x1, Pallas kernels, feed(): pl.pallas_call(functools.partial(feed_kernel, tokens=len(queries), sides=...  7.07 us
    pallas_call x1, Pallas kernels, project(): pl.pallas_call(functools.partial(project_kernel, tokens=len(tokens), star...  5.35 us
    pallas_call x1, Pallas kernels, outer(): pl.pallas_call(functools.partial(outer_kernel, tokens=len(tokens), atts=l...  4.95 us
  transfers between devices with their start and end apart: 45, of which 22 were waited for; matrix products, arithmetic and copies ran while one was open for 4% of the time, Pallas kernels for 10%

profile of v2, /device:TPU:0, one launch (start us, length us, event | category | flops | bytes accessed | tf_op | source)
XLA Modules:
  0.0 205.6 jit_solution(2239985101284558380)
XLA Ops:
  0.7 1.6 copy-done.10
  4.6 4.1 %collective-permute-start.3 = (bf16[1280,256]{1,0:T(8,128)(2,1)S(1)}, bf16[1280,256]{1,0:T(8,128)(2,1)S(1)}, u32[]{:S(2)}, u32[]{:S(2)}) collective-permute-start(bf16[1280,256]{1,0:T(8,128)(2,1)S(1)} %get-tuple-element.44), channel_id=1, source_target_pairs={{0,2},{1,3},{2,0},{3,1},{4,6},{5,7},{6,4},{7,5},{8,10},{9,11},{10,... | collective-permute-start | bytes 1966088 | tf_op jit(solution)/shard_map/ppermute | solution.py:19
  8.7 1.5 collective-permute-start
  10.2 1.5 collective-permute-start.1
  12.2 1.6 collective-permute-start.4
  13.7 9.8 %collective-permute-done.refs_0_.refs_2_.refs_1_ = bf16[128,2048]{1,0:T(8,128)(2,1)S(1)} collective-permute-done((bf16[128,2048]{1,0:T(8,128)(2,1)S(1)}, bf16[128,2048]{1,0:T(8,128)(2,1)S(1)}, u32[]{:S(2)}, u32[]{:S(2)}) %collective-permute-start) | collective-permute-done | bytes 524320 | tf_op jit(solution)/shard_map/ppermute | solution.py:19
  23.5 11.0 %collective-permute-done.1.refs_1_.refs_3_.refs_2_ = bf16[128,2048]{1,0:T(8,128)(2,1)S(1)} collective-permute-done((bf16[128,2048]{1,0:T(8,128)(2,1)S(1)}, bf16[128,2048]{1,0:T(8,128)(2,1)S(1)}, u32[]{:S(2)}, u32[]{:S(2)}) %collective-permute-start.1) | collective-permute-done | bytes 524320 | tf_op jit(solution)/shard_map/ppermute | solution.py:19
  34.5 3.0 %collective-permute-done.3.x_ref.refs_6_ = bf16[1280,256]{1,0:T(8,128)(2,1)S(1)} collective-permute-done((bf16[1280,256]{1,0:T(8,128)(2,1)S(1)}, bf16[1280,256]{1,0:T(8,128)(2,1)S(1)}, u32[]{:S(2)}, u32[]{:S(2)}) %collective-permute-start.3) | collective-permute-done | bytes 655392 | tf_op jit(solution)/shard_map/ppermute | solution.py:19
  39.1 13.1 %collective-permute-done.5.refs_8_ = bf16[1152,256]{1,0:T(8,128)(2,1)} collective-permute-done((bf16[1152,256]{1,0:T(8,128)(2,1)S(1)}, bf16[1152,256]{1,0:T(8,128)(2,1)}, u32[]{:S(2)}, u32[]{:S(2)}) %collective-permute-start.5) | collective-permute-done | bytes 589856 | tf_op jit(solution)/shard_map/ppermute | solution.py:19
  52.8 1.3 collective-permute-start.10
  54.1 4.1 %collective-permute-done.10.refs_13_.refs_4_ = bf16[256,256]{1,0:T(8,128)(2,1)S(1)} collective-permute-done((bf16[256,256]{1,0:T(8,128)(2,1)S(1)}, bf16[256,256]{1,0:T(8,128)(2,1)S(1)}, u32[]{:S(2)}, u32[]{:S(2)}) %collective-permute-start.10) | collective-permute-done | bytes 131104 | tf_op jit(solution)/shard_map/ppermute | solution.py:19
  58.2 3.1 %collective-permute-start.17 = (bf16[256,1024]{1,0:T(8,128)(2,1)}, bf16[256,1024]{1,0:T(8,128)(2,1)S(1)}, u32[]{:S(2)}, u32[]{:S(2)}) collective-permute-start(bf16[256,1024]{1,0:T(8,128)(2,1)} %refs_8_.1), channel_id=1, source_target_pairs={{0,2},{1,3},{2,0},{3,1},{4,6},{5,7},{6,4},{7,5},{8,10},{9,11},{10,... | collective-permute-start | bytes 1572872 | tf_op jit(solution)/shard_map/ppermute | solution.py:19
  61.4 5.4 %project.1 = (f32[128,1024]{1,0:T(8,128)S(1)}, bf16[128,1024]{1,0:T(8,128)(2,1)}, bf16[128,1024]{1,0:T(8,128)(2,1)}, bf16[128,1024]{1,0:T(8,128)(2,1)}, bf16[128,1024]{1,0:T(8,128)(2,1)}) custom-call(bf16[128,256]{1,0:T(8,128)(2,1)S(1)} %get-tuple-element.39.refs_0_, bf16[128,2048]{1,0:T(8,128)(2,1)S(1)} %get-tuple-element.40.refs_1_.refs_0_, ...), custom_call_target="tpu_custom_call" | custom-call | tf_op jit(solution)/shard_map/project/pallas_call | solution.py:105
  67.5 1.5 collective-permute-start.11
  69.0 1.7 collective-permute-start.18
  70.8 1.5 collective-permute-start.12
  72.8 3.8 %collective-permute-done.11.refs_0_ = bf16[128,1024]{1,0:T(8,128)(2,1)S(1)} collective-permute-done((bf16[128,1024]{1,0:T(8,128)(2,1)}, bf16[128,1024]{1,0:T(8,128)(2,1)S(1)}, u32[]{:S(2)}, u32[]{:S(2)}) %collective-permute-start.11) | collective-permute-done | bytes 262176 | tf_op jit(solution)/shard_map/ppermute | solution.py:19
  76.6 1.9 collective-permute-start.31
  78.8 4.4 %collective-permute-done.12.refs_1_ = bf16[128,1024]{1,0:T(8,128)(2,1)} collective-permute-done((bf16[128,1024]{1,0:T(8,128)(2,1)}, bf16[128,1024]{1,0:T(8,128)(2,1)}, u32[]{:S(2)}, u32[]{:S(2)}) %collective-permute-start.12) | collective-permute-done | bytes 262176 | tf_op jit(solution)/shard_map/ppermute | solution.py:19
  83.3 2.0 add_up.1
  85.6 1.9 collective-permute-start.15
  87.5 2.4 %collective-permute-start.16 = (bf16[128,256]{1,0:T(8,128)(2,1)}, bf16[128,256]{1,0:T(8,128)(2,1)S(1)}, u32[]{:S(2)}, u32[]{:S(2)}) collective-permute-start(bf16[128,256]{1,0:T(8,128)(2,1)} %get-tuple-element.53), channel_id=1, source_target_pairs={{0,3},{1,2},{2,1},{3,0},{4,7},{5,6},{6,5},{7,4},{8,11},{9,10},{10,... | collective-permute-start | bytes 196616 | tf_op jit(solution)/shard_map/ppermute | solution.py:19
  89.9 5.2 %collective-permute-done.18.refs_6_.refs_1_ = bf16[256,1024]{1,0:T(8,128)(2,1)S(1)} collective-permute-done((bf16[256,1024]{1,0:T(8,128)(2,1)}, bf16[256,1024]{1,0:T(8,128)(2,1)S(1)}, u32[]{:S(2)}, u32[]{:S(2)}) %collective-permute-start.18) | collective-permute-done | bytes 524320 | tf_op jit(solution)/shard_map/ppermute | solution.py:19
  99.5 3.0 %attention.1 = (bf16[128,256]{1,0:T(8,128)(2,1)S(1)}, bf16[128,256]{1,0:T(8,128)(2,1)S(1)}, bf16[128,256]{1,0:T(8,128)(2,1)S(1)}, bf16[128,256]{1,0:T(8,128)(2,1...) custom-call(s32[3]{0:T(128)S(1)} %pad_add_fusion.4.ranks_ref, s32[512,1]{1,0:T(8,128)S(1)} %copy.20.seg_query_ref, ...), custom_call_target="tpu_custom_call" | custom-call | tf_op jit(solution)/shard_map/attention/pallas_call | solution.py:360
  103.9 1.5 collective-permute-start.22
  106.3 2.4 %collective-permute-start.20 = (bf16[128,256]{1,0:T(8,128)(2,1)S(1)}, bf16[128,256]{1,0:T(8,128)(2,1)S(1)}, u32[]{:S(2)}, u32[]{:S(2)}) collective-permute-start(bf16[128,256]{1,0:T(8,128)(2,1)S(1)} %get-tuple-element.57), channel_id=1, source_target_pairs={{0,1},{1,0},{2,3},{3,2},{4,5},{5,4},{6,7},{7,6},{8,9},{9,8},{10,11... | collective-permute-start | bytes 196616 | tf_op jit(solution)/shard_map/ppermute | solution.py:19
  109.8 1.9 pad_maximum_fusion
  112.3 2.4 %collective-permute-done.21.refs_5_ = bf16[128,256]{1,0:T(8,128)(2,1)S(1)} collective-permute-done((bf16[128,256]{1,0:T(8,128)(2,1)S(1)}, bf16[128,256]{1,0:T(8,128)(2,1)S(1)}, u32[]{:S(2)}, u32[]{:S(2)}) %collective-permute-start.21) | collective-permute-done | bytes 65568 | tf_op jit(solution)/shard_map/ppermute | solution.py:19
  115.4 2.1 %join.1 = (bf16[128,1024]{1,0:T(8,128)(2,1)}, bf16[256,256]{1,0:T(8,128)(2,1)}, f32[128,256]{1,0:T(8,128)}, f32[128,256]{1,0:T(8,128)}, bf16[256,1024]{1,0:T(8,128)(2,1)}, /*index=5*/bf16[256,1024]{1,0:T(8,128)(2,1)}) custom-call(s32[3]{0:T(128)} %copy-done.25, f32[512,256]{1,0:T(8,128)} %copy-done.16, ...), custom_call_target="tpu_custom_call", output_to_operand_aliasing={{4}: (2, {}), {5}: (3, {})} | custom-call | tf_op jit(solution)/shard_map/join/pallas_call | solution.py:188
  118.1 1.7 collective-permute-start.26
  119.8 8.8 %collective-permute-done.26.refs_11_ = bf16[256,256]{1,0:T(8,128)(2,1)S(1)} collective-permute-done((bf16[256,256]{1,0:T(8,128)(2,1)}, bf16[256,256]{1,0:T(8,128)(2,1)S(1)}, u32[]{:S(2)}, u32[]{:S(2)}) %collective-permute-start.26) | collective-permute-done | bytes 131104 | tf_op jit(solution)/shard_map/ppermute | solution.py:19
  128.6 2.1 %collective-permute-done.33.refs_9_ = bf16[256,1024]{1,0:T(8,128)(2,1)S(1)} collective-permute-done((bf16[256,1024]{1,0:T(8,128)(2,1)}, bf16[256,1024]{1,0:T(8,128)(2,1)S(1)}, u32[]{:S(2)}, u32[]{:S(2)}) %collective-permute-start.33) | collective-permute-done | bytes 524320 | tf_op jit(solution)/shard_map/ppermute | solution.py:19
  132.8 4.9 %outer.1 = (f32[1024,1024]{1,0:T(8,128)S(1)}, bf16[1024,1024]{1,0:T(8,128)(2,1)}, bf16[256,1024]{1,0:T(8,128)(2,1)S(1)}, bf16[256,1024]{1,0:T(8,128)(2,1)S(1)}, bf16[256,1024]{1,0:T(8,128)(2,1)S(1)}) custom-call(bf16[128,2048]{1,0:T(8,128)(2,1)S(1)} %copy-done.12, ...), custom_call_target="tpu_custom_call", output_to_operand_aliasing={{2}: (7, {}), {3}: (8, {}), {4}: (9, {})} | custom-call | tf_op jit(solution)/shard_map/outer/pallas_call | solution.py:230
  139.4 2.0 copy-done.8
  143.7 1.3 constant_dynamic-slice_fusion.1
  145.0 2.9 %collective-permute-done.27 = bf16[128,256]{1,0:T(8,128)(2,1)S(1)} collective-permute-done((bf16[128,256]{1,0:T(8,128)(2,1)S(1)}, bf16[128,256]{1,0:T(8,128)(2,1)S(1)}, u32[]{:S(2)}, u32[]{:S(2)}) %collective-permute-start.27) | collective-permute-done | bytes 65568 | tf_op jit(solution)/shard_map/ppermute | solution.py:19
  148.0 1.9 collective-permute-start.28
  150.5 6.2 %collective-permute-done.24.refs_2_ = bf16[128,1024]{1,0:T(8,128)(2,1)S(1)} collective-permute-done((bf16[128,1024]{1,0:T(8,128)(2,1)S(1)}, bf16[128,1024]{1,0:T(8,128)(2,1)S(1)}, u32[]{:S(2)}, u32[]{:S(2)}) %collective-permute-start.24) | collective-permute-done | bytes 262176 | tf_op jit(solution)/shard_map/ppermute | solution.py:19
  157.3 1.5 add_convert_fusion.2.refs_17_
  160.1 4.1 %collective-permute-done.30.refs_7_ = bf16[128,256]{1,0:T(8,128)(2,1)S(1)} collective-permute-done((bf16[128,256]{1,0:T(8,128)(2,1)S(1)}, bf16[128,256]{1,0:T(8,128)(2,1)S(1)}, u32[]{:S(2)}, u32[]{:S(2)}) %collective-permute-start.30) | collective-permute-done | bytes 65568 | tf_op jit(solution)/shard_map/ppermute | solution.py:19
  164.8 7.1 %feed.1 = (bf16[128,2048]{1,0:T(8,128)(2,1)}, bf16[128,2048]{1,0:T(8,128)(2,1)}, bf16[128,2048]{1,0:T(8,128)(2,1)}, bf16[128,2048]{1,0:T(8,128)(2,1)}) custom-call(bf16[128,1024]{1,0:T(8,128)(2,1)} %get-tuple-element.60.refs_0_, bf16[128,1024]{1,0:T(8,128)(2,1)} %copy-done.13, bf16[128,1024]{1,0:T(8,128)(2,1)} %copy-done.31, bf16[128,1024]{1,0:T(8,128)(2,1)} %copy-done.32, ...), custom_call_target="tpu_custom_call" | custom-call | tf_op jit(solution)/shard_map/feed/pallas_call | solution.py:274
  172.8 2.7 %collective-permute-start.41 = (bf16[128,2048]{1,0:T(8,128)(2,1)}, bf16[128,2048]{1,0:T(8,128)(2,1)S(1)}, u32[]{:S(2)}, u32[]{:S(2)}) collective-permute-start(bf16[128,2048]{1,0:T(8,128)(2,1)} %get-tuple-element.75), channel_id=1, source_target_pairs={{0,20},{4,16},{8,28},{12,24},{16,4},{20,0},{24,12},{28,8},{1,21},{... | collective-permute-start | bytes 1572872 | tf_op jit(solution)/shard_map/ppermute | solution.py:19
  175.8 2.3 %add_convert_fusion.1 = (bf16[1024,256]{1,0:T(8,128)(2,1)S(1)}, bf16[1024,256]{1,0:T(8,128)(2,1)S(1)}) fusion(f32[1024,1024]{1,0:T(8,128)} %copy-done.8, bf16[1024,1024]{1,0:T(8,128)(2,1)} %collective-permute-done.38, bf16[1024,256]{1,0:T(8,128)(2,1)} %collective-permute-done.43), kind=kLoop, calls=%fused_computation.3 | loop fusion | flops 2097152 | bytes 4718592 | tf_op jit(solution)/shard_map/convert_element_type | solution.py:486
  178.1 1.6 collective-permute-start.44
  179.7 7.3 %collective-permute-done.39 = bf16[128,2048]{1,0:T(8,128)(2,1)S(1)} collective-permute-done((bf16[128,2048]{1,0:T(8,128)(2,1)}, bf16[128,2048]{1,0:T(8,128)(2,1)S(1)}, u32[]{:S(2)}, u32[]{:S(2)}) %collective-permute-start.39) | collective-permute-done | bytes 524320 | tf_op jit(solution)/shard_map/ppermute | solution.py:19
  187.1 9.9 %collective-permute-done.40 = bf16[128,2048]{1,0:T(8,128)(2,1)S(1)} collective-permute-done((bf16[128,2048]{1,0:T(8,128)(2,1)}, bf16[128,2048]{1,0:T(8,128)(2,1)S(1)}, u32[]{:S(2)}, u32[]{:S(2)}) %collective-permute-start.40) | collective-permute-done | bytes 524320 | tf_op jit(solution)/shard_map/ppermute | solution.py:19
  197.1 4.7 %collective-permute-done.42 = bf16[1024,256]{1,0:T(8,128)(2,1)S(1)} collective-permute-done((bf16[1024,256]{1,0:T(8,128)(2,1)S(1)}, bf16[1024,256]{1,0:T(8,128)(2,1)S(1)}, u32[]{:S(2)}, u32[]{:S(2)}) %collective-permute-start.42) | collective-permute-done | bytes 524320 | tf_op jit(solution)/shard_map/ppermute | solution.py:19
  203.0 2.6 %convert_add_fusion = f32[1024,256]{1,0:T(8,128)} fusion(bf16[1024,256]{1,0:T(8,128)(2,1)S(1)} %collective-permute-done.44, bf16[1024,256]{1,0:T(8,128)(2,1)S(1)} %collective-permute-done.42, f32[1024,1024]{1,0:T(8,128)} %copy-done.8, bf16[1024,1024]{1,0:T(8,128)(2,1)} %collective-permute-done.38), kind=kLoop, calls=%fused_computation.1 | loop fusion | flops 1572864 | bytes 3670016 | tf_op jit(solution)/shard_map/add | solution.py:488
  (166 shorter events, 28.1 us)
Async XLA Ops:
  3.3 92.6 %copy-start.25 = (s32[3]{0:T(128)}, s32[3]{0:T(128)S(1)}, u32[]{:S(2)}) copy-start(s32[3]{0:T(128)S(1)} %pad_add_fusion.4.ranks_ref) | copy-start | bytes 40
  4.5 62.2 %copy-start.11 = (bf16[128,2048]{1,0:T(8,128)(2,1)}, bf16[128,2048]{1,0:T(8,128)(2,1)S(1)}, u32[]{:S(2)}) copy-start(bf16[128,2048]{1,0:T(8,128)(2,1)S(1)} %get-tuple-element.40.refs_1_.refs_0_) | copy-start | bytes 1572868
  4.6 48.2 %copy-start.17 = (bf16[512,128]{1,0:T(8,128)(2,1)S(1)}, bf16[512,128]{1,0:T(8,128)(2,1)}, u32[]{:S(2)}) copy-start(bf16[512,128]{1,0:T(8,128)(2,1)} %key_ref.1) | copy-start | bytes 393220
  4.6 33.0 %collective-permute-start.3 = (bf16[1280,256]{1,0:T(8,128)(2,1)S(1)}, bf16[1280,256]{1,0:T(8,128)(2,1)S(1)}, u32[]{:S(2)}, u32[]{:S(2)}) collective-permute-start(bf16[1280,256]{1,0:T(8,128)(2,1)S(1)} %get-tuple-element.44), channel_id=1, source_target_pairs={{0,2},{1,3},{2,0},{3,1},{4,6},{5,7},{6,4},{7,5},{8,10},{9,11},{10,... | collective-permute-start | bytes 1966088 | tf_op jit(solution)/shard_map/ppermute | solution.py:19
  8.7 14.8 %collective-permute-start = (bf16[128,2048]{1,0:T(8,128)(2,1)S(1)}, bf16[128,2048]{1,0:T(8,128)(2,1)S(1)}, u32[]{:S(2)}, u32[]{:S(2)}) collective-permute-start(bf16[128,2048]{1,0:T(8,128)(2,1)S(1)} %get-tuple-element.41), channel_id=1, source_target_pairs={{0,16},{4,20},{8,24},{12,28},{16,0},{20,4},{24,8},{28,12},{1,17},{... | collective-permute-start | bytes 1572872 | tf_op jit(solution)/shard_map/ppermute | solution.py:19
  10.2 24.3 %collective-permute-start.1 = (bf16[128,2048]{1,0:T(8,128)(2,1)S(1)}, bf16[128,2048]{1,0:T(8,128)(2,1)S(1)}, u32[]{:S(2)}, u32[]{:S(2)}) collective-permute-start(bf16[128,2048]{1,0:T(8,128)(2,1)S(1)} %get-tuple-element.42), channel_id=1, source_target_pairs={{0,4},{4,0},{8,12},{12,8},{16,20},{20,16},{24,28},{28,24},{1,5},{5... | collective-permute-start | bytes 1572872 | tf_op jit(solution)/shard_map/ppermute | solution.py:19
  11.7 22.8 %collective-permute-start.2 = (bf16[128,2048]{1,0:T(8,128)(2,1)S(1)}, bf16[128,2048]{1,0:T(8,128)(2,1)S(1)}, u32[]{:S(2)}, u32[]{:S(2)}) collective-permute-start(bf16[128,2048]{1,0:T(8,128)(2,1)S(1)} %get-tuple-element.43), channel_id=1, source_target_pairs={{0,20},{4,16},{8,28},{12,24},{16,4},{20,0},{24,12},{28,8},{1,21},{... | collective-permute-start | bytes 1572872 | tf_op jit(solution)/shard_map/ppermute | solution.py:19
  12.2 26.9 %collective-permute-start.4 = (bf16[1152,256]{1,0:T(8,128)(2,1)S(1)}, bf16[1152,256]{1,0:T(8,128)(2,1)}, u32[]{:S(2)}, u32[]{:S(2)}) collective-permute-start(bf16[1152,256]{1,0:T(8,128)(2,1)S(1)} %get-tuple-element.45), channel_id=1, source_target_pairs={{0,1},{1,0},{2,3},{3,2},{4,5},{5,4},{6,7},{7,6},{8,9},{9,8},{10,11... | collective-permute-start | bytes 1769480 | tf_op jit(solution)/shard_map/ppermute | solution.py:19
  37.6 14.6 %collective-permute-start.5 = (bf16[1152,256]{1,0:T(8,128)(2,1)S(1)}, bf16[1152,256]{1,0:T(8,128)(2,1)}, u32[]{:S(2)}, u32[]{:S(2)}) collective-permute-start(bf16[1152,256]{1,0:T(8,128)(2,1)S(1)} %hand_on.1), channel_id=1, source_target_pairs={{0,1},{1,0},{2,3},{3,2},{4,5},{5,4},{6,7},{7,6},{8,9},{9,8},{10,11... | collective-permute-start | bytes 1769480 | tf_op jit(solution)/shard_map/ppermute | solution.py:19
  38.3 23.0 %collective-permute-start.7 = (bf16[1280,256]{1,0:T(8,128)(2,1)S(1)}, bf16[1280,256]{1,0:T(8,128)(2,1)}, u32[]{:S(2)}, u32[]{:S(2)}) collective-permute-start(bf16[1280,256]{1,0:T(8,128)(2,1)S(1)} %collective-permute-done.3.x_ref.refs_6_), channel_id=1, source_target_pairs={{0,8},{4,12},{8,0},{12,4},{16,24},{20,28},{24,16},{28,20},{1,9},{5... | collective-permute-start | bytes 1966088 | tf_op jit(solution)/shard_map/ppermute | solution.py:19
  39.1 22.2 %collective-permute-start.8 = (bf16[1152,256]{1,0:T(8,128)(2,1)}, bf16[1152,256]{1,0:T(8,128)(2,1)}, u32[]{:S(2)}, u32[]{:S(2)}) collective-permute-start(bf16[1152,256]{1,0:T(8,128)(2,1)} %collective-permute-done.4.refs_7_), channel_id=1, source_target_pairs={{0,8},{4,12},{8,0},{12,4},{16,24},{20,28},{24,16},{28,20},{1,9},{5... | collective-permute-start | bytes 1769480 | tf_op jit(solution)/shard_map/ppermute | solution.py:19
  52.2 9.1 %collective-permute-start.9 = (bf16[1152,256]{1,0:T(8,128)(2,1)}, bf16[1152,256]{1,0:T(8,128)(2,1)}, u32[]{:S(2)}, u32[]{:S(2)}) collective-permute-start(bf16[1152,256]{1,0:T(8,128)(2,1)} %collective-permute-done.5.refs_8_), channel_id=1, source_target_pairs={{0,8},{4,12},{8,0},{12,4},{16,24},{20,28},{24,16},{28,20},{1,9},{5... | collective-permute-start | bytes 1769480 | tf_op jit(solution)/shard_map/ppermute | solution.py:19
  52.2 9.1 %collective-permute-start.6 = (bf16[1024,256]{1,0:T(8,128)(2,1)}, bf16[1024,256]{1,0:T(8,128)(2,1)}, u32[]{:S(2)}, u32[]{:S(2)}) collective-permute-start(bf16[1024,256]{1,0:T(8,128)(2,1)} %refs_5_.1), channel_id=1, source_target_pairs={{0,8},{4,12},{8,0},{12,4},{16,24},{20,28},{24,16},{28,20},{1,9},{5... | collective-permute-start | bytes 1572872 | tf_op jit(solution)/shard_map/ppermute | solution.py:19
  52.8 5.5 %collective-permute-start.10 = (bf16[256,256]{1,0:T(8,128)(2,1)S(1)}, bf16[256,256]{1,0:T(8,128)(2,1)S(1)}, u32[]{:S(2)}, u32[]{:S(2)}) collective-permute-start(bf16[256,256]{1,0:T(8,128)(2,1)S(1)} %fusion), channel_id=1, source_target_pairs={{0,4},{4,0},{1,5},{5,1},{2,6},{6,2},{3,7},{7,3},{8,12},{12,8},{9,1... | collective-permute-start | bytes 393224 | tf_op jit(solution)/shard_map/ppermute | solution.py:19
  58.2 29.2 %collective-permute-start.17 = (bf16[256,1024]{1,0:T(8,128)(2,1)}, bf16[256,1024]{1,0:T(8,128)(2,1)S(1)}, u32[]{:S(2)}, u32[]{:S(2)}) collective-permute-start(bf16[256,1024]{1,0:T(8,128)(2,1)} %refs_8_.1), channel_id=1, source_target_pairs={{0,2},{1,3},{2,0},{3,1},{4,6},{5,7},{6,4},{7,5},{8,10},{9,11},{10,... | collective-permute-start | bytes 1572872 | tf_op jit(solution)/shard_map/ppermute | solution.py:19
  67.5 9.0 %collective-permute-start.11 = (bf16[128,1024]{1,0:T(8,128)(2,1)}, bf16[128,1024]{1,0:T(8,128)(2,1)S(1)}, u32[]{:S(2)}, u32[]{:S(2)}) collective-permute-start(bf16[128,1024]{1,0:T(8,128)(2,1)} %get-tuple-element.47), channel_id=1, source_target_pairs={{0,16},{4,20},{8,24},{12,28},{16,0},{20,4},{24,8},{28,12},{1,17},{... | collective-permute-start | bytes 786440 | tf_op jit(solution)/shard_map/ppermute | solution.py:19
  69.0 26.1 %collective-permute-start.18 = (bf16[256,1024]{1,0:T(8,128)(2,1)}, bf16[256,1024]{1,0:T(8,128)(2,1)S(1)}, u32[]{:S(2)}, u32[]{:S(2)}) collective-permute-start(bf16[256,1024]{1,0:T(8,128)(2,1)} %refs_8_.1), channel_id=1, source_target_pairs={{0,1},{1,0},{2,3},{3,2},{4,5},{5,4},{6,7},{7,6},{8,9},{9,8},{10,11... | collective-permute-start | bytes 1572872 | tf_op jit(solution)/shard_map/ppermute | solution.py:19
  70.8 12.4 %collective-permute-start.12 = (bf16[128,1024]{1,0:T(8,128)(2,1)}, bf16[128,1024]{1,0:T(8,128)(2,1)}, u32[]{:S(2)}, u32[]{:S(2)}) collective-permute-start(bf16[128,1024]{1,0:T(8,128)(2,1)} %get-tuple-element.48), channel_id=1, source_target_pairs={{0,4},{4,0},{8,12},{12,8},{16,20},{20,16},{24,28},{28,24},{1,5},{5... | collective-permute-start | bytes 786440 | tf_op jit(solution)/shard_map/ppermute | solution.py:19
  72.3 11.0 %collective-permute-start.13 = (bf16[128,1024]{1,0:T(8,128)(2,1)}, bf16[128,1024]{1,0:T(8,128)(2,1)}, u32[]{:S(2)}, u32[]{:S(2)}) collective-permute-start(bf16[128,1024]{1,0:T(8,128)(2,1)} %get-tuple-element.49), channel_id=1, source_target_pairs={{0,20},{4,16},{8,28},{12,24},{16,4},{20,0},{24,12},{28,8},{1,21},{... | collective-permute-start | bytes 786440 | tf_op jit(solution)/shard_map/ppermute | solution.py:19
  76.6 33.3 %collective-permute-start.31 = (bf16[128,1024]{1,0:T(8,128)(2,1)}, bf16[128,1024]{1,0:T(8,128)(2,1)}, u32[]{:S(2)}, u32[]{:S(2)}) collective-permute-start(bf16[128,1024]{1,0:T(8,128)(2,1)} %get-tuple-element.64.refs_4_), channel_id=1, source_target_pairs={{0,16},{4,20},{8,24},{12,28},{16,0},{20,4},{24,8},{28,12},{1,17},{... | collective-permute-start | bytes 786440 | tf_op jit(solution)/shard_map/ppermute | solution.py:19
  85.3 9.9 %collective-permute-start.14 = (bf16[128,256]{1,0:T(8,128)(2,1)}, bf16[128,256]{1,0:T(8,128)(2,1)S(1)}, u32[]{:S(2)}, u32[]{:S(2)}) collective-permute-start(bf16[128,256]{1,0:T(8,128)(2,1)} %get-tuple-element.51), channel_id=1, source_target_pairs={{0,2},{1,3},{2,0},{3,1},{4,6},{5,7},{6,4},{7,5},{8,10},{9,11},{10,... | collective-permute-start | bytes 196616 | tf_op jit(solution)/shard_map/ppermute | solution.py:19
  85.6 10.3 %collective-permute-start.15 = (bf16[128,256]{1,0:T(8,128)(2,1)}, bf16[128,256]{1,0:T(8,128)(2,1)S(1)}, u32[]{:S(2)}, u32[]{:S(2)}) collective-permute-start(bf16[128,256]{1,0:T(8,128)(2,1)} %get-tuple-element.52), channel_id=1, source_target_pairs={{0,1},{1,0},{2,3},{3,2},{4,5},{5,4},{6,7},{7,6},{8,9},{9,8},{10,11... | collective-permute-start | bytes 196616 | tf_op jit(solution)/shard_map/ppermute | solution.py:19
  87.5 8.4 %collective-permute-start.16 = (bf16[128,256]{1,0:T(8,128)(2,1)}, bf16[128,256]{1,0:T(8,128)(2,1)S(1)}, u32[]{:S(2)}, u32[]{:S(2)}) collective-permute-start(bf16[128,256]{1,0:T(8,128)(2,1)} %get-tuple-element.53), channel_id=1, source_target_pairs={{0,3},{1,2},{2,1},{3,0},{4,7},{5,6},{6,5},{7,4},{8,11},{9,10},{10,... | collective-permute-start | bytes 196616 | tf_op jit(solution)/shard_map/ppermute | solution.py:19
  103.9 10.8 %collective-permute-start.22 = (bf16[256,256]{1,0:T(8,128)(2,1)S(1)}, bf16[256,256]{1,0:T(8,128)(2,1)S(1)}, u32[]{:S(2)}, u32[]{:S(2)}) collective-permute-start(bf16[256,256]{1,0:T(8,128)(2,1)S(1)} %get-tuple-element.59), channel_id=1, source_target_pairs={{0,4},{4,0},{1,5},{5,1},{2,6},{6,2},{3,7},{7,3},{8,12},{12,8},{9,1... | collective-permute-start | bytes 393224 | tf_op jit(solution)/shard_map/ppermute | solution.py:19
  105.4 6.8 %collective-permute-start.19 = (bf16[128,256]{1,0:T(8,128)(2,1)S(1)}, bf16[128,256]{1,0:T(8,128)(2,1)S(1)}, u32[]{:S(2)}, u32[]{:S(2)}) collective-permute-start(bf16[128,256]{1,0:T(8,128)(2,1)S(1)} %get-tuple-element.56), channel_id=1, source_target_pairs={{0,2},{1,3},{2,0},{3,1},{4,6},{5,7},{6,4},{7,5},{8,10},{9,11},{10,... | collective-permute-start | bytes 196616 | tf_op jit(solution)/shard_map/ppermute | solution.py:19
  106.3 6.0 %collective-permute-start.20 = (bf16[128,256]{1,0:T(8,128)(2,1)S(1)}, bf16[128,256]{1,0:T(8,128)(2,1)S(1)}, u32[]{:S(2)}, u32[]{:S(2)}) collective-permute-start(bf16[128,256]{1,0:T(8,128)(2,1)S(1)} %get-tuple-element.57), channel_id=1, source_target_pairs={{0,1},{1,0},{2,3},{3,2},{4,5},{5,4},{6,7},{7,6},{8,9},{9,8},{10,11... | collective-permute-start | bytes 196616 | tf_op jit(solution)/shard_map/ppermute | solution.py:19
  108.7 6.1 %collective-permute-start.21 = (bf16[128,256]{1,0:T(8,128)(2,1)S(1)}, bf16[128,256]{1,0:T(8,128)(2,1)S(1)}, u32[]{:S(2)}, u32[]{:S(2)}) collective-permute-start(bf16[128,256]{1,0:T(8,128)(2,1)S(1)} %get-tuple-element.58), channel_id=1, source_target_pairs={{0,3},{1,2},{2,1},{3,0},{4,7},{5,6},{6,5},{7,4},{8,11},{9,10},{10,... | collective-permute-start | bytes 196616 | tf_op jit(solution)/shard_map/ppermute | solution.py:19
  111.7 16.9 %collective-permute-start.32 = (bf16[256,1024]{1,0:T(8,128)(2,1)}, bf16[256,1024]{1,0:T(8,128)(2,1)}, u32[]{:S(2)}, u32[]{:S(2)}) collective-permute-start(bf16[256,1024]{1,0:T(8,128)(2,1)} %pad_maximum_fusion), channel_id=1, source_target_pairs={{0,4},{4,0},{8,12},{12,8},{16,20},{20,16},{24,28},{28,24},{1,5},{5... | collective-permute-start | bytes 1572872 | tf_op jit(solution)/shard_map/ppermute | solution.py:19
  117.5 13.1 %collective-permute-start.33 = (bf16[256,1024]{1,0:T(8,128)(2,1)}, bf16[256,1024]{1,0:T(8,128)(2,1)S(1)}, u32[]{:S(2)}, u32[]{:S(2)}) collective-permute-start(bf16[256,1024]{1,0:T(8,128)(2,1)} %get-tuple-element.65.refs_7_), channel_id=1, source_target_pairs={{0,1},{1,0},{2,3},{3,2},{4,5},{5,4},{6,7},{7,6},{8,9},{9,8},{10,11... | collective-permute-start | bytes 1572872 | tf_op jit(solution)/shard_map/ppermute | solution.py:19
  117.5 11.0 %collective-permute-start.23 = (bf16[128,1024]{1,0:T(8,128)(2,1)}, bf16[128,1024]{1,0:T(8,128)(2,1)S(1)}, u32[]{:S(2)}, u32[]{:S(2)}) collective-permute-start(bf16[128,1024]{1,0:T(8,128)(2,1)} %get-tuple-element.60.refs_0_), channel_id=1, source_target_pairs={{0,16},{4,20},{8,24},{12,28},{16,0},{20,4},{24,8},{28,12},{1,17},{... | collective-permute-start | bytes 786440 | tf_op jit(solution)/shard_map/ppermute | solution.py:19
  118.1 10.5 %collective-permute-start.26 = (bf16[256,256]{1,0:T(8,128)(2,1)}, bf16[256,256]{1,0:T(8,128)(2,1)S(1)}, u32[]{:S(2)}, u32[]{:S(2)}) collective-permute-start(bf16[256,256]{1,0:T(8,128)(2,1)} %get-tuple-element.62), channel_id=1, source_target_pairs={{0,2},{1,3},{2,0},{3,1},{4,6},{5,7},{6,4},{7,5},{8,10},{9,11},{10,... | collective-permute-start | bytes 393224 | tf_op jit(solution)/shard_map/ppermute | solution.py:19
  141.4 15.8 %collective-permute-start.38 = (bf16[1024,1024]{1,0:T(8,128)(2,1)}, bf16[1024,1024]{1,0:T(8,128)(2,1)}, u32[]{:S(2)}, u32[]{:S(2)}) collective-permute-start(bf16[1024,1024]{1,0:T(8,128)(2,1)} %get-tuple-element.71), channel_id=1, source_target_pairs={{0,8},{4,12},{8,0},{12,4},{16,24},{20,28},{24,16},{28,20},{1,9},{5... | collective-permute-start | bytes 6291464 | tf_op jit(solution)/shard_map/ppermute | solution.py:19
  141.5 8.4 %collective-permute-start.34 = (bf16[256,1024]{1,0:T(8,128)(2,1)}, bf16[256,1024]{1,0:T(8,128)(2,1)S(1)}, u32[]{:S(2)}, u32[]{:S(2)}) collective-permute-start(bf16[256,1024]{1,0:T(8,128)(2,1)} %refs_8_.1), channel_id=1, source_target_pairs={{0,8},{4,12},{8,0},{12,4},{16,24},{20,28},{24,16},{28,20},{1,9},{5... | collective-permute-start | bytes 1572872 | tf_op jit(solution)/shard_map/ppermute | solution.py:19
  142.0 14.6 %collective-permute-start.24 = (bf16[128,1024]{1,0:T(8,128)(2,1)S(1)}, bf16[128,1024]{1,0:T(8,128)(2,1)S(1)}, u32[]{:S(2)}, u32[]{:S(2)}) collective-permute-start(bf16[128,1024]{1,0:T(8,128)(2,1)S(1)} %copy-done.30), channel_id=1, source_target_pairs={{0,4},{4,0},{8,12},{12,8},{16,20},{20,16},{24,28},{28,24},{1,5},{5... | collective-permute-start | bytes 786440 | tf_op jit(solution)/shard_map/ppermute | solution.py:19
  142.5 14.1 %collective-permute-start.25 = (bf16[128,1024]{1,0:T(8,128)(2,1)S(1)}, bf16[128,1024]{1,0:T(8,128)(2,1)S(1)}, u32[]{:S(2)}, u32[]{:S(2)}) collective-permute-start(bf16[128,1024]{1,0:T(8,128)(2,1)S(1)} %copy-done.30), channel_id=1, source_target_pairs={{0,20},{4,16},{8,28},{12,24},{16,4},{20,0},{24,12},{28,8},{1,21},{... | collective-permute-start | bytes 786440 | tf_op jit(solution)/shard_map/ppermute | solution.py:19
  143.7 4.3 %collective-permute-start.27 = (bf16[128,256]{1,0:T(8,128)(2,1)S(1)}, bf16[128,256]{1,0:T(8,128)(2,1)S(1)}, u32[]{:S(2)}, u32[]{:S(2)}) collective-permute-start(bf16[128,256]{1,0:T(8,128)(2,1)S(1)} %add_convert_fusion.4), channel_id=1, source_target_pairs={{0,1},{1,0},{2,3},{3,2},{4,5},{5,4},{6,7},{7,6},{8,9},{9,8},{10,11... | collective-permute-start | bytes 196616 | tf_op jit(solution)/shard_map/ppermute | solution.py:19
  148.0 10.8 %collective-permute-start.28 = (bf16[128,256]{1,0:T(8,128)(2,1)S(1)}, bf16[128,256]{1,0:T(8,128)(2,1)S(1)}, u32[]{:S(2)}, u32[]{:S(2)}) collective-permute-start(bf16[128,256]{1,0:T(8,128)(2,1)S(1)} %add_convert_fusion.3.refs_4_), channel_id=1, source_target_pairs={{0,16},{4,20},{8,24},{12,28},{16,0},{20,4},{24,8},{28,12},{1,17},{... | collective-permute-start | bytes 196616 | tf_op jit(solution)/shard_map/ppermute | solution.py:19
  149.9 9.0 %collective-permute-start.29 = (bf16[128,256]{1,0:T(8,128)(2,1)S(1)}, bf16[128,256]{1,0:T(8,128)(2,1)S(1)}, u32[]{:S(2)}, u32[]{:S(2)}) collective-permute-start(bf16[128,256]{1,0:T(8,128)(2,1)S(1)} %add_convert_fusion.3.refs_4_), channel_id=1, source_target_pairs={{0,4},{4,0},{8,12},{12,8},{16,20},{20,16},{24,28},{28,24},{1,5},{5... | collective-permute-start | bytes 196616 | tf_op jit(solution)/shard_map/ppermute | solution.py:19
  156.6 7.6 %collective-permute-start.35 = (bf16[256,1024]{1,0:T(8,128)(2,1)S(1)}, bf16[256,1024]{1,0:T(8,128)(2,1)}, u32[]{:S(2)}, u32[]{:S(2)}) collective-permute-start(bf16[256,1024]{1,0:T(8,128)(2,1)S(1)} %copy-done.3), channel_id=1, source_target_pairs={{0,8},{4,12},{8,0},{12,4},{16,24},{20,28},{24,16},{28,20},{1,9},{5... | collective-permute-start | bytes 1572872 | tf_op jit(solution)/shard_map/ppermute | solution.py:19
  156.6 7.6 %collective-permute-start.36 = (bf16[256,1024]{1,0:T(8,128)(2,1)S(1)}, bf16[256,1024]{1,0:T(8,128)(2,1)}, u32[]{:S(2)}, u32[]{:S(2)}) collective-permute-start(bf16[256,1024]{1,0:T(8,128)(2,1)S(1)} %copy-done.7), channel_id=1, source_target_pairs={{0,8},{4,12},{8,0},{12,4},{16,24},{20,28},{24,16},{28,20},{1,9},{5... | collective-permute-start | bytes 1572872 | tf_op jit(solution)/shard_map/ppermute | solution.py:19
  157.2 7.0 %collective-permute-start.37 = (bf16[256,1024]{1,0:T(8,128)(2,1)S(1)}, bf16[256,1024]{1,0:T(8,128)(2,1)}, u32[]{:S(2)}, u32[]{:S(2)}) collective-permute-start(bf16[256,1024]{1,0:T(8,128)(2,1)S(1)} %get-tuple-element.69.refs_11_), channel_id=1, source_target_pairs={{0,8},{4,12},{8,0},{12,4},{16,24},{20,28},{24,16},{28,20},{1,9},{5... | collective-permute-start | bytes 1572872 | tf_op jit(solution)/shard_map/ppermute | solution.py:19
  158.8 5.4 %collective-permute-start.30 = (bf16[128,256]{1,0:T(8,128)(2,1)S(1)}, bf16[128,256]{1,0:T(8,128)(2,1)S(1)}, u32[]{:S(2)}, u32[]{:S(2)}) collective-permute-start(bf16[128,256]{1,0:T(8,128)(2,1)S(1)} %add_convert_fusion.3.refs_4_), channel_id=1, source_target_pairs={{0,20},{4,16},{8,28},{12,24},{16,4},{20,0},{24,12},{28,8},{1,21},{... | collective-permute-start | bytes 196616 | tf_op jit(solution)/shard_map/ppermute | solution.py:19
  159.0 16.8 %collective-permute-start.43 = (bf16[1024,256]{1,0:T(8,128)(2,1)S(1)}, bf16[1024,256]{1,0:T(8,128)(2,1)}, u32[]{:S(2)}, u32[]{:S(2)}) collective-permute-start(bf16[1024,256]{1,0:T(8,128)(2,1)S(1)} %add_convert_fusion.2.refs_17_), channel_id=1, source_target_pairs={{0,1},{1,0},{2,3},{3,2},{4,5},{5,4},{6,7},{7,6},{8,9},{9,8},{10,11... | collective-permute-start | bytes 1572872 | tf_op jit(solution)/shard_map/ppermute | solution.py:19
  171.9 15.1 %collective-permute-start.39 = (bf16[128,2048]{1,0:T(8,128)(2,1)}, bf16[128,2048]{1,0:T(8,128)(2,1)S(1)}, u32[]{:S(2)}, u32[]{:S(2)}) collective-permute-start(bf16[128,2048]{1,0:T(8,128)(2,1)} %get-tuple-element.73), channel_id=1, source_target_pairs={{0,16},{4,20},{8,24},{12,28},{16,0},{20,4},{24,8},{28,12},{1,17},{... | collective-permute-start | bytes 1572872 | tf_op jit(solution)/shard_map/ppermute | solution.py:19
  172.2 24.8 %collective-permute-start.40 = (bf16[128,2048]{1,0:T(8,128)(2,1)}, bf16[128,2048]{1,0:T(8,128)(2,1)S(1)}, u32[]{:S(2)}, u32[]{:S(2)}) collective-permute-start(bf16[128,2048]{1,0:T(8,128)(2,1)} %get-tuple-element.74), channel_id=1, source_target_pairs={{0,4},{4,0},{8,12},{12,8},{16,20},{20,16},{24,28},{28,24},{1,5},{5... | collective-permute-start | bytes 1572872 | tf_op jit(solution)/shard_map/ppermute | solution.py:19
  172.8 24.2 %collective-permute-start.41 = (bf16[128,2048]{1,0:T(8,128)(2,1)}, bf16[128,2048]{1,0:T(8,128)(2,1)S(1)}, u32[]{:S(2)}, u32[]{:S(2)}) collective-permute-start(bf16[128,2048]{1,0:T(8,128)(2,1)} %get-tuple-element.75), channel_id=1, source_target_pairs={{0,20},{4,16},{8,28},{12,24},{16,4},{20,0},{24,12},{28,8},{1,21},{... | collective-permute-start | bytes 1572872 | tf_op jit(solution)/shard_map/ppermute | solution.py:19
  178.0 23.7 %collective-permute-start.42 = (bf16[1024,256]{1,0:T(8,128)(2,1)S(1)}, bf16[1024,256]{1,0:T(8,128)(2,1)S(1)}, u32[]{:S(2)}, u32[]{:S(2)}) collective-permute-start(bf16[1024,256]{1,0:T(8,128)(2,1)S(1)} %get-tuple-element.76), channel_id=1, source_target_pairs={{0,1},{1,0},{2,3},{3,2},{4,5},{5,4},{6,7},{7,6},{8,9},{9,8},{10,11... | collective-permute-start | bytes 1572872 | tf_op jit(solution)/shard_map/ppermute | solution.py:19
  178.1 24.9 %collective-permute-start.44 = (bf16[1024,256]{1,0:T(8,128)(2,1)S(1)}, bf16[1024,256]{1,0:T(8,128)(2,1)S(1)}, u32[]{:S(2)}, u32[]{:S(2)}) collective-permute-start(bf16[1024,256]{1,0:T(8,128)(2,1)S(1)} %get-tuple-element.77), channel_id=1, source_target_pairs={{0,2},{1,3},{2,0},{3,1},{4,6},{5,7},{6,4},{7,5},{8,10},{9,11},{10,... | collective-permute-start | bytes 1572872 | tf_op jit(solution)/shard_map/ppermute | solution.py:19
  (43 other events, 350.2 us)

commit v3 on v2

v3 whole, which is shorter than its diff:
```python
import functools
import math

import jax
import jax.numpy as jnp
from jax import lax
from jax.experimental import pallas as pl
from jax.experimental.pallas import tpu as pltpu
from jax.sharding import PartitionSpec as P

PLANE = ("dp", "context")
BF16 = jnp.bfloat16
F32 = jnp.float32
TENSOR_ORDER = (0, 2, 1, 3)


def swapped(x, axes, bit, name):
    size = lax.axis_size(axes)
    with jax.named_scope(name):
        return lax.ppermute(x, axes, [(i, i ^ bit) for i in range(size)])


def neighbours(to_left, to_right):
    size = lax.axis_size("context")
    up = [(i, i + 1) for i in range(size - 1)]
    down = [(i + 1, i) for i in range(size - 1)]
    return [lax.ppermute(to_right, "context", up), lax.ppermute(to_left, "context", down)]


def contract(x, y, dims):
    return lax.dot_general(x, y, (dims, ((), ())), preferred_element_type=F32)


VMEM = pl.BlockSpec(memory_space=pltpu.VMEM)
ANY = pl.BlockSpec(memory_space=pl.ANY)
FLOPS = 4 * 10**10
SMALL = pl.CostEstimate(flops=0, bytes_accessed=0, transcendentals=0)


def cut_kernel(ranks_ref, x_ref, key_ref, value_ref, *refs, parts, pair, width, carrier):
    out_refs, sems = refs[:-1], refs[-1]
    moves = []
    for i, k in enumerate(parts):
        for half in range(2):
            owner = lax.bitwise_xor(ranks_ref[0], k ^ (half * pair))
            start = pl.multiple_of(owner * width, width)
            moves.append(
                (x_ref.at[:, pl.ds(start, width)], out_refs[i].at[:, half * width : (half + 1) * width])
            )
    if carrier is not None:
        rows, start = x_ref.shape[0], 2 * width
        for half in range(2):
            at = pl.ds(pl.multiple_of((2 * ranks_ref[2] + half) * rows, rows), rows)
            for ref in (key_ref, value_ref):
                end = start + ref.shape[1]
                moves.append((ref.at[at, :], out_refs[carrier].at[:, start:end]))
                start = end
    copies = [pltpu.make_async_copy(x, y, sems.at[i]) for i, (x, y) in enumerate(moves)]
    for copy in copies:
        copy.start()
    for copy in copies:
        copy.wait()


def cut(ranks, x, keys, values, parts, pair, width, carrier):
    rows = x.shape[0]
    extra = 2 * (keys.shape[1] + values.shape[1])
    return pl.pallas_call(
        functools.partial(cut_kernel, parts=parts, pair=pair, width=width, carrier=carrier),
        out_shape=[
            jax.ShapeDtypeStruct((rows, 2 * width + (extra if i == carrier else 0)), x.dtype)
            for i in range(len(parts))
        ],
        in_specs=[pl.BlockSpec(memory_space=pltpu.SMEM)] + [ANY] * 3,
        out_specs=[VMEM] * len(parts),
        scratch_shapes=[pltpu.SemaphoreType.DMA((2 * len(parts) + 4,))],
        compiler_params=pltpu.CompilerParams(vmem_limit_bytes=60 * 2**20),
        cost_estimate=SMALL,
        name="cut",
    )(ranks, x, keys, values)


def project_kernel(*refs, tokens, pieces, carrier):
    token_refs, refs = refs[:tokens], refs[tokens:]
    own_refs, pair_refs, refs = refs[:pieces], refs[pieces : 2 * pieces], refs[2 * pieces :]
    out_refs, held = refs[:tokens], refs[-1]
    rows = token_refs[0].shape[0]
    width, cols = own_refs[0].shape
    for i, ref in enumerate(token_refs):
        held[i * rows : (i + 1) * rows, :] = ref[:, : 2 * width]
    if carrier is not None:
        before_ref = refs[tokens]
        depth = before_ref.shape[1]
        for half in range(2):
            start = 2 * width + half * depth
            before_ref[half * rows : (half + 1) * rows, :] = token_refs[carrier][
                :, start : start + depth
            ]
    for j in range(pieces):
        total = contract(held[:, :width], own_refs[j][...], ((1,), (0,)))
        total = total + contract(held[:, width:], pair_refs[j][...], ((1,), (0,)))
        for i, ref in enumerate(out_refs):
            ref[:, j * cols : (j + 1) * cols] = total[i * rows : (i + 1) * rows].astype(ref.dtype)


def project(tokens, own, pair, carrier):
    rows = tokens[0].shape[0]
    width, cols = own[0].shape
    out_shape = [
        jax.ShapeDtypeStruct((rows, len(own) * cols), BF16 if i else F32)
        for i in range(len(tokens))
    ]
    if carrier is not None:
        extra = (tokens[carrier].shape[1] - 2 * width) // 2
        out_shape.append(jax.ShapeDtypeStruct((2 * rows, extra), BF16))
    return pl.pallas_call(
        functools.partial(
            project_kernel, tokens=len(tokens), pieces=len(own), carrier=carrier
        ),
        out_shape=out_shape,
        in_specs=[VMEM] * (len(tokens) + 2 * len(own)),
        out_specs=[VMEM] * len(out_shape),
        scratch_shapes=[pltpu.VMEM((rows * len(tokens), 2 * width), BF16)],
        compiler_params=pltpu.CompilerParams(vmem_limit_bytes=60 * 2**20),
        cost_estimate=SMALL,
        name="project",
    )(*tokens, *own, *pair)


def hand_on_kernel(*refs):
    pass


def hand_on(arrays, behind, flops=0):
    return pl.pallas_call(
        hand_on_kernel,
        out_shape=[jax.ShapeDtypeStruct(x.shape, x.dtype) for x in arrays],
        in_specs=[ANY] * (len(arrays) + len(behind)),
        out_specs=[ANY] * len(arrays),
        input_output_aliases={i: i for i in range(len(arrays))},
        compiler_params=pltpu.CompilerParams(vmem_limit_bytes=16 * 2**20),
        cost_estimate=pl.CostEstimate(flops=flops, bytes_accessed=0, transcendentals=0),
        name="hand_on",
    )(*arrays, *behind)


def add_kernel(ranks_ref, own_ref, att_ref, *refs, parts):
    part_refs, out_refs = refs[:parts], refs[parts:]
    rows, cols = out_refs[0].shape
    total = own_ref[...]
    for ref in part_refs:
        total = total + ref[...].astype(F32)
    for j, (distance, ref) in enumerate(zip(TENSOR_ORDER, out_refs)):
        ref[:rows, :] = total[:, j * cols : (j + 1) * cols].astype(BF16)
        if distance:
            owner = lax.bitwise_xor(ranks_ref[1], distance)
            ref[rows:, :] = att_ref[pl.ds(pl.multiple_of(owner * rows, rows), rows), :]


def add_up(ranks, own, attended, parts):
    rows, cols = own.shape[0], attended.shape[1]
    return pl.pallas_call(
        functools.partial(add_kernel, parts=len(parts)),
        out_shape=[
            jax.ShapeDtypeStruct((2 * rows if j else rows, cols), BF16) for j in TENSOR_ORDER
        ],
        in_specs=[pl.BlockSpec(memory_space=pltpu.SMEM)] + [VMEM] * (2 + len(parts)),
        out_specs=[VMEM] * len(TENSOR_ORDER),
        compiler_params=pltpu.CompilerParams(vmem_limit_bytes=60 * 2**20),
        cost_estimate=SMALL,
        name="add_up",
    )(ranks, own, attended, *parts)


def join_kernel(ranks_ref, kv_ref, *refs, backs):
    back_refs, (away_ref, next_ref, own_ref), held = refs[:backs], refs[-5:-2], refs[-1]
    rows = own_ref.shape[0]
    span = kv_ref.shape[0] // 2
    held[...] = kv_ref[...]
    if backs == 1:
        at = pl.ds(pl.multiple_of(ranks_ref[2] * span, span), span)
        held[at, :] = held[at, :] + back_refs[0][...].astype(F32)
    else:
        held[span:, :] = held[span:, :] + back_refs[0][...].astype(F32)
        held[:span, :] = held[:span, :] + back_refs[1][...].astype(F32)

    def rank_rows(j):
        at = pl.ds(pl.multiple_of(lax.bitwise_xor(ranks_ref[1], j) * rows, rows), rows)
        return held[at, :]

    away_ref[:rows, :] = rank_rows(2).astype(BF16)
    away_ref[rows:, :] = rank_rows(3).astype(BF16)
    next_ref[...] = rank_rows(1)
    own_ref[...] = rank_rows(0)


def join(ranks, kv, back, behind, later):
    rows, width = kv.shape[0] // len(TENSOR_ORDER), kv.shape[1]
    return pl.pallas_call(
        functools.partial(join_kernel, backs=len(back)),
        out_shape=[
            jax.ShapeDtypeStruct((2 * rows, width), BF16),
            jax.ShapeDtypeStruct((rows, width), F32),
            jax.ShapeDtypeStruct((rows, width), F32),
            jax.ShapeDtypeStruct(later.shape, later.dtype),
        ],
        in_specs=[pl.BlockSpec(memory_space=pltpu.SMEM)]
        + [VMEM] * (1 + len(back))
        + [ANY] * (len(behind) + 1),
        out_specs=[VMEM] * 3 + [ANY],
        input_output_aliases={2 + len(back) + len(behind): 3},
        scratch_shapes=[pltpu.VMEM(kv.shape, F32)],
        compiler_params=pltpu.CompilerParams(vmem_limit_bytes=16 * 2**20),
        cost_estimate=SMALL,
        name="join",
    )(ranks, kv, *back, *behind, later)


def inner_kernel(rest_ref, got_ref, next_ref, *refs, pieces):
    query_refs, out_ref = refs[:pieces], refs[-2]
    rows, cols = query_refs[0].shape
    for i, ref in enumerate(query_refs):
        out_ref[:, i * cols : (i + 1) * cols] = ref[...]
    kv = rest_ref[...] + got_ref[:rows, :].astype(F32) + next_ref[...].astype(F32)
    out_ref[:, pieces * cols :] = kv.astype(BF16)


def inner_grads(rest, got, from_next, queries, later, behind):
    rows, cols = queries[0].shape
    return pl.pallas_call(
        functools.partial(inner_kernel, pieces=len(queries)),
        out_shape=[
            jax.ShapeDtypeStruct((rows, cols * len(queries) + rest.shape[1]), BF16),
            jax.ShapeDtypeStruct(later.shape, later.dtype),
        ],
        in_specs=[VMEM] * (3 + len(queries)) + [ANY] * (1 + len(behind)),
        out_specs=[VMEM, ANY],
        input_output_aliases={3 + len(queries): 1},
        compiler_params=pltpu.CompilerParams(vmem_limit_bytes=16 * 2**20),
        cost_estimate=SMALL,
        name="inner",
    )(rest, got, from_next, *queries, later, *behind)


def outer_kernel(*refs, tokens, atts, weights):
    held, att_held = refs[-2:]
    *own_refs, pair_ref, whole_ref = refs[-4 - len(TENSOR_ORDER) : -2]
    width, cols = own_refs[0].shape
    weight_refs = refs[tokens + atts : tokens + atts + weights]
    for block_refs, whole in (
        (refs[:tokens], held), (refs[tokens : tokens + atts], att_held), (weight_refs, whole_ref),
    ):
        start, columns = 0, whole.shape[1]
        for ref in block_refs:
            whole[start : start + ref.shape[0], :] = ref[:, :columns]
            start += ref.shape[0]
    step = min(width, 256)
    for e in range(0, width, step):
        at = slice(e, e + step)
        total = contract(held[:, at], att_held[...], ((0,), (0,)))
        for j, ref in enumerate(own_refs):
            ref[at, :] = total[:, j * cols : (j + 1) * cols]
        pair_at = slice(width + e, width + e + step)
        pair_ref[at, :] = contract(held[:, pair_at], att_held[...], ((0,), (0,))).astype(BF16)


def outer(tokens, atts, weights, behind):
    width, columns = weights[0].shape[1], atts[0].shape[1]
    depth, cols = tokens[0].shape[0] * len(tokens), columns // len(TENSOR_ORDER)
    return pl.pallas_call(
        functools.partial(
            outer_kernel, tokens=len(tokens), atts=len(atts), weights=len(weights)
        ),
        out_shape=[jax.ShapeDtypeStruct((width, cols), F32)] * len(TENSOR_ORDER)
        + [
            jax.ShapeDtypeStruct((width, columns), BF16),
            jax.ShapeDtypeStruct((sum(w.shape[0] for w in weights), width), BF16),
        ],
        in_specs=[VMEM] * (len(tokens) + len(atts) + len(weights)) + [ANY] * len(behind),
        out_specs=[VMEM] * (len(TENSOR_ORDER) + 2),
        scratch_shapes=[pltpu.VMEM((depth, 2 * width), BF16), pltpu.VMEM((depth, columns), BF16)],
        compiler_params=pltpu.CompilerParams(vmem_limit_bytes=40 * 2**20),
        cost_estimate=SMALL,
        name="outer",
    )(*tokens, *atts, *weights, *behind)


def add_pair_kernel(*refs, addends):
    own_ref, pair_ref, out_ref = refs[0], refs[1], refs[-1]
    total = own_ref[...] + pair_ref[...].astype(F32)
    for ref in refs[2:addends]:
        total = total + ref[...].astype(F32)
    out_ref[...] = total.astype(out_ref.dtype)


def add_pair(own, pair, block, others, dtype, behind):
    columns = pl.BlockSpec(own.shape, lambda i: (0, block))
    whole = pl.BlockSpec(own.shape, lambda i: (0, 0))
    return pl.pallas_call(
        functools.partial(add_pair_kernel, addends=2 + len(others)),
        grid=(1,),
        out_shape=jax.ShapeDtypeStruct(own.shape, dtype),
        in_specs=[whole, columns] + [whole] * len(others) + [ANY] * len(behind),
        out_specs=whole,
        compiler_params=pltpu.CompilerParams(vmem_limit_bytes=16 * 2**20),
        cost_estimate=SMALL,
        name="add_pair",
    )(own, pair, *others, *behind)


def feed_kernel(ranks_ref, *refs, tokens, pieces, distance):
    inner_refs, refs = refs[:tokens], refs[tokens:]
    weights, refs = [refs[i * pieces : (i + 1) * pieces] for i in range(2)], refs[2 * pieces :]
    out_refs, (held, last, sems) = refs[-3 - tokens : -3], refs[-3:]
    rows, columns = inner_refs[0].shape
    width = last.shape[1] // 2
    depth = refs[0].shape[0]
    copies = []
    for half in range(2):
        owner = lax.bitwise_xor(ranks_ref[0], half * distance)
        at = pl.ds(pl.multiple_of(owner * width, width), width)
        for i, ref in enumerate(refs[:2]):
            copies.append(
                pltpu.make_async_copy(
                    ref.at[:, at],
                    last.at[i * depth : (i + 1) * depth, half * width : (half + 1) * width],
                    sems.at[2 * half + i],
                )
            )
    for copy in copies:
        copy.start()
    for i, ref in enumerate(inner_refs):
        held[i * rows : (i + 1) * rows, :] = ref[...]
    for copy in copies:
        copy.wait()
    step = min(width, 512)
    for half in range(2):
        for start in range(0, width, step):
            at = slice(half * width + start, half * width + start + step)
            total = contract(held[:, columns - 2 * depth :], last[:, at], ((1,), (0,)))
            done = 0
            for w in weights[half]:
                part = held[:, done : done + w.shape[0]]
                total = total + contract(part, w[:, start : start + step], ((1,), (0,)))
                done += w.shape[0]
            for i, ref in enumerate(out_refs):
                ref[:, at] = total[i * rows : (i + 1) * rows].astype(BF16)


def feed(ranks, inners, own, pair, w_key, w_value, distance, behind):
    rows, columns = inners[0].shape
    width = own[0].shape[1]
    return pl.pallas_call(
        functools.partial(feed_kernel, tokens=len(inners), pieces=len(own), distance=distance),
        out_shape=[jax.ShapeDtypeStruct((rows, 2 * width), BF16)] * len(inners),
        in_specs=[pl.BlockSpec(memory_space=pltpu.SMEM)]
        + [VMEM] * (len(inners) + 2 * len(own))
        + [ANY] * (2 + len(behind)),
        out_specs=[VMEM] * len(inners),
        scratch_shapes=[
            pltpu.VMEM((rows * len(inners), columns), BF16),
            pltpu.VMEM((2 * w_key.shape[0], 2 * width), BF16),
            pltpu.SemaphoreType.DMA((4,)),
        ],
        compiler_params=pltpu.CompilerParams(vmem_limit_bytes=60 * 2**20),
        cost_estimate=SMALL,
        name="feed",
    )(ranks, *inners, *own, *pair, w_key, w_value, *behind)


def attention_kernel(
    ranks_ref, seg_query_ref, seg_key_ref, query_ref, attended_ref, key_ref, value_ref, log_ref,
    *refs, peers, befores, cycle_size,
):
    dout_refs, before_refs = refs[:peers], refs[peers : peers + befores]
    dquery_refs, away_refs = refs[-4 - befores - peers : -4 - befores], refs[-4 - befores : -4]
    kv_grads_ref, att_own_ref, dout_held, dquery_held = refs[-4:]
    rank, last_rank = ranks_ref[1], ranks_ref[2] == cycle_size - 1
    head_dim = key_ref.shape[1]
    span = query_ref.shape[0] // 2
    heads = query_ref.shape[1] // head_dim
    sub = 2 * span // peers
    inv_root = 1.0 / math.sqrt(head_dim)

    def place(a):
        return pl.ds(pl.multiple_of(a * sub, sub), sub)

    def by_head(x):
        return jnp.concatenate(
            [x[:, h * head_dim : (h + 1) * head_dim] for h in range(heads)], axis=0
        )

    cols = query_ref.shape[1]
    for i, (j, ref) in enumerate(zip(TENSOR_ORDER, dout_refs)):
        dout_held[place(lax.bitwise_xor(rank, j)), :] = ref[:sub, :]
        att_own_ref[:, i * cols : (i + 1) * cols] = ref[sub:, :] if j else attended_ref[place(rank), :]
    before = []
    for b in range(2):
        rows = slice(b * span, (b + 1) * span)
        query = by_head(query_ref[rows, :])
        dout = by_head(dout_held[rows, :])
        attended = by_head(attended_ref[rows, :])
        key_before = before_refs[b % befores][:, :head_dim]
        value_before = before_refs[b % befores][:, head_dim:]
        if b == 1:
            key_before = jnp.where(last_rank, key_ref[:span, :], key_before)
            value_before = jnp.where(last_rank, value_ref[:span, :], value_before)
        key = jnp.concatenate([key_before, key_ref[rows, :]], axis=0)
        value = jnp.concatenate([value_before, value_ref[rows, :]], axis=0)
        log_rows = jnp.concatenate([log_ref[rows, h : h + 1] for h in range(heads)], axis=0)
        query_at = lax.broadcasted_iota(jnp.int32, (span, 2 * span), 0)
        key_at = lax.broadcasted_iota(jnp.int32, (span, 2 * span), 1) - span
        allowed = (key_at <= query_at) & (seg_query_ref[rows, :] == seg_key_ref[b : b + 1, :])
        allowed = jnp.concatenate([allowed] * heads, axis=0)
        scores = contract(query, key, ((1,), (1,))) * inv_root
        prob = jnp.where(allowed, jnp.exp(scores - log_rows), 0.0)
        delta = jnp.sum(dout.astype(F32) * attended.astype(F32), axis=1, keepdims=True)
        dprob = contract(dout, value, ((1,), (1,)))
        dscore = (prob * (dprob - delta)).astype(BF16)
        dquery = (contract(dscore, key, ((1,), (0,))) * inv_root).astype(BF16)
        for h in range(heads):
            dquery_held[rows, h * head_dim : (h + 1) * head_dim] = dquery[
                h * span : (h + 1) * span
            ]
        key_grads = contract(dscore, query, ((0,), (0,))) * inv_root
        value_grads = contract(prob.astype(BF16), dout, ((0,), (0,)))
        kv_grads_ref[rows, :head_dim] = key_grads[span:]
        kv_grads_ref[rows, head_dim:] = value_grads[span:]
        before.append((key_grads[:span], value_grads[:span]))
    for i, half in enumerate((slice(0, head_dim), slice(head_dim, 2 * head_dim))):
        low, high = before[0][i], before[1][i]
        kv_grads_ref[:span, half] = kv_grads_ref[:span, half] + jnp.where(last_rank, high, 0.0)
        if befores == 1:
            away_refs[0][:, half] = jnp.where(last_rank, low, high).astype(BF16)
        else:
            away_refs[0][:, half] = low.astype(BF16)
            away_refs[1][:, half] = jnp.where(last_rank, 0.0, high).astype(BF16)
    for j, ref in zip(TENSOR_ORDER, dquery_refs):
        ref[...] = dquery_held[place(lax.bitwise_xor(rank, j)), :]


def attention(
    ranks, seg_query, seg_key, queries, attended, keys, values, log_sums, dout, before, behind,
    cycle_size,
):
    kv_shape = (keys.shape[0], 2 * keys.shape[1])
    return pl.pallas_call(
        functools.partial(
            attention_kernel, peers=len(dout), befores=len(before), cycle_size=cycle_size
        ),
        out_shape=[jax.ShapeDtypeStruct(dout[0].shape, BF16) for _ in dout]
        + [jax.ShapeDtypeStruct(x.shape, BF16) for x in before]
        + [
            jax.ShapeDtypeStruct(kv_shape, F32),
            jax.ShapeDtypeStruct((dout[0].shape[0], len(dout) * dout[0].shape[1]), BF16),
        ],
        in_specs=[pl.BlockSpec(memory_space=pltpu.SMEM)]
        + [VMEM] * (7 + len(dout) + len(before))
        + [ANY] * len(behind),
        out_specs=[VMEM] * (len(dout) + len(before) + 2),
        scratch_shapes=[pltpu.VMEM(queries.shape, BF16)] * 2,
        compiler_params=pltpu.CompilerParams(vmem_limit_bytes=32 * 2**20),
        cost_estimate=SMALL,
        name="attention",
    )(ranks, seg_query, seg_key, queries, attended, keys, values, log_sums, *dout, *before, *behind)


def on_device(
    grad_out, queries, attended, keys, values, log_sums, segment_ids, w_out, w_query, w_key, w_value
):
    tensor_rank = lax.axis_index("tensor")
    plane_rank = lax.axis_index(PLANE)
    cycle_size, cycle_pos = lax.axis_size("context"), lax.axis_index("context")
    own_rows, features = grad_out.shape
    width = w_out.shape[0]
    cols = queries.shape[1]
    span = queries.shape[0] // 2
    pair = cycle_size
    bits = [1 << i for i in range(lax.axis_size(PLANE).bit_length() - 1)]
    bits = [bit for bit in reversed(bits) if bit != pair]
    meets = [0]
    for bit in bits:
        meets += [k ^ bit for k in meets]
    meets = meets[1:]

    def plane_gather(x, name):
        return [x] + [swapped(x, PLANE, k, f"{name}_{k}") for k in meets]

    def along(x, j, name):
        return swapped(x, "tensor", j, f"{name}_{j}")

    def across(x, name):
        return swapped(x, PLANE, pair, name)

    out_2, out_1 = along(w_out, 2, "w_out"), along(w_out, 1, "w_out")

    ranks = jnp.stack([plane_rank, tensor_rank, cycle_pos])
    carrier = meets.index(1) + 1 if cycle_size == 2 else None
    tokens = cut(ranks, grad_out, keys, values, [0] + meets, pair, width, carrier)
    tokens = [tokens[0]] + [swapped(x, PLANE, k, f"tokens_{k}") for k, x in zip(meets, tokens[1:])]
    out_2 = hand_on([out_2], [], FLOPS // 10)[0]
    out_2 = hand_on([out_2], tokens[1:2])[0]
    out_1 = hand_on([out_1], tokens[2:], FLOPS)[0]
    w_out_own = [w_out, out_2, out_1, along(out_2, 1, "w_out_on")]
    w_out_pair = [across(w, f"w_out_pair_{i}") for i, w in enumerate(w_out_own)]

    query_2, query_1 = along(w_query, 2, "w_query"), along(w_query, 1, "w_query")

    seg_row = segment_ids[0]
    high_span = 2 * cycle_size - 1 - cycle_pos

    def seg_slice(at):
        return lax.dynamic_slice_in_dim(seg_row, jnp.maximum(at, 0) * span, span)

    seg_low, seg_high = seg_slice(cycle_pos), seg_slice(high_span)
    seg_before = jnp.where(cycle_pos == 0, -1, seg_slice(cycle_pos - 1))
    seg_query = jnp.concatenate([seg_low, seg_high])[:, None]
    seg_key = jnp.stack(
        [
            jnp.concatenate([seg_before, seg_low]),
            jnp.concatenate([seg_slice(high_span - 1), seg_high]),
        ]
    )
    log_rows = log_sums.T

    partial_attn = project(tokens, w_out_own, w_out_pair, carrier)
    partial_attn, before = partial_attn[: len(tokens)], partial_attn[len(tokens) :]
    if cycle_size != 2:
        kv_pair = jnp.concatenate([keys, values], axis=1)
        before = neighbours(kv_pair[span:], kv_pair[:span])
    parts = [swapped(x, PLANE, k, f"attn_{k}") for k, x in zip(meets, partial_attn[1:])]
    dout = add_up(ranks, partial_attn[0], attended, parts)
    dout = [dout[0]] + [along(x, j, "dout") for x, j in zip(dout[1:], TENSOR_ORDER[1:])]
    *dquery, kv_grads, att_own = attention(
        ranks, seg_query, seg_key, queries, attended, keys, values, log_rows, dout, before,
        [query_2, query_1], cycle_size,
    )
    dquery, away = dquery[:4], dquery[4:]

    dquery = dquery[:1] + [along(x, j, "dquery") for x, j in zip(dquery[1:], TENSOR_ORDER[1:])]
    back = [swapped(away[0], "context", 1, "kv_back")] if cycle_size == 2 else neighbours(*away)
    kv_away, kv_next, kv_rest, att_own = join(ranks, kv_grads, back, dquery[1:], att_own)
    att_met = plane_gather(att_own, "attended")
    att_met[1:] = hand_on(att_met[1:], [], FLOPS // 10)
    got = along(kv_away, 2, "kv")
    kv_next = along((kv_next + got[own_rows:].astype(F32)).astype(BF16), 1, "kv")
    inner, query_2 = inner_grads(
        kv_rest, got, kv_next, dquery, query_2, []
    )
    inner_met = plane_gather(inner, "inner")

    *out_own, out_pair, w_query_own = outer(
        tokens, att_met, [w_query, query_2, query_1], [inner]
    )
    query_3 = along(query_2, 1, "w_query_on")

    out_pair = across(out_pair, "out_proj_pair")
    to_3 = add_pair(out_own[3], out_pair, 3, [], BF16, [])
    from_3 = along(to_3, 1, "out_proj_3")
    *inner_met[1:], query_3 = hand_on([*inner_met[1:], query_3], [], FLOPS)
    *inner_met[1:], query_3 = hand_on([*inner_met[1:], query_3], [out_pair])
    w_query_own = [w_query_own, query_3]
    w_query_pair = [across(w, f"w_query_pair_{i}") for i, w in enumerate(w_query_own)]

    blocks = feed(
        ranks, inner_met, w_query_own, w_query_pair, w_key, w_value, pair, [to_3]
    )
    to_1 = add_pair(out_own[2], out_pair, 2, [], BF16, [to_3])
    to_2 = add_pair(out_own[1], out_pair, 1, [from_3], BF16, [blocks[1]])
    out_proj_grad = add_pair(
        out_own[0], out_pair, 0, [along(to_1, 1, "out_proj"), along(to_2, 2, "out_proj")], F32, []
    )
    blocks = [(0, blocks[0])] + [(k, swapped(x, PLANE, k, f"grads_{k}")) for k, x in zip(meets, blocks[1:])]
    received = hand_on([x for _, x in blocks[1:]], [], FLOPS)
    blocks = blocks[:1] + list(zip(meets, received))
    grad_input = jnp.zeros((own_rows, features), BF16)
    for k, block in blocks:
        for i, owner in enumerate((plane_rank ^ k, plane_rank ^ k ^ pair)):
            grad_input = lax.dynamic_update_slice_in_dim(
                grad_input, block[:, i * width : (i + 1) * width], owner * width, axis=1
            )
    return (grad_input, out_proj_grad)


def solution(mesh):
    placed = (
        P(("dp", "context", "tensor"), None),
        P(("dp", "context"), "tensor"),
        P(("dp", "context"), "tensor"),
        P(("dp", "context"), None),
        P(("dp", "context"), None),
        P("tensor", ("dp", "context")),
        P("dp", None),
        P(("dp", "context"), "tensor"),
        P("tensor", ("dp", "context")),
        P(),
        P(),
    )
    return jax.shard_map(
        on_device,
        mesh=mesh,
        in_specs=placed,
        out_specs=(P(("dp", "context", "tensor"), None), P(("dp", "context"), "tensor")),
        check_vma=False,
    )
```

time: 206 us -> 176 us (0.85)
  waiting for transfers between devices: 106 us -> 87.1 us
  other arithmetic: 9.43 us -> 0.63 us
  local copies, waits for them, and re-layouts: 17.4 us -> 13.9 us
  Pallas kernels: 25.8 us -> 29 us
  starting transfers between devices: 46.1 us -> 43.5 us
    ppermute x45 -> x40, waiting for transfers between devices: 106 us -> 87.1 us  [swapped(): return lax.ppermute(x, axes, [(i, i ^ bit) for i in range(size)])]
    unnamed x93, local copies, waits for them, and re-layouts: 15.6 us -> 7.62 us
    dynamic_update_slice x8, local copies, waits for them, and re-layouts: 0.19 us -> 5.98 us  [on_device(): lax.dynamic_update_slice_in_dim(grad_input, block[:, i * width:(i + 1) *...]
    pallas_call x6 -> x17, Pallas kernels: 17.9 us -> 22.4 us  [the longest x1 7.88 us: feed(): pl.pallas_call(functools.partial(feed_kernel, tokens=len(inners), pieces=...]
    convert_element_type x4 -> x1, other arithmetic: 3.81 us -> 0.01 us  [on_device(): (kv_next + got[own_rows:].astype(F32)).astype(BF16)]
    concatenate x3 -> x0, other arithmetic: 2.93 us -> none  [the longest x1 1.85 us: on_device(): atts.append(swapped(jnp.concatenate(atts, axis=0), PLANE, bit))]
    add x1 -> x0, other arithmetic: 2.59 us -> none  [on_device(): out_proj_grad = out_block(0) + from_1.astype(F32) + from_2.astype(F32)]
    ppermute x45 -> x40, starting transfers between devices: 46.1 us -> 43.5 us  [swapped(): return lax.ppermute(x, axes, [(i, i ^ bit) for i in range(size)])]
  transfers between devices with their start and end apart: 45 -> 40, of which waited for: 22 -> 18; matrix products, arithmetic and copies ran while one was open for 4% -> 4% of each run, Pallas kernels for 10% -> 14%
where the time goes in v3:
time: 176 us; the launch traced here: 175 us
  waiting for transfers between devices  87.1 us (49%)
  starting transfers between devices  43.5 us (25%)
  Pallas kernels  29 us (16%)
  local copies, waits for them, and re-layouts  13.9 us (8%)
    ppermute x40, waiting for transfers between devices, swapped(): return lax.ppermute(x, axes, [(i, i ^ bit) for i in range(size)])  87.1 us
    ppermute x40, starting transfers between devices, swapped(): return lax.ppermute(x, axes, [(i, i ^ bit) for i in range(size)])  43.5 us
    pallas_call x1, Pallas kernels, feed(): pl.pallas_call(functools.partial(feed_kernel, tokens=len(inners), pieces=...  7.88 us
    unnamed x93, local copies, waits for them, and re-layouts  7.62 us
    pallas_call x1, Pallas kernels, project(): pl.pallas_call(functools.partial(project_kernel, tokens=len(tokens), piec...  6.18 us
    dynamic_update_slice x8, local copies, waits for them, and re-layouts, on_device(): lax.dynamic_update_slice_in_dim(grad_input, block[:, i * width:(i + 1) *...  5.98 us
    pallas_call x1, Pallas kernels, cut(): pl.pallas_call(functools.partial(cut_kernel, parts=parts, pair=pair, widt...  3.65 us
    pallas_call x1, Pallas kernels, outer(): pl.pallas_call(functools.partial(outer_kernel, tokens=len(tokens), atts=l...  3.52 us
  transfers between devices with their start and end apart: 40, of which 18 were waited for; matrix products, arithmetic and copies ran while one was open for 4% of the time, Pallas kernels for 14%

profile of v3, /device:TPU:0, one launch (start us, length us, event | category | flops | bytes accessed | tf_op | source)
XLA Modules:
  0.0 175.5 jit_solution(8832950449778917078)
XLA Ops:
  0.6 4.1 %collective-permute-start.3 = (bf16[1024,256]{1,0:T(8,128)(2,1)}, bf16[1024,256]{1,0:T(8,128)(2,1)S(1)}, u32[]{:S(2)}, u32[]{:S(2)}) collective-permute-start(bf16[1024,256]{1,0:T(8,128)(2,1)} %refs_4_.1), channel_id=1, source_target_pairs={{0,2},{1,3},{2,0},{3,1},{4,6},{5,7},{6,4},{7,5},{8,10},{9,11},{10,... | collective-permute-start | bytes 1572872 | tf_op jit(solution)/shard_map/w_out_2/ppermute | solution.py:20
  5.3 3.6 %cut.1 = (bf16[128,2048]{1,0:T(8,128)(2,1)}, bf16[128,2048]{1,0:T(8,128)(2,1)}, bf16[128,2560]{1,0:T(8,128)(2,1)}, bf16[128,2048]{1,0:T(8,128)(2,1)}) custom-call(s32[3]{0:T(128)} %pad_add_fusion.4.ranks_ref, bf16[128,8192]{1,0:T(8,128)(2,1)} %x_ref.1, bf16[512,128]{1,0:T(8,128)(2,1)} %key_ref.3, bf16[512,128]{1,0:T(8,128)(2,1)} %value_ref.3), custom_call_target="tpu_custom_call" | custom-call | tf_op jit(solution)/shard_map/cut/pallas_call | solution.py:68
  9.0 1.6 collective-permute-start.1
  10.6 1.5 collective-permute-start
  12.5 1.6 collective-permute-start.4
  14.1 14.1 %collective-permute-done.3.refs_0_ = bf16[1024,256]{1,0:T(8,128)(2,1)S(1)} collective-permute-done((bf16[1024,256]{1,0:T(8,128)(2,1)}, bf16[1024,256]{1,0:T(8,128)(2,1)S(1)}, u32[]{:S(2)}, u32[]{:S(2)}) %collective-permute-start.3) | collective-permute-done | bytes 524320 | tf_op jit(solution)/shard_map/w_out_2/ppermute | solution.py:20
  29.1 6.1 %collective-permute-done.2.refs_2_.refs_3_ = bf16[128,2048]{1,0:T(8,128)(2,1)S(1)} collective-permute-done((bf16[128,2048]{1,0:T(8,128)(2,1)}, bf16[128,2048]{1,0:T(8,128)(2,1)S(1)}, u32[]{:S(2)}, u32[]{:S(2)}) %collective-permute-start.2) | collective-permute-done | bytes 524320 | tf_op jit(solution)/shard_map/tokens_5/ppermute | solution.py:20
  35.2 2.3 %collective-permute-done.4.refs_0_ = bf16[1024,256]{1,0:T(8,128)(2,1)S(1)} collective-permute-done((bf16[1024,256]{1,0:T(8,128)(2,1)S(1)}, bf16[1024,256]{1,0:T(8,128)(2,1)S(1)}, u32[]{:S(2)}, u32[]{:S(2)}) %collective-permute-start.4) | collective-permute-done | bytes 524320 | tf_op jit(solution)/shard_map/w_out_1/ppermute | solution.py:20
  38.3 8.1 %collective-permute-done.5.refs_7_ = bf16[1024,256]{1,0:T(8,128)(2,1)S(1)} collective-permute-done((bf16[1024,256]{1,0:T(8,128)(2,1)S(1)}, bf16[1024,256]{1,0:T(8,128)(2,1)S(1)}, u32[]{:S(2)}, u32[]{:S(2)}) %collective-permute-start.5) | collective-permute-done | bytes 524320 | tf_op jit(solution)/shard_map/w_out_on_1/ppermute | solution.py:20
  46.9 2.5 %collective-permute-start.17 = (bf16[256,1024]{1,0:T(8,128)(2,1)}, bf16[256,1024]{1,0:T(8,128)(2,1)S(1)}, u32[]{:S(2)}, u32[]{:S(2)}) collective-permute-start(bf16[256,1024]{1,0:T(8,128)(2,1)} %refs_8_.2), channel_id=1, source_target_pairs={{0,1},{1,0},{2,3},{3,2},{4,5},{5,4},{6,7},{7,6},{8,9},{9,8},{10,11... | collective-permute-start | bytes 1572872 | tf_op jit(solution)/shard_map/w_query_1/ppermute | solution.py:20
  51.2 6.2 %project.1 = (f32[128,1024]{1,0:T(8,128)}, bf16[128,1024]{1,0:T(8,128)(2,1)}, bf16[128,1024]{1,0:T(8,128)(2,1)}, bf16[128,1024]{1,0:T(8,128)(2,1)}, bf16[256,256]{1,0:T(8,128)(2,1)}) custom-call(bf16[128,2048]{1,0:T(8,128)(2,1)} %get-tuple-element.52.refs_0_, bf16[128,2048]{1,0:T(8,128)(2,1)} %copy-done, bf16[128,2560]{1,0:T(8,128)(2,1)} %copy-done.4, ...), custom_call_target="tpu_custom_call" | custom-call | tf_op jit(solution)/shard_map/project/pallas_call | solution.py:116
  57.4 1.6 collective-permute-start.10
  59.0 1.5 collective-permute-start.11
  61.0 5.9 %collective-permute-done.10.refs_0_ = bf16[128,1024]{1,0:T(8,128)(2,1)S(1)} collective-permute-done((bf16[128,1024]{1,0:T(8,128)(2,1)}, bf16[128,1024]{1,0:T(8,128)(2,1)S(1)}, u32[]{:S(2)}, u32[]{:S(2)}) %collective-permute-start.10) | collective-permute-done | bytes 262176 | tf_op jit(solution)/shard_map/attn_4/ppermute | solution.py:20
  66.9 5.8 %collective-permute-done.11.refs_1_ = bf16[128,1024]{1,0:T(8,128)(2,1)S(1)} collective-permute-done((bf16[128,1024]{1,0:T(8,128)(2,1)}, bf16[128,1024]{1,0:T(8,128)(2,1)S(1)}, u32[]{:S(2)}, u32[]{:S(2)}) %collective-permute-start.11) | collective-permute-done | bytes 262176 | tf_op jit(solution)/shard_map/attn_1/ppermute | solution.py:20
  73.5 2.2 %add_up.1 = (bf16[128,256]{1,0:T(8,128)(2,1)}, bf16[256,256]{1,0:T(8,128)(2,1)}, bf16[256,256]{1,0:T(8,128)(2,1)}, bf16[256,256]{1,0:T(8,128)(2,1)}) custom-call(s32[3]{0:T(128)} %pad_add_fusion.4.ranks_ref, f32[128,1024]{1,0:T(8,128)} %get-tuple-element.56.own_ref, bf16[512,256]{1,0:T(8,128)(2,1)} %attended_ref.1, bf16[128,1024]{1,0:T(8,128)(2,1)} %copy-done.41, ...), custom_call_target="tpu_custom_call" | custom-call | tf_op jit(solution)/shard_map/add_up/pallas_call | solution.py:162
  76.1 1.6 collective-permute-start.14
  77.7 2.4 %collective-permute-start.15 = (bf16[256,256]{1,0:T(8,128)(2,1)}, bf16[256,256]{1,0:T(8,128)(2,1)S(1)}, u32[]{:S(2)}, u32[]{:S(2)}) collective-permute-start(bf16[256,256]{1,0:T(8,128)(2,1)} %get-tuple-element.63), channel_id=1, source_target_pairs={{0,3},{1,2},{2,1},{3,0},{4,7},{5,6},{6,5},{7,4},{8,11},{9,10},{10,... | collective-permute-start | bytes 393224 | tf_op jit(solution)/shard_map/dout_3/ppermute | solution.py:20
  80.4 6.9 %collective-permute-done.13.refs_1_ = bf16[256,256]{1,0:T(8,128)(2,1)S(1)} collective-permute-done((bf16[256,256]{1,0:T(8,128)(2,1)}, bf16[256,256]{1,0:T(8,128)(2,1)S(1)}, u32[]{:S(2)}, u32[]{:S(2)}) %collective-permute-start.13) | collective-permute-done | bytes 131104 | tf_op jit(solution)/shard_map/dout_2/ppermute | solution.py:20
  88.2 3.1 %attention.1 = (bf16[128,256]{1,0:T(8,128)(2,1)S(1)}, bf16[128,256]{1,0:T(8,128)(2,1)S(1)}, bf16[128,256]{1,0:T(8,128)(2,1)S(1)}, bf16[128,256]{1,0:T(8,128)(2,1...) custom-call(s32[3]{0:T(128)S(1)} %copy-done.30, ...), custom_call_target="tpu_custom_call" | custom-call | tf_op jit(solution)/shard_map/attention/pallas_call | solution.py:447
  91.3 1.2 collective-permute-start.18
  92.5 1.9 %collective-permute-start.19 = (bf16[128,256]{1,0:T(8,128)(2,1)S(1)}, bf16[128,256]{1,0:T(8,128)(2,1)S(1)}, u32[]{:S(2)}, u32[]{:S(2)}) collective-permute-start(bf16[128,256]{1,0:T(8,128)(2,1)S(1)} %get-tuple-element.67), channel_id=1, source_target_pairs={{0,2},{1,3},{2,0},{3,1},{4,6},{5,7},{6,4},{7,5},{8,10},{9,11},{10,... | collective-permute-start | bytes 196616 | tf_op jit(solution)/shard_map/dquery_2/ppermute | solution.py:20
  94.5 2.4 %collective-permute-start.21 = (bf16[128,256]{1,0:T(8,128)(2,1)S(1)}, bf16[128,256]{1,0:T(8,128)(2,1)S(1)}, u32[]{:S(2)}, u32[]{:S(2)}) collective-permute-start(bf16[128,256]{1,0:T(8,128)(2,1)S(1)} %get-tuple-element.69), channel_id=1, source_target_pairs={{0,3},{1,2},{2,1},{3,0},{4,7},{5,6},{6,5},{7,4},{8,11},{9,10},{10,... | collective-permute-start | bytes 196616 | tf_op jit(solution)/shard_map/dquery_3/ppermute | solution.py:20
  96.9 2.9 %collective-permute-done.19.refs_1_ = bf16[128,256]{1,0:T(8,128)(2,1)S(1)} collective-permute-done((bf16[128,256]{1,0:T(8,128)(2,1)S(1)}, bf16[128,256]{1,0:T(8,128)(2,1)S(1)}, u32[]{:S(2)}, u32[]{:S(2)}) %collective-permute-start.19) | collective-permute-done | bytes 65568 | tf_op jit(solution)/shard_map/dquery_2/ppermute | solution.py:20
  101.3 1.7 collective-permute-start.22
  103.1 1.5 collective-permute-start.28
  104.6 1.5 collective-permute-start.29
  106.6 2.2 %collective-permute-done.22.got_ref = bf16[256,256]{1,0:T(8,128)(2,1)S(1)} collective-permute-done((bf16[256,256]{1,0:T(8,128)(2,1)S(1)}, bf16[256,256]{1,0:T(8,128)(2,1)S(1)}, u32[]{:S(2)}, u32[]{:S(2)}) %collective-permute-start.22) | collective-permute-done | bytes 131104 | tf_op jit(solution)/shard_map/kv_2/ppermute | solution.py:20
  108.9 5.0 %collective-permute-done.23.next_ref = bf16[128,256]{1,0:T(8,128)(2,1)S(1)} collective-permute-done((bf16[128,256]{1,0:T(8,128)(2,1)S(1)}, bf16[128,256]{1,0:T(8,128)(2,1)S(1)}, u32[]{:S(2)}, u32[]{:S(2)}) %collective-permute-start.23) | collective-permute-done | bytes 65568 | tf_op jit(solution)/shard_map/kv_1/ppermute | solution.py:20
  114.0 1.8 %collective-permute-start.24 = (bf16[128,1280]{1,0:T(8,128)(2,1)S(1)}, bf16[128,1280]{1,0:T(8,128)(2,1)S(1)}, u32[]{:S(2)}, u32[]{:S(2)}) collective-permute-start(bf16[128,1280]{1,0:T(8,128)(2,1)S(1)} %get-tuple-element.75.refs_11_.refs_0_), channel_id=1, source_target_pairs={{0,16},{4,20},{8,24},{12,28},{16,0},{20,4},{24,8},{28,12},{1,17},{... | collective-permute-start | bytes 983048 | tf_op jit(solution)/shard_map/inner_4/ppermute | solution.py:20
  116.3 1.3 collective-permute-start.26
  117.6 3.5 %outer.1 = (f32[1024,256]{1,0:T(8,128)S(1)}, f32[1024,256]{1,0:T(8,128)S(1)}, f32[1024,256]{1,0:T(8,128)S(1)}, f32[1024,256]{1,0:T(8,128)S(1)}, bf16[1024,1024]{...) custom-call(bf16[128,2048]{1,0:T(8,128)(2,1)S(1)} %copy-done.6, bf16[128,2048]{1,0:T(8,128)(2,1)S(1)} %copy-done.1, ...), custom_call_target="tpu_custom_call" | custom-call | tf_op jit(solution)/shard_map/outer/pallas_call | solution.py:270
  121.3 3.5 %collective-permute-done.24.refs_0_ = bf16[128,1280]{1,0:T(8,128)(2,1)S(1)} collective-permute-done((bf16[128,1280]{1,0:T(8,128)(2,1)S(1)}, bf16[128,1280]{1,0:T(8,128)(2,1)S(1)}, u32[]{:S(2)}, u32[]{:S(2)}) %collective-permute-start.24) | collective-permute-done | bytes 327712 | tf_op jit(solution)/shard_map/inner_4/ppermute | solution.py:20
  124.7 5.6 %collective-permute-done.25.refs_1_ = bf16[128,1280]{1,0:T(8,128)(2,1)S(1)} collective-permute-done((bf16[128,1280]{1,0:T(8,128)(2,1)S(1)}, bf16[128,1280]{1,0:T(8,128)(2,1)S(1)}, u32[]{:S(2)}, u32[]{:S(2)}) %collective-permute-start.25) | collective-permute-done | bytes 327712 | tf_op jit(solution)/shard_map/inner_1/ppermute | solution.py:20
  130.6 1.2 collective-permute-start.38
  133.3 7.9 %feed.1 = (bf16[128,2048]{1,0:T(8,128)(2,1)}, bf16[128,2048]{1,0:T(8,128)(2,1)}, bf16[128,2048]{1,0:T(8,128)(2,1)}, bf16[128,2048]{1,0:T(8,128)(2,1)}) custom-call(s32[3]{0:T(128)} %pad_add_fusion.4.ranks_ref, bf16[128,1280]{1,0:T(8,128)(2,1)} %copy-done.12, bf16[128,1280]{1,0:T(8,128)(2,1)} %copy-done.13, bf16[128,1280]{1,0:T(8,128)(2,1)} %copy-done.14, ...), custom_call_target="tpu_custom_call" | custom-call | tf_op jit(solution)/shard_map/feed/pallas_call | solution.py:353
  141.2 1.4 collective-permute-start.34
  142.5 1.7 collective-permute-start.35
  144.7 1.0 copy-done.3
  145.7 1.2 copy-done.22
  147.1 1.2 collective-permute-start.37
  148.5 1.9 %collective-permute-start.39 = (bf16[1024,256]{1,0:T(8,128)(2,1)S(1)}, bf16[1024,256]{1,0:T(8,128)(2,1)S(1)}, u32[]{:S(2)}, u32[]{:S(2)}) collective-permute-start(bf16[1024,256]{1,0:T(8,128)(2,1)S(1)} %add_pair.6), channel_id=1, source_target_pairs={{0,2},{1,3},{2,0},{3,1},{4,6},{5,7},{6,4},{7,5},{8,10},{9,11},{10,... | collective-permute-start | bytes 1572872 | tf_op jit(solution)/shard_map/out_proj_2/ppermute | solution.py:20
  150.7 5.6 %collective-permute-done.34.refs_0_ = bf16[128,2048]{1,0:T(8,128)(2,1)} collective-permute-done((bf16[128,2048]{1,0:T(8,128)(2,1)}, bf16[128,2048]{1,0:T(8,128)(2,1)}, u32[]{:S(2)}, u32[]{:S(2)}) %collective-permute-start.34) | collective-permute-done | bytes 524320 | tf_op jit(solution)/shard_map/grads_4/ppermute | solution.py:20
  156.3 10.7 %collective-permute-done.35.refs_1_ = bf16[128,2048]{1,0:T(8,128)(2,1)} collective-permute-done((bf16[128,2048]{1,0:T(8,128)(2,1)}, bf16[128,2048]{1,0:T(8,128)(2,1)}, u32[]{:S(2)}, u32[]{:S(2)}) %collective-permute-start.35) | collective-permute-done | bytes 524320 | tf_op jit(solution)/shard_map/grads_1/ppermute | solution.py:20
  167.8 1.1 slice_dynamic-update-slice_fusion.5
  168.9 1.0 slice_dynamic-update-slice_fusion.4
  169.9 1.0 slice_dynamic-update-slice_fusion.3
  173.9 1.5 add_pair.7
  (159 shorter events, 17.3 us)
Async XLA Ops:
  0.6 27.6 %collective-permute-start.3 = (bf16[1024,256]{1,0:T(8,128)(2,1)}, bf16[1024,256]{1,0:T(8,128)(2,1)S(1)}, u32[]{:S(2)}, u32[]{:S(2)}) collective-permute-start(bf16[1024,256]{1,0:T(8,128)(2,1)} %refs_4_.1), channel_id=1, source_target_pairs={{0,2},{1,3},{2,0},{3,1},{4,6},{5,7},{6,4},{7,5},{8,10},{9,11},{10,... | collective-permute-start | bytes 1572872 | tf_op jit(solution)/shard_map/w_out_2/ppermute | solution.py:20
  9.0 28.5 %collective-permute-start.1 = (bf16[128,2560]{1,0:T(8,128)(2,1)}, bf16[128,2560]{1,0:T(8,128)(2,1)S(1)}, u32[]{:S(2)}, u32[]{:S(2)}) collective-permute-start(bf16[128,2560]{1,0:T(8,128)(2,1)} %get-tuple-element.54), channel_id=1, source_target_pairs={{0,4},{4,0},{8,12},{12,8},{16,20},{20,16},{24,28},{28,24},{1,5},{5... | collective-permute-start | bytes 1966088 | tf_op jit(solution)/shard_map/tokens_1/ppermute | solution.py:20
  10.6 17.6 %collective-permute-start = (bf16[128,2048]{1,0:T(8,128)(2,1)}, bf16[128,2048]{1,0:T(8,128)(2,1)S(1)}, u32[]{:S(2)}, u32[]{:S(2)}) collective-permute-start(bf16[128,2048]{1,0:T(8,128)(2,1)} %get-tuple-element.53), channel_id=1, source_target_pairs={{0,16},{4,20},{8,24},{12,28},{16,0},{20,4},{24,8},{28,12},{1,17},{... | collective-permute-start | bytes 1572872 | tf_op jit(solution)/shard_map/tokens_4/ppermute | solution.py:20
  12.1 23.1 %collective-permute-start.2 = (bf16[128,2048]{1,0:T(8,128)(2,1)}, bf16[128,2048]{1,0:T(8,128)(2,1)S(1)}, u32[]{:S(2)}, u32[]{:S(2)}) collective-permute-start(bf16[128,2048]{1,0:T(8,128)(2,1)} %get-tuple-element.55), channel_id=1, source_target_pairs={{0,20},{4,16},{8,28},{12,24},{16,4},{20,0},{24,12},{28,8},{1,21},{... | collective-permute-start | bytes 1572872 | tf_op jit(solution)/shard_map/tokens_5/ppermute | solution.py:20
  12.5 24.9 %collective-permute-start.4 = (bf16[1024,256]{1,0:T(8,128)(2,1)S(1)}, bf16[1024,256]{1,0:T(8,128)(2,1)S(1)}, u32[]{:S(2)}, u32[]{:S(2)}) collective-permute-start(bf16[1024,256]{1,0:T(8,128)(2,1)S(1)} %copy-done.33), channel_id=1, source_target_pairs={{0,1},{1,0},{2,3},{3,2},{4,5},{5,4},{6,7},{7,6},{8,9},{9,8},{10,11... | collective-permute-start | bytes 1572872 | tf_op jit(solution)/shard_map/w_out_1/ppermute | solution.py:20
  28.2 18.7 %collective-permute-start.6 = (bf16[1024,256]{1,0:T(8,128)(2,1)S(1)}, bf16[1024,256]{1,0:T(8,128)(2,1)S(1)}, u32[]{:S(2)}, u32[]{:S(2)}) collective-permute-start(bf16[1024,256]{1,0:T(8,128)(2,1)S(1)} %copy-done.33), channel_id=1, source_target_pairs={{0,8},{4,12},{8,0},{12,4},{16,24},{20,28},{24,16},{28,20},{1,9},{5... | collective-permute-start | bytes 1572872 | tf_op jit(solution)/shard_map/w_out_pair_0/ppermute | solution.py:20
  28.3 18.1 %collective-permute-start.5 = (bf16[1024,256]{1,0:T(8,128)(2,1)S(1)}, bf16[1024,256]{1,0:T(8,128)(2,1)S(1)}, u32[]{:S(2)}, u32[]{:S(2)}) collective-permute-start(bf16[1024,256]{1,0:T(8,128)(2,1)S(1)} %hand_on.8.refs_5_), channel_id=1, source_target_pairs={{0,1},{1,0},{2,3},{3,2},{4,5},{5,4},{6,7},{7,6},{8,9},{9,8},{10,11... | collective-permute-start | bytes 1572872 | tf_op jit(solution)/shard_map/w_out_on_1/ppermute | solution.py:20
  35.2 14.2 %collective-permute-start.7 = (bf16[1024,256]{1,0:T(8,128)(2,1)S(1)}, bf16[1024,256]{1,0:T(8,128)(2,1)S(1)}, u32[]{:S(2)}, u32[]{:S(2)}) collective-permute-start(bf16[1024,256]{1,0:T(8,128)(2,1)S(1)} %hand_on.8.refs_5_), channel_id=1, source_target_pairs={{0,8},{4,12},{8,0},{12,4},{16,24},{20,28},{24,16},{28,20},{1,9},{5... | collective-permute-start | bytes 1572872 | tf_op jit(solution)/shard_map/w_out_pair_1/ppermute | solution.py:20
  38.3 12.9 %copy-start.24 = (bf16[1024,256]{1,0:T(8,128)(2,1)}, bf16[1024,256]{1,0:T(8,128)(2,1)S(1)}, u32[]{:S(2)}) copy-start(bf16[1024,256]{1,0:T(8,128)(2,1)S(1)} %hand_on.9.refs_6_) | copy-start | bytes 1572868
  38.3 11.1 %collective-permute-start.8 = (bf16[1024,256]{1,0:T(8,128)(2,1)S(1)}, bf16[1024,256]{1,0:T(8,128)(2,1)S(1)}, u32[]{:S(2)}, u32[]{:S(2)}) collective-permute-start(bf16[1024,256]{1,0:T(8,128)(2,1)S(1)} %hand_on.9.refs_6_), channel_id=1, source_target_pairs={{0,8},{4,12},{8,0},{12,4},{16,24},{20,28},{24,16},{28,20},{1,9},{5... | collective-permute-start | bytes 1572872 | tf_op jit(solution)/shard_map/w_out_pair_2/ppermute | solution.py:20
  46.4 3.0 %collective-permute-start.9 = (bf16[1024,256]{1,0:T(8,128)(2,1)S(1)}, bf16[1024,256]{1,0:T(8,128)(2,1)S(1)}, u32[]{:S(2)}, u32[]{:S(2)}) collective-permute-start(bf16[1024,256]{1,0:T(8,128)(2,1)S(1)} %collective-permute-done.5.refs_7_), channel_id=1, source_target_pairs={{0,8},{4,12},{8,0},{12,4},{16,24},{20,28},{24,16},{28,20},{1,9},{5... | collective-permute-start | bytes 1572872 | tf_op jit(solution)/shard_map/w_out_pair_3/ppermute | solution.py:20
  46.4 34.0 %collective-permute-start.16 = (bf16[256,1024]{1,0:T(8,128)(2,1)}, bf16[256,1024]{1,0:T(8,128)(2,1)S(1)}, u32[]{:S(2)}, u32[]{:S(2)}) collective-permute-start(bf16[256,1024]{1,0:T(8,128)(2,1)} %refs_8_.2), channel_id=1, source_target_pairs={{0,2},{1,3},{2,0},{3,1},{4,6},{5,7},{6,4},{7,5},{8,10},{9,11},{10,... | collective-permute-start | bytes 1572872 | tf_op jit(solution)/shard_map/w_query_2/ppermute | solution.py:20
  46.9 33.5 %collective-permute-start.17 = (bf16[256,1024]{1,0:T(8,128)(2,1)}, bf16[256,1024]{1,0:T(8,128)(2,1)S(1)}, u32[]{:S(2)}, u32[]{:S(2)}) collective-permute-start(bf16[256,1024]{1,0:T(8,128)(2,1)} %refs_8_.2), channel_id=1, source_target_pairs={{0,1},{1,0},{2,3},{3,2},{4,5},{5,4},{6,7},{7,6},{8,9},{9,8},{10,11... | collective-permute-start | bytes 1572872 | tf_op jit(solution)/shard_map/w_query_1/ppermute | solution.py:20
  51.2 29.0 %copy-start.44 = (f32[2,512]{1,0:T(2,128)S(1)}, f32[2,512]{1,0:T(2,128)}, u32[]{:S(2)}) copy-start(f32[2,512]{1,0:T(2,128)} %param.16) | copy-start | bytes 12292
  57.4 30.0 %copy-start.18 = (bf16[512,256]{1,0:T(8,128)(2,1)S(1)}, bf16[512,256]{1,0:T(8,128)(2,1)}, u32[]{:S(2)}) copy-start(bf16[512,256]{1,0:T(8,128)(2,1)} %attended_ref.1) | copy-start | bytes 786436
  57.4 30.0 %copy-start.25 = (bf16[512,128]{1,0:T(8,128)(2,1)S(1)}, bf16[512,128]{1,0:T(8,128)(2,1)}, u32[]{:S(2)}) copy-start(bf16[512,128]{1,0:T(8,128)(2,1)} %key_ref.3) | copy-start | bytes 393220
  57.4 30.0 %copy-start.26 = (bf16[512,128]{1,0:T(8,128)(2,1)S(1)}, bf16[512,128]{1,0:T(8,128)(2,1)}, u32[]{:S(2)}) copy-start(bf16[512,128]{1,0:T(8,128)(2,1)} %value_ref.3) | copy-start | bytes 393220
  57.4 30.0 %copy-start.27 = (bf16[512,256]{1,0:T(8,128)(2,1)S(1)}, bf16[512,256]{1,0:T(8,128)(2,1)}, u32[]{:S(2)}) copy-start(bf16[512,256]{1,0:T(8,128)(2,1)} %query_ref.1) | copy-start | bytes 786436
  57.4 30.0 %copy-start.28 = (bf16[256,256]{1,0:T(8,128)(2,1)S(1)}, bf16[256,256]{1,0:T(8,128)(2,1)}, u32[]{:S(2)}) copy-start(bf16[256,256]{1,0:T(8,128)(2,1)} %get-tuple-element.64.refs_4_) | copy-start | bytes 393220
  57.4 30.0 %copy-start.30 = (s32[3]{0:T(128)S(1)}, s32[3]{0:T(128)}, u32[]{:S(2)}) copy-start(s32[3]{0:T(128)} %pad_add_fusion.4.ranks_ref) | copy-start | bytes 40
  57.4 9.5 %collective-permute-start.10 = (bf16[128,1024]{1,0:T(8,128)(2,1)}, bf16[128,1024]{1,0:T(8,128)(2,1)S(1)}, u32[]{:S(2)}, u32[]{:S(2)}) collective-permute-start(bf16[128,1024]{1,0:T(8,128)(2,1)} %get-tuple-element.57), channel_id=1, source_target_pairs={{0,16},{4,20},{8,24},{12,28},{16,0},{20,4},{24,8},{28,12},{1,17},{... | collective-permute-start | bytes 786440 | tf_op jit(solution)/shard_map/attn_4/ppermute | solution.py:20
  59.0 13.7 %collective-permute-start.11 = (bf16[128,1024]{1,0:T(8,128)(2,1)}, bf16[128,1024]{1,0:T(8,128)(2,1)S(1)}, u32[]{:S(2)}, u32[]{:S(2)}) collective-permute-start(bf16[128,1024]{1,0:T(8,128)(2,1)} %get-tuple-element.58), channel_id=1, source_target_pairs={{0,4},{4,0},{8,12},{12,8},{16,20},{20,16},{24,28},{28,24},{1,5},{5... | collective-permute-start | bytes 786440 | tf_op jit(solution)/shard_map/attn_1/ppermute | solution.py:20
  60.5 12.2 %collective-permute-start.12 = (bf16[128,1024]{1,0:T(8,128)(2,1)}, bf16[128,1024]{1,0:T(8,128)(2,1)S(1)}, u32[]{:S(2)}, u32[]{:S(2)}) collective-permute-start(bf16[128,1024]{1,0:T(8,128)(2,1)} %get-tuple-element.59), channel_id=1, source_target_pairs={{0,20},{4,16},{8,28},{12,24},{16,4},{20,0},{24,12},{28,8},{1,21},{... | collective-permute-start | bytes 786440 | tf_op jit(solution)/shard_map/attn_5/ppermute | solution.py:20
  75.7 11.7 %collective-permute-start.13 = (bf16[256,256]{1,0:T(8,128)(2,1)}, bf16[256,256]{1,0:T(8,128)(2,1)S(1)}, u32[]{:S(2)}, u32[]{:S(2)}) collective-permute-start(bf16[256,256]{1,0:T(8,128)(2,1)} %get-tuple-element.61), channel_id=1, source_target_pairs={{0,2},{1,3},{2,0},{3,1},{4,6},{5,7},{6,4},{7,5},{8,10},{9,11},{10,... | collective-permute-start | bytes 393224 | tf_op jit(solution)/shard_map/dout_2/ppermute | solution.py:20
  76.1 11.3 %collective-permute-start.14 = (bf16[256,256]{1,0:T(8,128)(2,1)}, bf16[256,256]{1,0:T(8,128)(2,1)S(1)}, u32[]{:S(2)}, u32[]{:S(2)}) collective-permute-start(bf16[256,256]{1,0:T(8,128)(2,1)} %get-tuple-element.62), channel_id=1, source_target_pairs={{0,1},{1,0},{2,3},{3,2},{4,5},{5,4},{6,7},{7,6},{8,9},{9,8},{10,11... | collective-permute-start | bytes 393224 | tf_op jit(solution)/shard_map/dout_1/ppermute | solution.py:20
  77.7 9.7 %collective-permute-start.15 = (bf16[256,256]{1,0:T(8,128)(2,1)}, bf16[256,256]{1,0:T(8,128)(2,1)S(1)}, u32[]{:S(2)}, u32[]{:S(2)}) collective-permute-start(bf16[256,256]{1,0:T(8,128)(2,1)} %get-tuple-element.63), channel_id=1, source_target_pairs={{0,3},{1,2},{2,1},{3,0},{4,7},{5,6},{6,5},{7,4},{8,11},{9,10},{10,... | collective-permute-start | bytes 393224 | tf_op jit(solution)/shard_map/dout_3/ppermute | solution.py:20
  91.3 9.4 %collective-permute-start.18 = (bf16[256,256]{1,0:T(8,128)(2,1)S(1)}, bf16[256,256]{1,0:T(8,128)(2,1)S(1)}, u32[]{:S(2)}, u32[]{:S(2)}) collective-permute-start(bf16[256,256]{1,0:T(8,128)(2,1)S(1)} %get-tuple-element.66), channel_id=1, source_target_pairs={{0,4},{4,0},{1,5},{5,1},{2,6},{6,2},{3,7},{7,3},{8,12},{12,8},{9,1... | collective-permute-start | bytes 393224 | tf_op jit(solution)/shard_map/kv_back/ppermute | solution.py:20
  92.5 7.3 %collective-permute-start.19 = (bf16[128,256]{1,0:T(8,128)(2,1)S(1)}, bf16[128,256]{1,0:T(8,128)(2,1)S(1)}, u32[]{:S(2)}, u32[]{:S(2)}) collective-permute-start(bf16[128,256]{1,0:T(8,128)(2,1)S(1)} %get-tuple-element.67), channel_id=1, source_target_pairs={{0,2},{1,3},{2,0},{3,1},{4,6},{5,7},{6,4},{7,5},{8,10},{9,11},{10,... | collective-permute-start | bytes 196616 | tf_op jit(solution)/shard_map/dquery_2/ppermute | solution.py:20
  94.4 5.4 %collective-permute-start.20 = (bf16[128,256]{1,0:T(8,128)(2,1)S(1)}, bf16[128,256]{1,0:T(8,128)(2,1)S(1)}, u32[]{:S(2)}, u32[]{:S(2)}) collective-permute-start(bf16[128,256]{1,0:T(8,128)(2,1)S(1)} %get-tuple-element.68), channel_id=1, source_target_pairs={{0,1},{1,0},{2,3},{3,2},{4,5},{5,4},{6,7},{7,6},{8,9},{9,8},{10,11... | collective-permute-start | bytes 196616 | tf_op jit(solution)/shard_map/dquery_1/ppermute | solution.py:20
  94.5 6.2 %collective-permute-start.21 = (bf16[128,256]{1,0:T(8,128)(2,1)S(1)}, bf16[128,256]{1,0:T(8,128)(2,1)S(1)}, u32[]{:S(2)}, u32[]{:S(2)}) collective-permute-start(bf16[128,256]{1,0:T(8,128)(2,1)S(1)} %get-tuple-element.69), channel_id=1, source_target_pairs={{0,3},{1,2},{2,1},{3,0},{4,7},{5,6},{6,5},{7,4},{8,11},{9,10},{10,... | collective-permute-start | bytes 196616 | tf_op jit(solution)/shard_map/dquery_3/ppermute | solution.py:20
  101.3 7.4 %collective-permute-start.22 = (bf16[256,256]{1,0:T(8,128)(2,1)S(1)}, bf16[256,256]{1,0:T(8,128)(2,1)S(1)}, u32[]{:S(2)}, u32[]{:S(2)}) collective-permute-start(bf16[256,256]{1,0:T(8,128)(2,1)S(1)} %get-tuple-element.72), channel_id=1, source_target_pairs={{0,2},{1,3},{2,0},{3,1},{4,6},{5,7},{6,4},{7,5},{8,10},{9,11},{10,... | collective-permute-start | bytes 393224 | tf_op jit(solution)/shard_map/kv_2/ppermute | solution.py:20
  103.1 12.7 %collective-permute-start.28 = (bf16[128,1024]{1,0:T(8,128)(2,1)S(1)}, bf16[128,1024]{1,0:T(8,128)(2,1)S(1)}, u32[]{:S(2)}, u32[]{:S(2)}) collective-permute-start(bf16[128,1024]{1,0:T(8,128)(2,1)S(1)} %get-tuple-element.81.refs_4_), channel_id=1, source_target_pairs={{0,16},{4,20},{8,24},{12,28},{16,0},{20,4},{24,8},{28,12},{1,17},{... | collective-permute-start | bytes 786440 | tf_op jit(solution)/shard_map/attended_4/ppermute | solution.py:20
  104.6 11.7 %collective-permute-start.29 = (bf16[128,1024]{1,0:T(8,128)(2,1)S(1)}, bf16[128,1024]{1,0:T(8,128)(2,1)S(1)}, u32[]{:S(2)}, u32[]{:S(2)}) collective-permute-start(bf16[128,1024]{1,0:T(8,128)(2,1)S(1)} %get-tuple-element.81.refs_4_), channel_id=1, source_target_pairs={{0,4},{4,0},{8,12},{12,8},{16,20},{20,16},{24,28},{28,24},{1,5},{5... | collective-permute-start | bytes 786440 | tf_op jit(solution)/shard_map/attended_1/ppermute | solution.py:20
  106.0 11.5 %collective-permute-start.30 = (bf16[128,1024]{1,0:T(8,128)(2,1)S(1)}, bf16[128,1024]{1,0:T(8,128)(2,1)S(1)}, u32[]{:S(2)}, u32[]{:S(2)}) collective-permute-start(bf16[128,1024]{1,0:T(8,128)(2,1)S(1)} %get-tuple-element.81.refs_4_), channel_id=1, source_target_pairs={{0,20},{4,16},{8,28},{12,24},{16,4},{20,0},{24,12},{28,8},{1,21},{... | collective-permute-start | bytes 786440 | tf_op jit(solution)/shard_map/attended_5/ppermute | solution.py:20
  108.8 5.0 %collective-permute-start.23 = (bf16[128,256]{1,0:T(8,128)(2,1)S(1)}, bf16[128,256]{1,0:T(8,128)(2,1)S(1)}, u32[]{:S(2)}, u32[]{:S(2)}) collective-permute-start(bf16[128,256]{1,0:T(8,128)(2,1)S(1)} %add_convert_fusion), channel_id=1, source_target_pairs={{0,1},{1,0},{2,3},{3,2},{4,5},{5,4},{6,7},{7,6},{8,9},{9,8},{10,11... | collective-permute-start | bytes 196616 | tf_op jit(solution)/shard_map/kv_1/ppermute | solution.py:20
  113.9 16.5 %collective-permute-start.27 = (bf16[256,1024]{1,0:T(8,128)(2,1)S(1)}, bf16[256,1024]{1,0:T(8,128)(2,1)S(1)}, u32[]{:S(2)}, u32[]{:S(2)}) collective-permute-start(bf16[256,1024]{1,0:T(8,128)(2,1)S(1)} %get-tuple-element.76.refs_9_), channel_id=1, source_target_pairs={{0,1},{1,0},{2,3},{3,2},{4,5},{5,4},{6,7},{7,6},{8,9},{9,8},{10,11... | collective-permute-start | bytes 1572872 | tf_op jit(solution)/shard_map/w_query_on_1/ppermute | solution.py:20
  114.0 10.7 %collective-permute-start.24 = (bf16[128,1280]{1,0:T(8,128)(2,1)S(1)}, bf16[128,1280]{1,0:T(8,128)(2,1)S(1)}, u32[]{:S(2)}, u32[]{:S(2)}) collective-permute-start(bf16[128,1280]{1,0:T(8,128)(2,1)S(1)} %get-tuple-element.75.refs_11_.refs_0_), channel_id=1, source_target_pairs={{0,16},{4,20},{8,24},{12,28},{16,0},{20,4},{24,8},{28,12},{1,17},{... | collective-permute-start | bytes 983048 | tf_op jit(solution)/shard_map/inner_4/ppermute | solution.py:20
  115.8 14.6 %collective-permute-start.25 = (bf16[128,1280]{1,0:T(8,128)(2,1)S(1)}, bf16[128,1280]{1,0:T(8,128)(2,1)S(1)}, u32[]{:S(2)}, u32[]{:S(2)}) collective-permute-start(bf16[128,1280]{1,0:T(8,128)(2,1)S(1)} %get-tuple-element.75.refs_11_.refs_0_), channel_id=1, source_target_pairs={{0,4},{4,0},{8,12},{12,8},{16,20},{20,16},{24,28},{28,24},{1,5},{5... | collective-permute-start | bytes 983048 | tf_op jit(solution)/shard_map/inner_1/ppermute | solution.py:20
  116.3 14.1 %collective-permute-start.26 = (bf16[128,1280]{1,0:T(8,128)(2,1)S(1)}, bf16[128,1280]{1,0:T(8,128)(2,1)S(1)}, u32[]{:S(2)}, u32[]{:S(2)}) collective-permute-start(bf16[128,1280]{1,0:T(8,128)(2,1)S(1)} %get-tuple-element.75.refs_11_.refs_0_), channel_id=1, source_target_pairs={{0,20},{4,16},{8,28},{12,24},{16,4},{20,0},{24,12},{28,8},{1,21},{... | collective-permute-start | bytes 983048 | tf_op jit(solution)/shard_map/inner_5/ppermute | solution.py:20
  121.2 9.2 %collective-permute-start.31 = (bf16[1024,1024]{1,0:T(8,128)(2,1)S(1)}, bf16[1024,1024]{1,0:T(8,128)(2,1)S(1)}, u32[]{:S(2)}, u32[]{:S(2)}) collective-permute-start(bf16[1024,1024]{1,0:T(8,128)(2,1)S(1)} %get-tuple-element.85), channel_id=1, source_target_pairs={{0,8},{4,12},{8,0},{12,4},{16,24},{20,28},{24,16},{28,20},{1,9},{5... | collective-permute-start | bytes 6291464 | tf_op jit(solution)/shard_map/out_proj_pair/ppermute | solution.py:20
  124.7 7.1 %collective-permute-start.32 = (bf16[768,1024]{1,0:T(8,128)(2,1)S(1)}, bf16[768,1024]{1,0:T(8,128)(2,1)S(1)}, u32[]{:S(2)}, u32[]{:S(2)}) collective-permute-start(bf16[768,1024]{1,0:T(8,128)(2,1)S(1)} %get-tuple-element.89.refs_4_), channel_id=1, source_target_pairs={{0,8},{4,12},{8,0},{12,4},{16,24},{20,28},{24,16},{28,20},{1,9},{5... | collective-permute-start | bytes 4718600 | tf_op jit(solution)/shard_map/w_query_pair_0/ppermute | solution.py:20
  130.4 2.0 %collective-permute-start.33 = (bf16[256,1024]{1,0:T(8,128)(2,1)S(1)}, bf16[256,1024]{1,0:T(8,128)(2,1)S(1)}, u32[]{:S(2)}, u32[]{:S(2)}) collective-permute-start(bf16[256,1024]{1,0:T(8,128)(2,1)S(1)} %get-tuple-element.90.refs_5_), channel_id=1, source_target_pairs={{0,8},{4,12},{8,0},{12,4},{16,24},{20,28},{24,16},{28,20},{1,9},{5... | collective-permute-start | bytes 1572872 | tf_op jit(solution)/shard_map/w_query_pair_1/ppermute | solution.py:20
  130.6 17.7 %collective-permute-start.38 = (bf16[1024,256]{1,0:T(8,128)(2,1)S(1)}, bf16[1024,256]{1,0:T(8,128)(2,1)S(1)}, u32[]{:S(2)}, u32[]{:S(2)}) collective-permute-start(bf16[1024,256]{1,0:T(8,128)(2,1)S(1)} %add_pair.4.refs_10_.refs_2_), channel_id=1, source_target_pairs={{0,1},{1,0},{2,3},{3,2},{4,5},{5,4},{6,7},{7,6},{8,9},{9,8},{10,11... | collective-permute-start | bytes 1572872 | tf_op jit(solution)/shard_map/out_proj_3_1/ppermute | solution.py:20
  141.2 15.1 %collective-permute-start.34 = (bf16[128,2048]{1,0:T(8,128)(2,1)}, bf16[128,2048]{1,0:T(8,128)(2,1)}, u32[]{:S(2)}, u32[]{:S(2)}) collective-permute-start(bf16[128,2048]{1,0:T(8,128)(2,1)} %get-tuple-element.93.refs_3_), channel_id=1, source_target_pairs={{0,16},{4,20},{8,24},{12,28},{16,0},{20,4},{24,8},{28,12},{1,17},{... | collective-permute-start | bytes 1572872 | tf_op jit(solution)/shard_map/grads_4/ppermute | solution.py:20
  142.5 24.5 %collective-permute-start.35 = (bf16[128,2048]{1,0:T(8,128)(2,1)}, bf16[128,2048]{1,0:T(8,128)(2,1)}, u32[]{:S(2)}, u32[]{:S(2)}) collective-permute-start(bf16[128,2048]{1,0:T(8,128)(2,1)} %get-tuple-element.94), channel_id=1, source_target_pairs={{0,4},{4,0},{8,12},{12,8},{16,20},{20,16},{24,28},{28,24},{1,5},{5... | collective-permute-start | bytes 1572872 | tf_op jit(solution)/shard_map/grads_1/ppermute | solution.py:20
  144.2 23.6 %collective-permute-start.36 = (bf16[128,2048]{1,0:T(8,128)(2,1)}, bf16[128,2048]{1,0:T(8,128)(2,1)}, u32[]{:S(2)}, u32[]{:S(2)}) collective-permute-start(bf16[128,2048]{1,0:T(8,128)(2,1)} %get-tuple-element.95), channel_id=1, source_target_pairs={{0,20},{4,16},{8,28},{12,24},{16,4},{20,0},{24,12},{28,8},{1,21},{... | collective-permute-start | bytes 1572872 | tf_op jit(solution)/shard_map/grads_5/ppermute | solution.py:20
  147.1 26.7 %collective-permute-start.37 = (bf16[1024,256]{1,0:T(8,128)(2,1)S(1)}, bf16[1024,256]{1,0:T(8,128)(2,1)S(1)}, u32[]{:S(2)}, u32[]{:S(2)}) collective-permute-start(bf16[1024,256]{1,0:T(8,128)(2,1)S(1)} %add_pair.5), channel_id=1, source_target_pairs={{0,1},{1,0},{2,3},{3,2},{4,5},{5,4},{6,7},{7,6},{8,9},{9,8},{10,11... | collective-permute-start | bytes 1572872 | tf_op jit(solution)/shard_map/out_proj_1/ppermute | solution.py:20
  148.5 25.4 %collective-permute-start.39 = (bf16[1024,256]{1,0:T(8,128)(2,1)S(1)}, bf16[1024,256]{1,0:T(8,128)(2,1)S(1)}, u32[]{:S(2)}, u32[]{:S(2)}) collective-permute-start(bf16[1024,256]{1,0:T(8,128)(2,1)S(1)} %add_pair.6), channel_id=1, source_target_pairs={{0,2},{1,3},{2,0},{3,1},{4,6},{5,7},{6,4},{7,5},{8,10},{9,11},{10,... | collective-permute-start | bytes 1572872 | tf_op jit(solution)/shard_map/out_proj_2/ppermute | solution.py:20
  (38 other events, 147.4 us)

commit v4 on v3

--- a/solution.py
+++ b/solution.py
@@ -37,9 +37,11 @@
 SMALL = pl.CostEstimate(flops=0, bytes_accessed=0, transcendentals=0)
 
 
-def cut_kernel(ranks_ref, x_ref, key_ref, value_ref, *refs, parts, pair, width, carrier):
-    out_refs, sems = refs[:-1], refs[-1]
-    moves = []
+def cut_kernel(
+    ranks_ref, x_ref, key_ref, value_ref, weight_ref, *refs, parts, pair, width, carrier
+):
+    out_refs, weight_out_ref, sems = refs[:-2], refs[-2], refs[-1]
+    moves = [(weight_ref, weight_out_ref)]
     for i, k in enumerate(parts):
         for half in range(2):
             owner = lax.bitwise_xor(ranks_ref[0], k ^ (half * pair))
@@ -62,22 +64,23 @@
         copy.wait()
 
 
-def cut(ranks, x, keys, values, parts, pair, width, carrier):
-    rows = x.shape[0]
+def cut(ranks, x, keys, values, weight, parts, pair, carrier):
+    rows, width = x.shape[0], weight.shape[0]
     extra = 2 * (keys.shape[1] + values.shape[1])
     return pl.pallas_call(
         functools.partial(cut_kernel, parts=parts, pair=pair, width=width, carrier=carrier),
         out_shape=[
             jax.ShapeDtypeStruct((rows, 2 * width + (extra if i == carrier else 0)), x.dtype)
             for i in range(len(parts))
-        ],
-        in_specs=[pl.BlockSpec(memory_space=pltpu.SMEM)] + [ANY] * 3,
-        out_specs=[VMEM] * len(parts),
-        scratch_shapes=[pltpu.SemaphoreType.DMA((2 * len(parts) + 4,))],
+        ]
+        + [jax.ShapeDtypeStruct(weight.shape, weight.dtype)],
+        in_specs=[pl.BlockSpec(memory_space=pltpu.SMEM)] + [ANY] * 4,
+        out_specs=[VMEM] * (len(parts) + 1),
+        scratch_shapes=[pltpu.SemaphoreType.DMA((2 * len(parts) + 5,))],
         compiler_params=pltpu.CompilerParams(vmem_limit_bytes=60 * 2**20),
         cost_estimate=SMALL,
         name="cut",
-    )(ranks, x, keys, values)
+    )(ranks, x, keys, values, weight)
 
 
 def project_kernel(*refs, tokens, pieces, carrier):
@@ -121,7 +124,7 @@
         in_specs=[VMEM] * (len(tokens) + 2 * len(own)),
         out_specs=[VMEM] * len(out_shape),
         scratch_shapes=[pltpu.VMEM((rows * len(tokens), 2 * width), BF16)],
-        compiler_params=pltpu.CompilerParams(vmem_limit_bytes=60 * 2**20),
+        compiler_params=pltpu.CompilerParams(vmem_limit_bytes=20 * 2**20),
         cost_estimate=SMALL,
         name="project",
     )(*tokens, *own, *pair)
@@ -145,35 +148,38 @@
 
 
 def add_kernel(ranks_ref, own_ref, att_ref, *refs, parts):
-    part_refs, out_refs = refs[:parts], refs[parts:]
+    part_refs, out_refs, share_refs = refs[:parts], refs[parts : -4], refs[-4:]
     rows, cols = out_refs[0].shape
     total = own_ref[...]
     for ref in part_refs:
         total = total + ref[...].astype(F32)
-    for j, (distance, ref) in enumerate(zip(TENSOR_ORDER, out_refs)):
-        ref[:rows, :] = total[:, j * cols : (j + 1) * cols].astype(BF16)
-        if distance:
-            owner = lax.bitwise_xor(ranks_ref[1], distance)
-            ref[rows:, :] = att_ref[pl.ds(pl.multiple_of(owner * rows, rows), rows), :]
+    for j, ref in enumerate(out_refs):
+        ref[...] = total[:, j * cols : (j + 1) * cols].astype(BF16)
+    for j, ref in zip(TENSOR_ORDER, share_refs):
+        owner = lax.bitwise_xor(ranks_ref[1], j)
+        ref[...] = att_ref[pl.ds(pl.multiple_of(owner * rows, rows), rows), :]
 
 
 def add_up(ranks, own, attended, parts):
     rows, cols = own.shape[0], attended.shape[1]
+    peers = len(TENSOR_ORDER)
     return pl.pallas_call(
         functools.partial(add_kernel, parts=len(parts)),
-        out_shape=[
-            jax.ShapeDtypeStruct((2 * rows if j else rows, cols), BF16) for j in TENSOR_ORDER
-        ],
+        out_shape=[jax.ShapeDtypeStruct((rows, cols), BF16)] * (2 * peers),
         in_specs=[pl.BlockSpec(memory_space=pltpu.SMEM)] + [VMEM] * (2 + len(parts)),
-        out_specs=[VMEM] * len(TENSOR_ORDER),
+        out_specs=[VMEM] * (2 * peers),
         compiler_params=pltpu.CompilerParams(vmem_limit_bytes=60 * 2**20),
         cost_estimate=SMALL,
         name="add_up",
     )(ranks, own, attended, *parts)
 
 
-def join_kernel(ranks_ref, kv_ref, *refs, backs):
-    back_refs, (away_ref, next_ref, own_ref), held = refs[:backs], refs[-5:-2], refs[-1]
+def join_kernel(ranks_ref, kv_ref, *refs, backs, atts):
+    back_refs, att_refs = refs[:backs], refs[backs : backs + atts]
+    (away_ref, next_ref, own_ref, att_own_ref), held = refs[-5:-1], refs[-1]
+    cols = att_refs[0].shape[1]
+    for i, ref in enumerate(att_refs):
+        att_own_ref[:, i * cols : (i + 1) * cols] = ref[...]
     rows = own_ref.shape[0]
     span = kv_ref.shape[0] // 2
     held[...] = kv_ref[...]
@@ -194,26 +200,25 @@
     own_ref[...] = rank_rows(0)
 
 
-def join(ranks, kv, back, behind, later):
+def join(ranks, kv, back, atts, behind):
     rows, width = kv.shape[0] // len(TENSOR_ORDER), kv.shape[1]
     return pl.pallas_call(
-        functools.partial(join_kernel, backs=len(back)),
+        functools.partial(join_kernel, backs=len(back), atts=len(atts)),
         out_shape=[
             jax.ShapeDtypeStruct((2 * rows, width), BF16),
             jax.ShapeDtypeStruct((rows, width), F32),
             jax.ShapeDtypeStruct((rows, width), F32),
-            jax.ShapeDtypeStruct(later.shape, later.dtype),
+            jax.ShapeDtypeStruct((rows, len(atts) * atts[0].shape[1]), BF16),
         ],
         in_specs=[pl.BlockSpec(memory_space=pltpu.SMEM)]
-        + [VMEM] * (1 + len(back))
-        + [ANY] * (len(behind) + 1),
-        out_specs=[VMEM] * 3 + [ANY],
-        input_output_aliases={2 + len(back) + len(behind): 3},
+        + [VMEM] * (1 + len(back) + len(atts))
+        + [ANY] * len(behind),
+        out_specs=[VMEM] * 4,
         scratch_shapes=[pltpu.VMEM(kv.shape, F32)],
-        compiler_params=pltpu.CompilerParams(vmem_limit_bytes=16 * 2**20),
+        compiler_params=pltpu.CompilerParams(vmem_limit_bytes=8 * 2**20),
         cost_estimate=SMALL,
         name="join",
-    )(ranks, kv, *back, *behind, later)
+    )(ranks, kv, *back, *atts, *behind)
 
 
 def inner_kernel(rest_ref, got_ref, next_ref, *refs, pieces):
@@ -236,7 +241,7 @@
         in_specs=[VMEM] * (3 + len(queries)) + [ANY] * (1 + len(behind)),
         out_specs=[VMEM, ANY],
         input_output_aliases={3 + len(queries): 1},
-        compiler_params=pltpu.CompilerParams(vmem_limit_bytes=16 * 2**20),
+        compiler_params=pltpu.CompilerParams(vmem_limit_bytes=8 * 2**20),
         cost_estimate=SMALL,
         name="inner",
     )(rest, got, from_next, *queries, later, *behind)
@@ -279,7 +284,7 @@
         in_specs=[VMEM] * (len(tokens) + len(atts) + len(weights)) + [ANY] * len(behind),
         out_specs=[VMEM] * (len(TENSOR_ORDER) + 2),
         scratch_shapes=[pltpu.VMEM((depth, 2 * width), BF16), pltpu.VMEM((depth, columns), BF16)],
-        compiler_params=pltpu.CompilerParams(vmem_limit_bytes=40 * 2**20),
+        compiler_params=pltpu.CompilerParams(vmem_limit_bytes=20 * 2**20),
         cost_estimate=SMALL,
         name="outer",
     )(*tokens, *atts, *weights, *behind)
@@ -362,10 +367,48 @@
             pltpu.VMEM((2 * w_key.shape[0], 2 * width), BF16),
             pltpu.SemaphoreType.DMA((4,)),
         ],
-        compiler_params=pltpu.CompilerParams(vmem_limit_bytes=60 * 2**20),
+        compiler_params=pltpu.CompilerParams(vmem_limit_bytes=20 * 2**20),
         cost_estimate=SMALL,
         name="feed",
     )(ranks, *inners, *own, *pair, w_key, w_value, *behind)
+
+
+def place_kernel(ranks_ref, *refs, parts, distance):
+    out_ref, sems = refs[-2], refs[-1]
+    width = refs[0].shape[1] // 2
+    copies = []
+    for i, (k, ref) in enumerate(zip(parts, refs)):
+        for half in range(2):
+            owner = lax.bitwise_xor(ranks_ref[0], k ^ (half * distance))
+            at = pl.ds(pl.multiple_of(owner * width, width), width)
+            copies.append(
+                pltpu.make_async_copy(
+                    ref.at[:, half * width : (half + 1) * width],
+                    out_ref.at[:, at],
+                    sems.at[2 * i + half],
+                )
+            )
+    for copy in copies:
+        copy.start()
+    for copy in copies:
+        copy.wait()
+
+
+def place_blocks(ranks, blocks, parts, distance, features, out):
+    given = [] if out is None else [out]
+    return pl.pallas_call(
+        functools.partial(place_kernel, parts=parts, distance=distance),
+        out_shape=jax.ShapeDtypeStruct((blocks[0].shape[0], features), BF16),
+        in_specs=[pl.BlockSpec(memory_space=pltpu.SMEM)]
+        + [VMEM] * len(blocks)
+        + [ANY] * len(given),
+        out_specs=ANY,
+        scratch_shapes=[pltpu.SemaphoreType.DMA((2 * len(blocks),))],
+        input_output_aliases={1 + len(blocks): 0} if given else {},
+        compiler_params=pltpu.CompilerParams(vmem_limit_bytes=16 * 2**20),
+        cost_estimate=SMALL,
+        name="place",
+    )(ranks, *blocks, *given)
 
 
 def attention_kernel(
@@ -373,8 +416,8 @@
     *refs, peers, befores, cycle_size,
 ):
     dout_refs, before_refs = refs[:peers], refs[peers : peers + befores]
-    dquery_refs, away_refs = refs[-4 - befores - peers : -4 - befores], refs[-4 - befores : -4]
-    kv_grads_ref, att_own_ref, dout_held, dquery_held = refs[-4:]
+    dquery_refs, away_refs = refs[-3 - befores - peers : -3 - befores], refs[-3 - befores : -3]
+    kv_grads_ref, dout_held, dquery_held = refs[-3:]
     rank, last_rank = ranks_ref[1], ranks_ref[2] == cycle_size - 1
     head_dim = key_ref.shape[1]
     span = query_ref.shape[0] // 2
@@ -390,10 +433,8 @@
             [x[:, h * head_dim : (h + 1) * head_dim] for h in range(heads)], axis=0
         )
 
-    cols = query_ref.shape[1]
-    for i, (j, ref) in enumerate(zip(TENSOR_ORDER, dout_refs)):
-        dout_held[place(lax.bitwise_xor(rank, j)), :] = ref[:sub, :]
-        att_own_ref[:, i * cols : (i + 1) * cols] = ref[sub:, :] if j else attended_ref[place(rank), :]
+    for j, ref in zip(TENSOR_ORDER, dout_refs):
+        dout_held[place(lax.bitwise_xor(rank, j)), :] = ref[...]
     before = []
     for b in range(2):
         rows = slice(b * span, (b + 1) * span)
@@ -450,14 +491,11 @@
         ),
         out_shape=[jax.ShapeDtypeStruct(dout[0].shape, BF16) for _ in dout]
         + [jax.ShapeDtypeStruct(x.shape, BF16) for x in before]
-        + [
-            jax.ShapeDtypeStruct(kv_shape, F32),
-            jax.ShapeDtypeStruct((dout[0].shape[0], len(dout) * dout[0].shape[1]), BF16),
-        ],
+        + [jax.ShapeDtypeStruct(kv_shape, F32)],
         in_specs=[pl.BlockSpec(memory_space=pltpu.SMEM)]
         + [VMEM] * (7 + len(dout) + len(before))
         + [ANY] * len(behind),
-        out_specs=[VMEM] * (len(dout) + len(before) + 2),
+        out_specs=[VMEM] * (len(dout) + len(before) + 1),
         scratch_shapes=[pltpu.VMEM(queries.shape, BF16)] * 2,
         compiler_params=pltpu.CompilerParams(vmem_limit_bytes=32 * 2**20),
         cost_estimate=SMALL,
@@ -496,15 +534,16 @@
 
     ranks = jnp.stack([plane_rank, tensor_rank, cycle_pos])
     carrier = meets.index(1) + 1 if cycle_size == 2 else None
-    tokens = cut(ranks, grad_out, keys, values, [0] + meets, pair, width, carrier)
+    *tokens, w_out_copy = cut(ranks, grad_out, keys, values, w_out, [0] + meets, pair, carrier)
     tokens = [tokens[0]] + [swapped(x, PLANE, k, f"tokens_{k}") for k, x in zip(meets, tokens[1:])]
-    out_2 = hand_on([out_2], [], FLOPS // 10)[0]
-    out_2 = hand_on([out_2], tokens[1:2])[0]
+    out_2, out_1 = hand_on([out_2, out_1], [], FLOPS // 10)
+    out_2, w_out_copy = hand_on([out_2, w_out_copy], tokens[1:2])
     out_1 = hand_on([out_1], tokens[2:], FLOPS)[0]
-    w_out_own = [w_out, out_2, out_1, along(out_2, 1, "w_out_on")]
+    w_out_own = [w_out_copy, out_2, out_1, along(out_2, 1, "w_out_on")]
     w_out_pair = [across(w, f"w_out_pair_{i}") for i, w in enumerate(w_out_own)]
 
     query_2, query_1 = along(w_query, 2, "w_query"), along(w_query, 1, "w_query")
+    query_2, query_1 = hand_on([query_2, query_1], [], FLOPS // 10)
 
     seg_row = segment_ids[0]
     high_span = 2 * cycle_size - 1 - cycle_pos
@@ -529,9 +568,13 @@
         kv_pair = jnp.concatenate([keys, values], axis=1)
         before = neighbours(kv_pair[span:], kv_pair[:span])
     parts = [swapped(x, PLANE, k, f"attn_{k}") for k, x in zip(meets, partial_attn[1:])]
-    dout = add_up(ranks, partial_attn[0], attended, parts)
+    shared = add_up(ranks, partial_attn[0], attended, parts)
+    dout, atts = shared[:4], shared[4:]
     dout = [dout[0]] + [along(x, j, "dout") for x, j in zip(dout[1:], TENSOR_ORDER[1:])]
-    *dquery, kv_grads, att_own = attention(
+    dout[1:] = hand_on(dout[1:], [], FLOPS // 10)
+    atts = [along(x, j, "attended") for x, j in zip(atts[1:], TENSOR_ORDER[1:])]
+    atts = [shared[4], *hand_on(atts, [], FLOPS // 10)]
+    *dquery, kv_grads = attention(
         ranks, seg_query, seg_key, queries, attended, keys, values, log_rows, dout, before,
         [query_2, query_1], cycle_size,
     )
@@ -539,7 +582,7 @@
 
     dquery = dquery[:1] + [along(x, j, "dquery") for x, j in zip(dquery[1:], TENSOR_ORDER[1:])]
     back = [swapped(away[0], "context", 1, "kv_back")] if cycle_size == 2 else neighbours(*away)
-    kv_away, kv_next, kv_rest, att_own = join(ranks, kv_grads, back, dquery[1:], att_own)
+    kv_away, kv_next, kv_rest, att_own = join(ranks, kv_grads, back, atts, dquery[1:])
     att_met = plane_gather(att_own, "attended")
     att_met[1:] = hand_on(att_met[1:], [], FLOPS // 10)
     got = along(kv_away, 2, "kv")
@@ -557,28 +600,24 @@
     out_pair = across(out_pair, "out_proj_pair")
     to_3 = add_pair(out_own[3], out_pair, 3, [], BF16, [])
     from_3 = along(to_3, 1, "out_proj_3")
+    to_1 = add_pair(out_own[2], out_pair, 2, [], BF16, [to_3])
     *inner_met[1:], query_3 = hand_on([*inner_met[1:], query_3], [], FLOPS)
     *inner_met[1:], query_3 = hand_on([*inner_met[1:], query_3], [out_pair])
     w_query_own = [w_query_own, query_3]
     w_query_pair = [across(w, f"w_query_pair_{i}") for i, w in enumerate(w_query_own)]
 
     blocks = feed(
-        ranks, inner_met, w_query_own, w_query_pair, w_key, w_value, pair, [to_3]
-    )
-    to_1 = add_pair(out_own[2], out_pair, 2, [], BF16, [to_3])
+        ranks, inner_met, w_query_own, w_query_pair, w_key, w_value, pair, [to_3, to_1]
+    )
     to_2 = add_pair(out_own[1], out_pair, 1, [from_3], BF16, [blocks[1]])
     out_proj_grad = add_pair(
         out_own[0], out_pair, 0, [along(to_1, 1, "out_proj"), along(to_2, 2, "out_proj")], F32, []
     )
     blocks = [(0, blocks[0])] + [(k, swapped(x, PLANE, k, f"grads_{k}")) for k, x in zip(meets, blocks[1:])]
-    received = hand_on([x for _, x in blocks[1:]], [], FLOPS)
-    blocks = blocks[:1] + list(zip(meets, received))
-    grad_input = jnp.zeros((own_rows, features), BF16)
-    for k, block in blocks:
-        for i, owner in enumerate((plane_rank ^ k, plane_rank ^ k ^ pair)):
-            grad_input = lax.dynamic_update_slice_in_dim(
-                grad_input, block[:, i * width : (i + 1) * width], owner * width, axis=1
-            )
+    grad_input = place_blocks(ranks, [blocks[0][1]], [0], pair, features, None)
+    for k, block in blocks[1:]:
+        grad_input = place_blocks(ranks, [block], [k], pair, features, grad_input)
+    grad_input = hand_on([grad_input], [], FLOPS)[0]
     return (grad_input, out_proj_grad)
 
 

time: 176 us -> 164 us (0.932)
  local copies, waits for them, and re-layouts: 13.9 us -> 4.28 us
  waiting for transfers between devices: 87.1 us -> 79.9 us
  starting transfers between devices: 43.5 us -> 48.7 us
    ppermute x40 -> x43, waiting for transfers between devices: 87.1 us -> 79.9 us  [swapped(): return lax.ppermute(x, axes, [(i, i ^ bit) for i in range(size)])]
    dynamic_update_slice x8 -> x0, local copies, waits for them, and re-layouts: 5.98 us -> none  [on_device(): lax.dynamic_update_slice_in_dim(grad_input, block[:, i * width:(i + 1) *...]
    pallas_call x1 -> x5, Pallas kernels: 0.63 us -> 6.06 us  [the longest x4 5.4 us: place_blocks(): pl.pallas_call(functools.partial(place_kernel, parts=parts, distance=dist...]
    ppermute x40 -> x43, starting transfers between devices: 43.5 us -> 48.7 us  [swapped(): return lax.ppermute(x, axes, [(i, i ^ bit) for i in range(size)])]
    pallas_call x1, Pallas kernels: 7.88 us -> 3.82 us  [feed(): pl.pallas_call(functools.partial(feed_kernel, tokens=len(inners), pieces=...]
    unnamed x93 -> x37, local copies, waits for them, and re-layouts: 7.62 us -> 4.14 us
  transfers between devices with their start and end apart: 40 -> 43, of which waited for: 18 -> 20; matrix products, arithmetic and copies ran while one was open for 4% -> 1% of each run, Pallas kernels for 14% -> 17%
where the time goes in v4:
time: 164 us
  waiting for transfers between devices  79.9 us (49%)
  starting transfers between devices  48.7 us (30%)
  Pallas kernels  29.4 us (18%)
  local copies, waits for them, and re-layouts  4.28 us (3%)
    ppermute x43, waiting for transfers between devices, swapped(): return lax.ppermute(x, axes, [(i, i ^ bit) for i in range(size)])  79.9 us
    ppermute x43, starting transfers between devices, swapped(): return lax.ppermute(x, axes, [(i, i ^ bit) for i in range(size)])  48.7 us
    pallas_call x4, Pallas kernels, place_blocks(): pl.pallas_call(functools.partial(place_kernel, parts=parts, distance=dist...  5.4 us
    pallas_call x1, Pallas kernels, project(): pl.pallas_call(functools.partial(project_kernel, tokens=len(tokens), piec...  5.01 us
    unnamed x37, local copies, waits for them, and re-layouts  4.14 us
    pallas_call x1, Pallas kernels, cut(): pl.pallas_call(functools.partial(cut_kernel, parts=parts, pair=pair, widt...  3.98 us
    pallas_call x1, Pallas kernels, feed(): pl.pallas_call(functools.partial(feed_kernel, tokens=len(inners), pieces=...  3.82 us
    pallas_call x1, Pallas kernels, outer(): pl.pallas_call(functools.partial(outer_kernel, tokens=len(tokens), atts=l...  3.67 us
  transfers between devices with their start and end apart: 43, of which 20 were waited for; matrix products, arithmetic and copies ran while one was open for 1% of the time, Pallas kernels for 17%

profile of v4, /device:TPU:0, one launch (start us, length us, event | category | flops | bytes accessed | tf_op | source)
XLA Modules:
  0.0 163.9 jit_solution(15244843431950989267)
XLA Ops:
  0.6 4.1 %collective-permute-start.3 = (bf16[1024,256]{1,0:T(8,128)(2,1)}, bf16[1024,256]{1,0:T(8,128)(2,1)S(1)}, u32[]{:S(2)}, u32[]{:S(2)}) collective-permute-start(bf16[1024,256]{1,0:T(8,128)(2,1)} %weight_ref.1), channel_id=1, source_target_pairs={{0,2},{1,3},{2,0},{3,1},{4,6},{5,7},{6,4},{7,5},{8,10},{9,11},{10,... | collective-permute-start | bytes 1572872 | tf_op jit(solution)/shard_map/w_out_2/ppermute | solution.py:20
  4.7 1.6 collective-permute-start.4
  6.9 4.0 %cut.1 = (bf16[128,2048]{1,0:T(8,128)(2,1)}, bf16[128,2048]{1,0:T(8,128)(2,1)}, bf16[128,2560]{1,0:T(8,128)(2,1)}, bf16[128,2048]{1,0:T(8,128)(2,1)}, bf16[1024,256]{1,0:T(8,128)(2,1)}) custom-call(s32[3]{0:T(128)} %pad_add_fusion.4.ranks_ref, bf16[128,8192]{1,0:T(8,128)(2,1)} %x_ref.1, bf16[512,128]{1,0:T(8,128)(2,1)} %key_ref.3, ...), custom_call_target="tpu_custom_call" | custom-call | tf_op jit(solution)/shard_map/cut/pallas_call | solution.py:70
  10.9 1.6 collective-permute-start.1
  12.5 1.5 collective-permute-start
  14.5 13.7 %collective-permute-done.3.refs_0_ = bf16[1024,256]{1,0:T(8,128)(2,1)S(1)} collective-permute-done((bf16[1024,256]{1,0:T(8,128)(2,1)}, bf16[1024,256]{1,0:T(8,128)(2,1)S(1)}, u32[]{:S(2)}, u32[]{:S(2)}) %collective-permute-start.3) | collective-permute-done | bytes 524320 | tf_op jit(solution)/shard_map/w_out_2/ppermute | solution.py:20
  28.5 1.5 collective-permute-start.5
  30.5 6.3 %collective-permute-done.2.refs_2_.refs_3_ = bf16[128,2048]{1,0:T(8,128)(2,1)S(1)} collective-permute-done((bf16[128,2048]{1,0:T(8,128)(2,1)}, bf16[128,2048]{1,0:T(8,128)(2,1)S(1)}, u32[]{:S(2)}, u32[]{:S(2)}) %collective-permute-start.2) | collective-permute-done | bytes 524320 | tf_op jit(solution)/shard_map/tokens_5/ppermute | solution.py:20
  36.8 1.5 collective-permute-done.1.refs_1_.refs_2_
  38.3 3.1 %collective-permute-done.5.refs_7_ = bf16[1024,256]{1,0:T(8,128)(2,1)} collective-permute-done((bf16[1024,256]{1,0:T(8,128)(2,1)S(1)}, bf16[1024,256]{1,0:T(8,128)(2,1)}, u32[]{:S(2)}, u32[]{:S(2)}) %collective-permute-start.5) | collective-permute-done | bytes 524320 | tf_op jit(solution)/shard_map/w_out_on_1/ppermute | solution.py:20
  41.4 3.0 %collective-permute-start.16 = (bf16[256,1024]{1,0:T(8,128)(2,1)}, bf16[256,1024]{1,0:T(8,128)(2,1)S(1)}, u32[]{:S(2)}, u32[]{:S(2)}) collective-permute-start(bf16[256,1024]{1,0:T(8,128)(2,1)} %refs_8_.2), channel_id=1, source_target_pairs={{0,2},{1,3},{2,0},{3,1},{4,6},{5,7},{6,4},{7,5},{8,10},{9,11},{10,... | collective-permute-start | bytes 1572872 | tf_op jit(solution)/shard_map/w_query_2/ppermute | solution.py:20
  45.3 1.7 %collective-permute-start.17 = (bf16[256,1024]{1,0:T(8,128)(2,1)}, bf16[256,1024]{1,0:T(8,128)(2,1)}, u32[]{:S(2)}, u32[]{:S(2)}) collective-permute-start(bf16[256,1024]{1,0:T(8,128)(2,1)} %refs_8_.2), channel_id=1, source_target_pairs={{0,1},{1,0},{2,3},{3,2},{4,5},{5,4},{6,7},{7,6},{8,9},{9,8},{10,11... | collective-permute-start | bytes 1572872 | tf_op jit(solution)/shard_map/w_query_1/ppermute | solution.py:20
  48.1 5.0 %project.1 = (f32[128,1024]{1,0:T(8,128)S(1)}, bf16[128,1024]{1,0:T(8,128)(2,1)}, bf16[128,1024]{1,0:T(8,128)(2,1)}, bf16[128,1024]{1,0:T(8,128)(2,1)}, bf16[256,256]{1,0:T(8,128)(2,1)S(1)}) custom-call(bf16[128,2048]{1,0:T(8,128)(2,1)S(1)} %copy-done, bf16[128,2048]{1,0:T(8,128)(2,1)S(1)} %collective-permute-done.refs_2_.refs_1_, ...), custom_call_target="tpu_custom_call" | custom-call | tf_op jit(solution)/shard_map/project/pallas_call | solution.py:119
  53.9 1.5 collective-permute-start.10
  55.4 1.5 collective-permute-start.11
  57.8 5.6 %collective-permute-done.10.refs_0_ = bf16[128,1024]{1,0:T(8,128)(2,1)} collective-permute-done((bf16[128,1024]{1,0:T(8,128)(2,1)}, bf16[128,1024]{1,0:T(8,128)(2,1)}, u32[]{:S(2)}, u32[]{:S(2)}) %collective-permute-start.10) | collective-permute-done | bytes 262176 | tf_op jit(solution)/shard_map/attn_4/ppermute | solution.py:20
  63.4 5.8 %collective-permute-done.11.refs_1_ = bf16[128,1024]{1,0:T(8,128)(2,1)} collective-permute-done((bf16[128,1024]{1,0:T(8,128)(2,1)}, bf16[128,1024]{1,0:T(8,128)(2,1)}, u32[]{:S(2)}, u32[]{:S(2)}) %collective-permute-start.11) | collective-permute-done | bytes 262176 | tf_op jit(solution)/shard_map/attn_1/ppermute | solution.py:20
  69.2 2.2 %add_up.1 = (bf16[128,256]{1,0:T(8,128)(2,1)}, bf16[128,256]{1,0:T(8,128)(2,1)}, bf16[128,256]{1,0:T(8,128)(2,1)}, bf16[128,256]{1,0:T(8,128)(2,1)}, bf16[128,25...) custom-call(s32[3]{0:T(128)} %pad_add_fusion.4.ranks_ref, ...), custom_call_target="tpu_custom_call" | custom-call | tf_op jit(solution)/shard_map/add_up/pallas_call | solution.py:166
  71.7 1.3 collective-permute-start.14
  73.1 2.8 %collective-permute-start.15 = (bf16[128,256]{1,0:T(8,128)(2,1)}, bf16[128,256]{1,0:T(8,128)(2,1)S(1)}, u32[]{:S(2)}, u32[]{:S(2)}) collective-permute-start(bf16[128,256]{1,0:T(8,128)(2,1)} %get-tuple-element.81), channel_id=1, source_target_pairs={{0,3},{1,2},{2,1},{3,0},{4,7},{5,6},{6,5},{7,4},{8,11},{9,10},{10,... | collective-permute-start | bytes 196616 | tf_op jit(solution)/shard_map/dout_3/ppermute | solution.py:20
  75.9 1.6 collective-permute-start.20
  77.5 2.3 %collective-permute-done.13.refs_0_ = bf16[128,256]{1,0:T(8,128)(2,1)S(1)} collective-permute-done((bf16[128,256]{1,0:T(8,128)(2,1)}, bf16[128,256]{1,0:T(8,128)(2,1)S(1)}, u32[]{:S(2)}, u32[]{:S(2)}) %collective-permute-start.13) | collective-permute-done | bytes 65568 | tf_op jit(solution)/shard_map/dout_2/ppermute | solution.py:20
  81.0 3.0 %attention.1 = (bf16[128,256]{1,0:T(8,128)(2,1)S(1)}, bf16[128,256]{1,0:T(8,128)(2,1)S(1)}, bf16[128,256]{1,0:T(8,128)(2,1)S(1)}, bf16[128,256]{1,0:T(8,128)(2,1...) custom-call(s32[3]{0:T(128)S(1)} %copy-done.12, s32[512,1]{1,0:T(8,128)S(1)} %copy.44.seg_query_ref, ...), custom_call_target="tpu_custom_call" | custom-call | tf_op jit(solution)/shard_map/attention/pallas_call | solution.py:488
  84.1 1.5 collective-permute-start.18
  85.5 2.4 %collective-permute-start.22 = (bf16[128,256]{1,0:T(8,128)(2,1)S(1)}, bf16[128,256]{1,0:T(8,128)(2,1)S(1)}, u32[]{:S(2)}, u32[]{:S(2)}) collective-permute-start(bf16[128,256]{1,0:T(8,128)(2,1)S(1)} %get-tuple-element.97), channel_id=1, source_target_pairs={{0,2},{1,3},{2,0},{3,1},{4,6},{5,7},{6,4},{7,5},{8,10},{9,11},{10,... | collective-permute-start | bytes 196616 | tf_op jit(solution)/shard_map/dquery_2/ppermute | solution.py:20
  88.8 1.7 %collective-permute-start.24 = (bf16[128,256]{1,0:T(8,128)(2,1)S(1)}, bf16[128,256]{1,0:T(8,128)(2,1)S(1)}, u32[]{:S(2)}, u32[]{:S(2)}) collective-permute-start(bf16[128,256]{1,0:T(8,128)(2,1)S(1)} %get-tuple-element.99), channel_id=1, source_target_pairs={{0,3},{1,2},{2,1},{3,0},{4,7},{5,6},{6,5},{7,4},{8,11},{9,10},{10,... | collective-permute-start | bytes 196616 | tf_op jit(solution)/shard_map/dquery_3/ppermute | solution.py:20
  90.7 1.5 collective-permute-done.23.refs_6_.refs_2_
  92.3 3.2 %collective-permute-done.24.refs_7_.refs_3_ = bf16[128,256]{1,0:T(8,128)(2,1)S(1)} collective-permute-done((bf16[128,256]{1,0:T(8,128)(2,1)S(1)}, bf16[128,256]{1,0:T(8,128)(2,1)S(1)}, u32[]{:S(2)}, u32[]{:S(2)}) %collective-permute-start.24) | collective-permute-done | bytes 65568 | tf_op jit(solution)/shard_map/dquery_3/ppermute | solution.py:20
  96.1 1.7 %collective-permute-start.25 = (bf16[256,256]{1,0:T(8,128)(2,1)S(1)}, bf16[256,256]{1,0:T(8,128)(2,1)S(1)}, u32[]{:S(2)}, u32[]{:S(2)}) collective-permute-start(bf16[256,256]{1,0:T(8,128)(2,1)S(1)} %get-tuple-element.101), channel_id=1, source_target_pairs={{0,2},{1,3},{2,0},{3,1},{4,6},{5,7},{6,4},{7,5},{8,10},{9,11},{10,... | collective-permute-start | bytes 393224 | tf_op jit(solution)/shard_map/kv_2/ppermute | solution.py:20
  98.9 1.4 collective-permute-start.32
  101.3 2.2 %collective-permute-done.25.got_ref = bf16[256,256]{1,0:T(8,128)(2,1)S(1)} collective-permute-done((bf16[256,256]{1,0:T(8,128)(2,1)S(1)}, bf16[256,256]{1,0:T(8,128)(2,1)S(1)}, u32[]{:S(2)}, u32[]{:S(2)}) %collective-permute-start.25) | collective-permute-done | bytes 131104 | tf_op jit(solution)/shard_map/kv_2/ppermute | solution.py:20
  104.0 4.7 %collective-permute-done.26.next_ref = bf16[128,256]{1,0:T(8,128)(2,1)S(1)} collective-permute-done((bf16[128,256]{1,0:T(8,128)(2,1)S(1)}, bf16[128,256]{1,0:T(8,128)(2,1)S(1)}, u32[]{:S(2)}, u32[]{:S(2)}) %collective-permute-start.26) | collective-permute-done | bytes 65568 | tf_op jit(solution)/shard_map/kv_1/ppermute | solution.py:20
  109.4 1.5 collective-permute-start.28
  110.8 1.8 %collective-permute-start.29 = (bf16[128,1280]{1,0:T(8,128)(2,1)S(1)}, bf16[128,1280]{1,0:T(8,128)(2,1)S(1)}, u32[]{:S(2)}, u32[]{:S(2)}) collective-permute-start(bf16[128,1280]{1,0:T(8,128)(2,1)S(1)} %get-tuple-element.104.refs_11_.refs_0_), channel_id=1, source_target_pairs={{0,20},{4,16},{8,28},{12,24},{16,4},{20,0},{24,12},{28,8},{1,21},{... | collective-permute-start | bytes 983048 | tf_op jit(solution)/shard_map/inner_5/ppermute | solution.py:20
  112.6 3.7 %outer.1 = (f32[1024,256]{1,0:T(8,128)S(1)}, f32[1024,256]{1,0:T(8,128)S(1)}, f32[1024,256]{1,0:T(8,128)S(1)}, f32[1024,256]{1,0:T(8,128)S(1)}, bf16[1024,1024]{...) custom-call(bf16[128,2048]{1,0:T(8,128)(2,1)S(1)} %copy-done, bf16[128,2048]{1,0:T(8,128)(2,1)S(1)} %collective-permute-done.refs_2_.refs_1_, ...), custom_call_target="tpu_custom_call" | custom-call | tf_op jit(solution)/shard_map/outer/pallas_call | solution.py:275
  117.6 4.5 %collective-permute-done.28.refs_1_ = bf16[128,1280]{1,0:T(8,128)(2,1)S(1)} collective-permute-done((bf16[128,1280]{1,0:T(8,128)(2,1)S(1)}, bf16[128,1280]{1,0:T(8,128)(2,1)S(1)}, u32[]{:S(2)}, u32[]{:S(2)}) %collective-permute-start.28) | collective-permute-done | bytes 327712 | tf_op jit(solution)/shard_map/inner_1/ppermute | solution.py:20
  124.8 3.8 %feed.1 = (bf16[128,2048]{1,0:T(8,128)(2,1)S(1)}, bf16[128,2048]{1,0:T(8,128)(2,1)S(1)}, bf16[128,2048]{1,0:T(8,128)(2,1)S(1)}, bf16[128,2048]{1,0:T(8,128)(2,1)S(1)}) custom-call(s32[3]{0:T(128)S(1)} %copy-done.12, bf16[128,1280]{1,0:T(8,128)(2,1)S(1)} %get-tuple-element.104.refs_11_.refs_0_, bf16[128,1280]{1,0:T(8,128)(2,1)S(1)} %get-tuple-element.115.refs_1_, ...), custom_call_target="tpu_custom_call" | custom-call | tf_op jit(solution)/shard_map/feed/pallas_call | solution.py:358
  128.7 1.4 collective-permute-start.39
  130.8 1.4 collective-permute-start.37
  132.2 1.8 %collective-permute-start.40 = (bf16[1024,256]{1,0:T(8,128)(2,1)S(1)}, bf16[1024,256]{1,0:T(8,128)(2,1)S(1)}, u32[]{:S(2)}, u32[]{:S(2)}) collective-permute-start(bf16[1024,256]{1,0:T(8,128)(2,1)S(1)} %add_pair.5.refs_11_), channel_id=1, source_target_pairs={{0,1},{1,0},{2,3},{3,2},{4,5},{5,4},{6,7},{7,6},{8,9},{9,8},{10,11... | collective-permute-start | bytes 1572872 | tf_op jit(solution)/shard_map/out_proj_1/ppermute | solution.py:20
  134.0 3.1 %collective-permute-done.41.refs_2_ = bf16[1024,256]{1,0:T(8,128)(2,1)S(1)} collective-permute-done((bf16[1024,256]{1,0:T(8,128)(2,1)S(1)}, bf16[1024,256]{1,0:T(8,128)(2,1)S(1)}, u32[]{:S(2)}, u32[]{:S(2)}) %collective-permute-start.41) | collective-permute-done | bytes 524320 | tf_op jit(solution)/shard_map/out_proj_3_1/ppermute | solution.py:20
  138.1 1.3 place.4.refs_1_
  139.4 4.0 %collective-permute-done.39.refs_0_ = bf16[128,2048]{1,0:T(8,128)(2,1)S(1)} collective-permute-done((bf16[128,2048]{1,0:T(8,128)(2,1)S(1)}, bf16[128,2048]{1,0:T(8,128)(2,1)S(1)}, u32[]{:S(2)}, u32[]{:S(2)}) %collective-permute-start.39) | collective-permute-done | bytes 524320 | tf_op jit(solution)/shard_map/grads_4/ppermute | solution.py:20
  143.5 1.4 place.5.refs_1_
  144.8 10.3 %collective-permute-done.38.refs_0_ = bf16[128,2048]{1,0:T(8,128)(2,1)S(1)} collective-permute-done((bf16[128,2048]{1,0:T(8,128)(2,1)S(1)}, bf16[128,2048]{1,0:T(8,128)(2,1)S(1)}, u32[]{:S(2)}, u32[]{:S(2)}) %collective-permute-start.38) | collective-permute-done | bytes 524320 | tf_op jit(solution)/shard_map/grads_1/ppermute | solution.py:20
  155.1 1.4 place.6.refs_1_
  156.5 1.4 place.7.refs_0_
  157.9 4.8 %collective-permute-done.42.refs_3_ = bf16[1024,256]{1,0:T(8,128)(2,1)S(1)} collective-permute-done((bf16[1024,256]{1,0:T(8,128)(2,1)S(1)}, bf16[1024,256]{1,0:T(8,128)(2,1)S(1)}, u32[]{:S(2)}, u32[]{:S(2)}) %collective-permute-start.42) | collective-permute-done | bytes 524320 | tf_op jit(solution)/shard_map/out_proj_2/ppermute | solution.py:20
  (107 shorter events, 18.8 us)
Async XLA Ops:
  0.6 27.6 %collective-permute-start.3 = (bf16[1024,256]{1,0:T(8,128)(2,1)}, bf16[1024,256]{1,0:T(8,128)(2,1)S(1)}, u32[]{:S(2)}, u32[]{:S(2)}) collective-permute-start(bf16[1024,256]{1,0:T(8,128)(2,1)} %weight_ref.1), channel_id=1, source_target_pairs={{0,2},{1,3},{2,0},{3,1},{4,6},{5,7},{6,4},{7,5},{8,10},{9,11},{10,... | collective-permute-start | bytes 1572872 | tf_op jit(solution)/shard_map/w_out_2/ppermute | solution.py:20
  4.7 23.8 %collective-permute-start.4 = (bf16[1024,256]{1,0:T(8,128)(2,1)}, bf16[1024,256]{1,0:T(8,128)(2,1)}, u32[]{:S(2)}, u32[]{:S(2)}) collective-permute-start(bf16[1024,256]{1,0:T(8,128)(2,1)} %weight_ref.1), channel_id=1, source_target_pairs={{0,1},{1,0},{2,3},{3,2},{4,5},{5,4},{6,7},{7,6},{8,9},{9,8},{10,11... | collective-permute-start | bytes 1572872 | tf_op jit(solution)/shard_map/w_out_1/ppermute | solution.py:20
  10.9 27.4 %collective-permute-start.1 = (bf16[128,2560]{1,0:T(8,128)(2,1)}, bf16[128,2560]{1,0:T(8,128)(2,1)S(1)}, u32[]{:S(2)}, u32[]{:S(2)}) collective-permute-start(bf16[128,2560]{1,0:T(8,128)(2,1)} %get-tuple-element.67), channel_id=1, source_target_pairs={{0,4},{4,0},{8,12},{12,8},{16,20},{20,16},{24,28},{28,24},{1,5},{5... | collective-permute-start | bytes 1966088 | tf_op jit(solution)/shard_map/tokens_1/ppermute | solution.py:20
  12.5 16.0 %collective-permute-start = (bf16[128,2048]{1,0:T(8,128)(2,1)}, bf16[128,2048]{1,0:T(8,128)(2,1)S(1)}, u32[]{:S(2)}, u32[]{:S(2)}) collective-permute-start(bf16[128,2048]{1,0:T(8,128)(2,1)} %get-tuple-element.66), channel_id=1, source_target_pairs={{0,16},{4,20},{8,24},{12,28},{16,0},{20,4},{24,8},{28,12},{1,17},{... | collective-permute-start | bytes 1572872 | tf_op jit(solution)/shard_map/tokens_4/ppermute | solution.py:20
  14.0 22.8 %collective-permute-start.2 = (bf16[128,2048]{1,0:T(8,128)(2,1)}, bf16[128,2048]{1,0:T(8,128)(2,1)S(1)}, u32[]{:S(2)}, u32[]{:S(2)}) collective-permute-start(bf16[128,2048]{1,0:T(8,128)(2,1)} %get-tuple-element.68), channel_id=1, source_target_pairs={{0,20},{4,16},{8,28},{12,24},{16,4},{20,0},{24,12},{28,8},{1,21},{... | collective-permute-start | bytes 1572872 | tf_op jit(solution)/shard_map/tokens_5/ppermute | solution.py:20
  28.5 12.9 %collective-permute-start.5 = (bf16[1024,256]{1,0:T(8,128)(2,1)S(1)}, bf16[1024,256]{1,0:T(8,128)(2,1)}, u32[]{:S(2)}, u32[]{:S(2)}) collective-permute-start(bf16[1024,256]{1,0:T(8,128)(2,1)S(1)} %get-tuple-element.72.refs_5_), channel_id=1, source_target_pairs={{0,1},{1,0},{2,3},{3,2},{4,5},{5,4},{6,7},{7,6},{8,9},{9,8},{10,11... | collective-permute-start | bytes 1572872 | tf_op jit(solution)/shard_map/w_out_on_1/ppermute | solution.py:20
  30.0 14.5 %collective-permute-start.7 = (bf16[1024,256]{1,0:T(8,128)(2,1)S(1)}, bf16[1024,256]{1,0:T(8,128)(2,1)S(1)}, u32[]{:S(2)}, u32[]{:S(2)}) collective-permute-start(bf16[1024,256]{1,0:T(8,128)(2,1)S(1)} %get-tuple-element.72.refs_5_), channel_id=1, source_target_pairs={{0,8},{4,12},{8,0},{12,4},{16,24},{20,28},{24,16},{28,20},{1,9},{5... | collective-permute-start | bytes 1572872 | tf_op jit(solution)/shard_map/w_out_pair_1/ppermute | solution.py:20
  30.0 17.0 %collective-permute-start.6 = (bf16[1024,256]{1,0:T(8,128)(2,1)}, bf16[1024,256]{1,0:T(8,128)(2,1)}, u32[]{:S(2)}, u32[]{:S(2)}) collective-permute-start(bf16[1024,256]{1,0:T(8,128)(2,1)} %get-tuple-element.71.refs_4_), channel_id=1, source_target_pairs={{0,8},{4,12},{8,0},{12,4},{16,24},{20,28},{24,16},{28,20},{1,9},{5... | collective-permute-start | bytes 1572872 | tf_op jit(solution)/shard_map/w_out_pair_0/ppermute | solution.py:20
  38.3 8.7 %copy-start = (bf16[128,2048]{1,0:T(8,128)(2,1)S(1)}, bf16[128,2048]{1,0:T(8,128)(2,1)}, u32[]{:S(2)}) copy-start(bf16[128,2048]{1,0:T(8,128)(2,1)} %get-tuple-element.65.refs_0_) | copy-start | bytes 1572868
  38.3 8.7 %collective-permute-start.8 = (bf16[1024,256]{1,0:T(8,128)(2,1)}, bf16[1024,256]{1,0:T(8,128)(2,1)}, u32[]{:S(2)}, u32[]{:S(2)}) collective-permute-start(bf16[1024,256]{1,0:T(8,128)(2,1)} %hand_on.12.refs_6_), channel_id=1, source_target_pairs={{0,8},{4,12},{8,0},{12,4},{16,24},{20,28},{24,16},{28,20},{1,9},{5... | collective-permute-start | bytes 1572872 | tf_op jit(solution)/shard_map/w_out_pair_2/ppermute | solution.py:20
  41.4 5.6 %collective-permute-start.9 = (bf16[1024,256]{1,0:T(8,128)(2,1)}, bf16[1024,256]{1,0:T(8,128)(2,1)}, u32[]{:S(2)}, u32[]{:S(2)}) collective-permute-start(bf16[1024,256]{1,0:T(8,128)(2,1)} %collective-permute-done.5.refs_7_), channel_id=1, source_target_pairs={{0,8},{4,12},{8,0},{12,4},{16,24},{20,28},{24,16},{28,20},{1,9},{5... | collective-permute-start | bytes 1572872 | tf_op jit(solution)/shard_map/w_out_pair_3/ppermute | solution.py:20
  41.4 34.4 %collective-permute-start.16 = (bf16[256,1024]{1,0:T(8,128)(2,1)}, bf16[256,1024]{1,0:T(8,128)(2,1)S(1)}, u32[]{:S(2)}, u32[]{:S(2)}) collective-permute-start(bf16[256,1024]{1,0:T(8,128)(2,1)} %refs_8_.2), channel_id=1, source_target_pairs={{0,2},{1,3},{2,0},{3,1},{4,6},{5,7},{6,4},{7,5},{8,10},{9,11},{10,... | collective-permute-start | bytes 1572872 | tf_op jit(solution)/shard_map/w_query_2/ppermute | solution.py:20
  45.3 30.5 %collective-permute-start.17 = (bf16[256,1024]{1,0:T(8,128)(2,1)}, bf16[256,1024]{1,0:T(8,128)(2,1)}, u32[]{:S(2)}, u32[]{:S(2)}) collective-permute-start(bf16[256,1024]{1,0:T(8,128)(2,1)} %refs_8_.2), channel_id=1, source_target_pairs={{0,1},{1,0},{2,3},{3,2},{4,5},{5,4},{6,7},{7,6},{8,9},{9,8},{10,11... | collective-permute-start | bytes 1572872 | tf_op jit(solution)/shard_map/w_query_1/ppermute | solution.py:20
  48.1 9.3 %copy-start.14 = (s32[1,1024]{1,0:T(1,128)S(1)}, s32[1,1024]{1,0:T(1,128)}, u32[]{:S(2)}) copy-start(s32[1,1024]{1,0:T(1,128)} %param.17) | copy-start | bytes 12292
  48.1 9.5 %copy-start.13 = (f32[2,512]{1,0:T(2,128)S(1)}, f32[2,512]{1,0:T(2,128)}, u32[]{:S(2)}) copy-start(f32[2,512]{1,0:T(2,128)} %param.16) | copy-start | bytes 12292
  53.9 9.5 %collective-permute-start.10 = (bf16[128,1024]{1,0:T(8,128)(2,1)}, bf16[128,1024]{1,0:T(8,128)(2,1)}, u32[]{:S(2)}, u32[]{:S(2)}) collective-permute-start(bf16[128,1024]{1,0:T(8,128)(2,1)} %get-tuple-element.75), channel_id=1, source_target_pairs={{0,16},{4,20},{8,24},{12,28},{16,0},{20,4},{24,8},{28,12},{1,17},{... | collective-permute-start | bytes 786440 | tf_op jit(solution)/shard_map/attn_4/ppermute | solution.py:20
  55.4 13.8 %collective-permute-start.11 = (bf16[128,1024]{1,0:T(8,128)(2,1)}, bf16[128,1024]{1,0:T(8,128)(2,1)}, u32[]{:S(2)}, u32[]{:S(2)}) collective-permute-start(bf16[128,1024]{1,0:T(8,128)(2,1)} %get-tuple-element.76), channel_id=1, source_target_pairs={{0,4},{4,0},{8,12},{12,8},{16,20},{20,16},{24,28},{28,24},{1,5},{5... | collective-permute-start | bytes 786440 | tf_op jit(solution)/shard_map/attn_1/ppermute | solution.py:20
  56.9 12.3 %collective-permute-start.12 = (bf16[128,1024]{1,0:T(8,128)(2,1)}, bf16[128,1024]{1,0:T(8,128)(2,1)}, u32[]{:S(2)}, u32[]{:S(2)}) collective-permute-start(bf16[128,1024]{1,0:T(8,128)(2,1)} %get-tuple-element.77), channel_id=1, source_target_pairs={{0,20},{4,16},{8,28},{12,24},{16,4},{20,0},{24,12},{28,8},{1,21},{... | collective-permute-start | bytes 786440 | tf_op jit(solution)/shard_map/attn_5/ppermute | solution.py:20
  71.4 8.5 %collective-permute-start.13 = (bf16[128,256]{1,0:T(8,128)(2,1)}, bf16[128,256]{1,0:T(8,128)(2,1)S(1)}, u32[]{:S(2)}, u32[]{:S(2)}) collective-permute-start(bf16[128,256]{1,0:T(8,128)(2,1)} %get-tuple-element.79), channel_id=1, source_target_pairs={{0,2},{1,3},{2,0},{3,1},{4,6},{5,7},{6,4},{7,5},{8,10},{9,11},{10,... | collective-permute-start | bytes 196616 | tf_op jit(solution)/shard_map/dout_2/ppermute | solution.py:20
  71.7 8.7 %collective-permute-start.14 = (bf16[128,256]{1,0:T(8,128)(2,1)}, bf16[128,256]{1,0:T(8,128)(2,1)S(1)}, u32[]{:S(2)}, u32[]{:S(2)}) collective-permute-start(bf16[128,256]{1,0:T(8,128)(2,1)} %get-tuple-element.80), channel_id=1, source_target_pairs={{0,1},{1,0},{2,3},{3,2},{4,5},{5,4},{6,7},{7,6},{8,9},{9,8},{10,11... | collective-permute-start | bytes 196616 | tf_op jit(solution)/shard_map/dout_1/ppermute | solution.py:20
  73.1 6.8 %copy-start.15 = (bf16[128,256]{1,0:T(8,128)(2,1)S(1)}, bf16[128,256]{1,0:T(8,128)(2,1)}, u32[]{:S(2)}) copy-start(bf16[128,256]{1,0:T(8,128)(2,1)} %get-tuple-element.93) | copy-start | bytes 196612
  73.1 7.4 %collective-permute-start.15 = (bf16[128,256]{1,0:T(8,128)(2,1)}, bf16[128,256]{1,0:T(8,128)(2,1)S(1)}, u32[]{:S(2)}, u32[]{:S(2)}) collective-permute-start(bf16[128,256]{1,0:T(8,128)(2,1)} %get-tuple-element.81), channel_id=1, source_target_pairs={{0,3},{1,2},{2,1},{3,0},{4,7},{5,6},{6,5},{7,4},{8,11},{9,10},{10,... | collective-permute-start | bytes 196616 | tf_op jit(solution)/shard_map/dout_3/ppermute | solution.py:20
  75.8 12.1 %collective-permute-start.19 = (bf16[128,256]{1,0:T(8,128)(2,1)S(1)}, bf16[128,256]{1,0:T(8,128)(2,1)S(1)}, u32[]{:S(2)}, u32[]{:S(2)}) collective-permute-start(bf16[128,256]{1,0:T(8,128)(2,1)S(1)} %copy-done.17), channel_id=1, source_target_pairs={{0,2},{1,3},{2,0},{3,1},{4,6},{5,7},{6,4},{7,5},{8,10},{9,11},{10,... | collective-permute-start | bytes 196616 | tf_op jit(solution)/shard_map/attended_2/ppermute | solution.py:20
  75.9 12.9 %collective-permute-start.20 = (bf16[128,256]{1,0:T(8,128)(2,1)S(1)}, bf16[128,256]{1,0:T(8,128)(2,1)S(1)}, u32[]{:S(2)}, u32[]{:S(2)}) collective-permute-start(bf16[128,256]{1,0:T(8,128)(2,1)S(1)} %copy-done.16), channel_id=1, source_target_pairs={{0,1},{1,0},{2,3},{3,2},{4,5},{5,4},{6,7},{7,6},{8,9},{9,8},{10,11... | collective-permute-start | bytes 196616 | tf_op jit(solution)/shard_map/attended_1/ppermute | solution.py:20
  79.9 10.6 %collective-permute-start.21 = (bf16[128,256]{1,0:T(8,128)(2,1)S(1)}, bf16[128,256]{1,0:T(8,128)(2,1)S(1)}, u32[]{:S(2)}, u32[]{:S(2)}) collective-permute-start(bf16[128,256]{1,0:T(8,128)(2,1)S(1)} %copy-done.15), channel_id=1, source_target_pairs={{0,3},{1,2},{2,1},{3,0},{4,7},{5,6},{6,5},{7,4},{8,11},{9,10},{10,... | collective-permute-start | bytes 196616 | tf_op jit(solution)/shard_map/attended_3/ppermute | solution.py:20
  84.1 11.4 %collective-permute-start.18 = (bf16[256,256]{1,0:T(8,128)(2,1)S(1)}, bf16[256,256]{1,0:T(8,128)(2,1)S(1)}, u32[]{:S(2)}, u32[]{:S(2)}) collective-permute-start(bf16[256,256]{1,0:T(8,128)(2,1)S(1)} %get-tuple-element.89), channel_id=1, source_target_pairs={{0,4},{4,0},{1,5},{5,1},{2,6},{6,2},{3,7},{7,3},{8,12},{12,8},{9,1... | collective-permute-start | bytes 393224 | tf_op jit(solution)/shard_map/kv_back/ppermute | solution.py:20
  85.5 5.2 %collective-permute-start.22 = (bf16[128,256]{1,0:T(8,128)(2,1)S(1)}, bf16[128,256]{1,0:T(8,128)(2,1)S(1)}, u32[]{:S(2)}, u32[]{:S(2)}) collective-permute-start(bf16[128,256]{1,0:T(8,128)(2,1)S(1)} %get-tuple-element.97), channel_id=1, source_target_pairs={{0,2},{1,3},{2,0},{3,1},{4,6},{5,7},{6,4},{7,5},{8,10},{9,11},{10,... | collective-permute-start | bytes 196616 | tf_op jit(solution)/shard_map/dquery_2/ppermute | solution.py:20
  88.0 4.3 %collective-permute-start.23 = (bf16[128,256]{1,0:T(8,128)(2,1)S(1)}, bf16[128,256]{1,0:T(8,128)(2,1)S(1)}, u32[]{:S(2)}, u32[]{:S(2)}) collective-permute-start(bf16[128,256]{1,0:T(8,128)(2,1)S(1)} %get-tuple-element.98), channel_id=1, source_target_pairs={{0,1},{1,0},{2,3},{3,2},{4,5},{5,4},{6,7},{7,6},{8,9},{9,8},{10,11... | collective-permute-start | bytes 196616 | tf_op jit(solution)/shard_map/dquery_1/ppermute | solution.py:20
  88.8 6.7 %copy-start.10 = (bf16[128,256]{1,0:T(8,128)(2,1)S(1)}, bf16[128,256]{1,0:T(8,128)(2,1)}, u32[]{:S(2)}) copy-start(bf16[128,256]{1,0:T(8,128)(2,1)} %get-tuple-element.90.refs_1_) | copy-start | bytes 196612
  88.8 6.6 %collective-permute-start.24 = (bf16[128,256]{1,0:T(8,128)(2,1)S(1)}, bf16[128,256]{1,0:T(8,128)(2,1)S(1)}, u32[]{:S(2)}, u32[]{:S(2)}) collective-permute-start(bf16[128,256]{1,0:T(8,128)(2,1)S(1)} %get-tuple-element.99), channel_id=1, source_target_pairs={{0,3},{1,2},{2,1},{3,0},{4,7},{5,6},{6,5},{7,4},{8,11},{9,10},{10,... | collective-permute-start | bytes 196616 | tf_op jit(solution)/shard_map/dquery_3/ppermute | solution.py:20
  96.1 7.4 %collective-permute-start.25 = (bf16[256,256]{1,0:T(8,128)(2,1)S(1)}, bf16[256,256]{1,0:T(8,128)(2,1)S(1)}, u32[]{:S(2)}, u32[]{:S(2)}) collective-permute-start(bf16[256,256]{1,0:T(8,128)(2,1)S(1)} %get-tuple-element.101), channel_id=1, source_target_pairs={{0,2},{1,3},{2,0},{3,1},{4,6},{5,7},{6,4},{7,5},{8,10},{9,11},{10,... | collective-permute-start | bytes 393224 | tf_op jit(solution)/shard_map/kv_2/ppermute | solution.py:20
  97.8 11.5 %collective-permute-start.31 = (bf16[128,1024]{1,0:T(8,128)(2,1)S(1)}, bf16[128,1024]{1,0:T(8,128)(2,1)S(1)}, u32[]{:S(2)}, u32[]{:S(2)}) collective-permute-start(bf16[128,1024]{1,0:T(8,128)(2,1)S(1)} %get-tuple-element.110.refs_4_), channel_id=1, source_target_pairs={{0,16},{4,20},{8,24},{12,28},{16,0},{20,4},{24,8},{28,12},{1,17},{... | collective-permute-start | bytes 786440 | tf_op jit(solution)/shard_map/attended_4/ppermute | solution.py:20
  98.9 12.0 %collective-permute-start.32 = (bf16[128,1024]{1,0:T(8,128)(2,1)S(1)}, bf16[128,1024]{1,0:T(8,128)(2,1)S(1)}, u32[]{:S(2)}, u32[]{:S(2)}) collective-permute-start(bf16[128,1024]{1,0:T(8,128)(2,1)S(1)} %get-tuple-element.110.refs_4_), channel_id=1, source_target_pairs={{0,4},{4,0},{8,12},{12,8},{16,20},{20,16},{24,28},{28,24},{1,5},{5... | collective-permute-start | bytes 786440 | tf_op jit(solution)/shard_map/attended_1/ppermute | solution.py:20
  100.3 12.3 %collective-permute-start.33 = (bf16[128,1024]{1,0:T(8,128)(2,1)S(1)}, bf16[128,1024]{1,0:T(8,128)(2,1)S(1)}, u32[]{:S(2)}, u32[]{:S(2)}) collective-permute-start(bf16[128,1024]{1,0:T(8,128)(2,1)S(1)} %get-tuple-element.110.refs_4_), channel_id=1, source_target_pairs={{0,20},{4,16},{8,28},{12,24},{16,4},{20,0},{24,12},{28,8},{1,21},{... | collective-permute-start | bytes 786440 | tf_op jit(solution)/shard_map/attended_5/ppermute | solution.py:20
  103.6 5.1 %collective-permute-start.26 = (bf16[128,256]{1,0:T(8,128)(2,1)S(1)}, bf16[128,256]{1,0:T(8,128)(2,1)S(1)}, u32[]{:S(2)}, u32[]{:S(2)}) collective-permute-start(bf16[128,256]{1,0:T(8,128)(2,1)S(1)} %add_convert_fusion), channel_id=1, source_target_pairs={{0,1},{1,0},{2,3},{3,2},{4,5},{5,4},{6,7},{7,6},{8,9},{9,8},{10,11... | collective-permute-start | bytes 196616 | tf_op jit(solution)/shard_map/kv_1/ppermute | solution.py:20
  108.7 13.4 %collective-permute-start.30 = (bf16[256,1024]{1,0:T(8,128)(2,1)S(1)}, bf16[256,1024]{1,0:T(8,128)(2,1)S(1)}, u32[]{:S(2)}, u32[]{:S(2)}) collective-permute-start(bf16[256,1024]{1,0:T(8,128)(2,1)S(1)} %get-tuple-element.105.refs_9_), channel_id=1, source_target_pairs={{0,1},{1,0},{2,3},{3,2},{4,5},{5,4},{6,7},{7,6},{8,9},{9,8},{10,11... | collective-permute-start | bytes 1572872 | tf_op jit(solution)/shard_map/w_query_on_1/ppermute | solution.py:20
  109.1 8.5 %collective-permute-start.27 = (bf16[128,1280]{1,0:T(8,128)(2,1)S(1)}, bf16[128,1280]{1,0:T(8,128)(2,1)S(1)}, u32[]{:S(2)}, u32[]{:S(2)}) collective-permute-start(bf16[128,1280]{1,0:T(8,128)(2,1)S(1)} %get-tuple-element.104.refs_11_.refs_0_), channel_id=1, source_target_pairs={{0,16},{4,20},{8,24},{12,28},{16,0},{20,4},{24,8},{28,12},{1,17},{... | collective-permute-start | bytes 983048 | tf_op jit(solution)/shard_map/inner_4/ppermute | solution.py:20
  109.4 12.7 %collective-permute-start.28 = (bf16[128,1280]{1,0:T(8,128)(2,1)S(1)}, bf16[128,1280]{1,0:T(8,128)(2,1)S(1)}, u32[]{:S(2)}, u32[]{:S(2)}) collective-permute-start(bf16[128,1280]{1,0:T(8,128)(2,1)S(1)} %get-tuple-element.104.refs_11_.refs_0_), channel_id=1, source_target_pairs={{0,4},{4,0},{8,12},{12,8},{16,20},{20,16},{24,28},{28,24},{1,5},{5... | collective-permute-start | bytes 983048 | tf_op jit(solution)/shard_map/inner_1/ppermute | solution.py:20
  110.8 11.3 %collective-permute-start.29 = (bf16[128,1280]{1,0:T(8,128)(2,1)S(1)}, bf16[128,1280]{1,0:T(8,128)(2,1)S(1)}, u32[]{:S(2)}, u32[]{:S(2)}) collective-permute-start(bf16[128,1280]{1,0:T(8,128)(2,1)S(1)} %get-tuple-element.104.refs_11_.refs_0_), channel_id=1, source_target_pairs={{0,20},{4,16},{8,28},{12,24},{16,4},{20,0},{24,12},{28,8},{1,21},{... | collective-permute-start | bytes 983048 | tf_op jit(solution)/shard_map/inner_5/ppermute | solution.py:20
  116.3 5.8 %collective-permute-start.34 = (bf16[1024,1024]{1,0:T(8,128)(2,1)S(1)}, bf16[1024,1024]{1,0:T(8,128)(2,1)S(1)}, u32[]{:S(2)}, u32[]{:S(2)}) collective-permute-start(bf16[1024,1024]{1,0:T(8,128)(2,1)S(1)} %get-tuple-element.114), channel_id=1, source_target_pairs={{0,8},{4,12},{8,0},{12,4},{16,24},{20,28},{24,16},{28,20},{1,9},{5... | collective-permute-start | bytes 6291464 | tf_op jit(solution)/shard_map/out_proj_pair/ppermute | solution.py:20
  117.6 5.2 %collective-permute-start.35 = (bf16[768,1024]{1,0:T(8,128)(2,1)S(1)}, bf16[768,1024]{1,0:T(8,128)(2,1)S(1)}, u32[]{:S(2)}, u32[]{:S(2)}) collective-permute-start(bf16[768,1024]{1,0:T(8,128)(2,1)S(1)} %get-tuple-element.118.refs_4_), channel_id=1, source_target_pairs={{0,8},{4,12},{8,0},{12,4},{16,24},{20,28},{24,16},{28,20},{1,9},{5... | collective-permute-start | bytes 4718600 | tf_op jit(solution)/shard_map/w_query_pair_0/ppermute | solution.py:20
  122.1 2.0 %collective-permute-start.36 = (bf16[256,1024]{1,0:T(8,128)(2,1)S(1)}, bf16[256,1024]{1,0:T(8,128)(2,1)S(1)}, u32[]{:S(2)}, u32[]{:S(2)}) collective-permute-start(bf16[256,1024]{1,0:T(8,128)(2,1)S(1)} %get-tuple-element.119.refs_5_), channel_id=1, source_target_pairs={{0,8},{4,12},{8,0},{12,4},{16,24},{20,28},{24,16},{28,20},{1,9},{5... | collective-permute-start | bytes 1572872 | tf_op jit(solution)/shard_map/w_query_pair_1/ppermute | solution.py:20
  122.3 14.8 %collective-permute-start.41 = (bf16[1024,256]{1,0:T(8,128)(2,1)S(1)}, bf16[1024,256]{1,0:T(8,128)(2,1)S(1)}, u32[]{:S(2)}, u32[]{:S(2)}) collective-permute-start(bf16[1024,256]{1,0:T(8,128)(2,1)S(1)} %add_pair.4.refs_2_.refs_10_), channel_id=1, source_target_pairs={{0,1},{1,0},{2,3},{3,2},{4,5},{5,4},{6,7},{7,6},{8,9},{9,8},{10,11... | collective-permute-start | bytes 1572872 | tf_op jit(solution)/shard_map/out_proj_3_1/ppermute | solution.py:20
  128.7 14.8 %collective-permute-start.39 = (bf16[128,2048]{1,0:T(8,128)(2,1)S(1)}, bf16[128,2048]{1,0:T(8,128)(2,1)S(1)}, u32[]{:S(2)}, u32[]{:S(2)}) collective-permute-start(bf16[128,2048]{1,0:T(8,128)(2,1)S(1)} %get-tuple-element.124.refs_3_), channel_id=1, source_target_pairs={{0,16},{4,20},{8,24},{12,28},{16,0},{20,4},{24,8},{28,12},{1,17},{... | collective-permute-start | bytes 1572872 | tf_op jit(solution)/shard_map/grads_4/ppermute | solution.py:20
  130.0 25.1 %collective-permute-start.38 = (bf16[128,2048]{1,0:T(8,128)(2,1)S(1)}, bf16[128,2048]{1,0:T(8,128)(2,1)S(1)}, u32[]{:S(2)}, u32[]{:S(2)}) collective-permute-start(bf16[128,2048]{1,0:T(8,128)(2,1)S(1)} %get-tuple-element.123), channel_id=1, source_target_pairs={{0,4},{4,0},{8,12},{12,8},{16,20},{20,16},{24,28},{28,24},{1,5},{5... | collective-permute-start | bytes 1572872 | tf_op jit(solution)/shard_map/grads_1/ppermute | solution.py:20
  130.8 25.7 %collective-permute-start.37 = (bf16[128,2048]{1,0:T(8,128)(2,1)S(1)}, bf16[128,2048]{1,0:T(8,128)(2,1)S(1)}, u32[]{:S(2)}, u32[]{:S(2)}) collective-permute-start(bf16[128,2048]{1,0:T(8,128)(2,1)S(1)} %get-tuple-element.122), channel_id=1, source_target_pairs={{0,20},{4,16},{8,28},{12,24},{16,4},{20,0},{24,12},{28,8},{1,21},{... | collective-permute-start | bytes 1572872 | tf_op jit(solution)/shard_map/grads_5/ppermute | solution.py:20
  132.2 25.6 %collective-permute-start.40 = (bf16[1024,256]{1,0:T(8,128)(2,1)S(1)}, bf16[1024,256]{1,0:T(8,128)(2,1)S(1)}, u32[]{:S(2)}, u32[]{:S(2)}) collective-permute-start(bf16[1024,256]{1,0:T(8,128)(2,1)S(1)} %add_pair.5.refs_11_), channel_id=1, source_target_pairs={{0,1},{1,0},{2,3},{3,2},{4,5},{5,4},{6,7},{7,6},{8,9},{9,8},{10,11... | collective-permute-start | bytes 1572872 | tf_op jit(solution)/shard_map/out_proj_1/ppermute | solution.py:20
  137.3 25.4 %collective-permute-start.42 = (bf16[1024,256]{1,0:T(8,128)(2,1)S(1)}, bf16[1024,256]{1,0:T(8,128)(2,1)S(1)}, u32[]{:S(2)}, u32[]{:S(2)}) collective-permute-start(bf16[1024,256]{1,0:T(8,128)(2,1)S(1)} %add_pair.6), channel_id=1, source_target_pairs={{0,2},{1,3},{2,0},{3,1},{4,6},{5,7},{6,4},{7,5},{8,10},{9,11},{10,... | collective-permute-start | bytes 1572872 | tf_op jit(solution)/shard_map/out_proj_2/ppermute | solution.py:20
  (13 other events, 18.5 us)

commit v5 on v4

--- a/solution.py
+++ b/solution.py
@@ -284,7 +284,7 @@
         in_specs=[VMEM] * (len(tokens) + len(atts) + len(weights)) + [ANY] * len(behind),
         out_specs=[VMEM] * (len(TENSOR_ORDER) + 2),
         scratch_shapes=[pltpu.VMEM((depth, 2 * width), BF16), pltpu.VMEM((depth, columns), BF16)],
-        compiler_params=pltpu.CompilerParams(vmem_limit_bytes=20 * 2**20),
+        compiler_params=pltpu.CompilerParams(vmem_limit_bytes=14 * 2**20),
         cost_estimate=SMALL,
         name="outer",
     )(*tokens, *atts, *weights, *behind)
@@ -307,7 +307,7 @@
         out_shape=jax.ShapeDtypeStruct(own.shape, dtype),
         in_specs=[whole, columns] + [whole] * len(others) + [ANY] * len(behind),
         out_specs=whole,
-        compiler_params=pltpu.CompilerParams(vmem_limit_bytes=16 * 2**20),
+        compiler_params=pltpu.CompilerParams(vmem_limit_bytes=8 * 2**20),
         cost_estimate=SMALL,
         name="add_pair",
     )(own, pair, *others, *behind)
@@ -367,7 +367,7 @@
             pltpu.VMEM((2 * w_key.shape[0], 2 * width), BF16),
             pltpu.SemaphoreType.DMA((4,)),
         ],
-        compiler_params=pltpu.CompilerParams(vmem_limit_bytes=20 * 2**20),
+        compiler_params=pltpu.CompilerParams(vmem_limit_bytes=14 * 2**20),
         cost_estimate=SMALL,
         name="feed",
     )(ranks, *inners, *own, *pair, w_key, w_value, *behind)
@@ -405,7 +405,7 @@
         out_specs=ANY,
         scratch_shapes=[pltpu.SemaphoreType.DMA((2 * len(blocks),))],
         input_output_aliases={1 + len(blocks): 0} if given else {},
-        compiler_params=pltpu.CompilerParams(vmem_limit_bytes=16 * 2**20),
+        compiler_params=pltpu.CompilerParams(vmem_limit_bytes=4 * 2**20),
         cost_estimate=SMALL,
         name="place",
     )(ranks, *blocks, *given)

time: 164 us -> 164 us (level)
  no operation moved by 1% of the time
where the time goes in v5:
time: 164 us
  waiting for transfers between devices  79.9 us (49%)
  starting transfers between devices  48.7 us (30%)
  Pallas kernels  29.5 us (18%)
  local copies, waits for them, and re-layouts  4.28 us (3%)
    ppermute x43, waiting for transfers between devices, swapped(): return lax.ppermute(x, axes, [(i, i ^ bit) for i in range(size)])  79.9 us
    ppermute x43, starting transfers between devices, swapped(): return lax.ppermute(x, axes, [(i, i ^ bit) for i in range(size)])  48.7 us
    pallas_call x4, Pallas kernels, place_blocks(): pl.pallas_call(functools.partial(place_kernel, parts=parts, distance=dist...  5.4 us
    pallas_call x1, Pallas kernels, project(): pl.pallas_call(functools.partial(project_kernel, tokens=len(tokens), piec...  5.01 us
    unnamed x37, local copies, waits for them, and re-layouts  4.14 us
    pallas_call x1, Pallas kernels, cut(): pl.pallas_call(functools.partial(cut_kernel, parts=parts, pair=pair, widt...  3.98 us
    pallas_call x1, Pallas kernels, feed(): pl.pallas_call(functools.partial(feed_kernel, tokens=len(inners), pieces=...  3.82 us
    pallas_call x1, Pallas kernels, outer(): pl.pallas_call(functools.partial(outer_kernel, tokens=len(tokens), atts=l...  3.67 us
  transfers between devices with their start and end apart: 43, of which 20 were waited for; matrix products, arithmetic and copies ran while one was open for 1% of the time, Pallas kernels for 17%

profile of v5, /device:TPU:0, one launch (start us, length us, event | category | flops | bytes accessed | tf_op | source)
XLA Modules:
  0.0 163.9 jit_solution(11625777119056067773)
XLA Ops:
  0.6 4.1 %collective-permute-start.3 = (bf16[1024,256]{1,0:T(8,128)(2,1)}, bf16[1024,256]{1,0:T(8,128)(2,1)S(1)}, u32[]{:S(2)}, u32[]{:S(2)}) collective-permute-start(bf16[1024,256]{1,0:T(8,128)(2,1)} %weight_ref.1), channel_id=1, source_target_pairs={{0,2},{1,3},{2,0},{3,1},{4,6},{5,7},{6,4},{7,5},{8,10},{9,11},{10,... | collective-permute-start | bytes 1572872 | tf_op jit(solution)/shard_map/w_out_2/ppermute | solution.py:20
  4.7 1.6 collective-permute-start.4
  6.9 4.0 %cut.1 = (bf16[128,2048]{1,0:T(8,128)(2,1)}, bf16[128,2048]{1,0:T(8,128)(2,1)}, bf16[128,2560]{1,0:T(8,128)(2,1)}, bf16[128,2048]{1,0:T(8,128)(2,1)}, bf16[1024,256]{1,0:T(8,128)(2,1)}) custom-call(s32[3]{0:T(128)} %pad_add_fusion.4.ranks_ref, bf16[128,8192]{1,0:T(8,128)(2,1)} %x_ref.1, bf16[512,128]{1,0:T(8,128)(2,1)} %key_ref.3, ...), custom_call_target="tpu_custom_call" | custom-call | tf_op jit(solution)/shard_map/cut/pallas_call | solution.py:70
  10.9 1.6 collective-permute-start.1
  12.5 1.5 collective-permute-start
  14.5 13.7 %collective-permute-done.3.refs_0_ = bf16[1024,256]{1,0:T(8,128)(2,1)S(1)} collective-permute-done((bf16[1024,256]{1,0:T(8,128)(2,1)}, bf16[1024,256]{1,0:T(8,128)(2,1)S(1)}, u32[]{:S(2)}, u32[]{:S(2)}) %collective-permute-start.3) | collective-permute-done | bytes 524320 | tf_op jit(solution)/shard_map/w_out_2/ppermute | solution.py:20
  28.5 1.5 collective-permute-start.5
  30.5 6.3 %collective-permute-done.2.refs_2_.refs_3_ = bf16[128,2048]{1,0:T(8,128)(2,1)S(1)} collective-permute-done((bf16[128,2048]{1,0:T(8,128)(2,1)}, bf16[128,2048]{1,0:T(8,128)(2,1)S(1)}, u32[]{:S(2)}, u32[]{:S(2)}) %collective-permute-start.2) | collective-permute-done | bytes 524320 | tf_op jit(solution)/shard_map/tokens_5/ppermute | solution.py:20
  36.8 1.5 collective-permute-done.1.refs_1_.refs_2_
  38.3 3.1 %collective-permute-done.5.refs_7_ = bf16[1024,256]{1,0:T(8,128)(2,1)} collective-permute-done((bf16[1024,256]{1,0:T(8,128)(2,1)S(1)}, bf16[1024,256]{1,0:T(8,128)(2,1)}, u32[]{:S(2)}, u32[]{:S(2)}) %collective-permute-start.5) | collective-permute-done | bytes 524320 | tf_op jit(solution)/shard_map/w_out_on_1/ppermute | solution.py:20
  41.4 3.0 %collective-permute-start.16 = (bf16[256,1024]{1,0:T(8,128)(2,1)}, bf16[256,1024]{1,0:T(8,128)(2,1)S(1)}, u32[]{:S(2)}, u32[]{:S(2)}) collective-permute-start(bf16[256,1024]{1,0:T(8,128)(2,1)} %refs_8_.2), channel_id=1, source_target_pairs={{0,2},{1,3},{2,0},{3,1},{4,6},{5,7},{6,4},{7,5},{8,10},{9,11},{10,... | collective-permute-start | bytes 1572872 | tf_op jit(solution)/shard_map/w_query_2/ppermute | solution.py:20
  45.3 1.7 %collective-permute-start.17 = (bf16[256,1024]{1,0:T(8,128)(2,1)}, bf16[256,1024]{1,0:T(8,128)(2,1)}, u32[]{:S(2)}, u32[]{:S(2)}) collective-permute-start(bf16[256,1024]{1,0:T(8,128)(2,1)} %refs_8_.2), channel_id=1, source_target_pairs={{0,1},{1,0},{2,3},{3,2},{4,5},{5,4},{6,7},{7,6},{8,9},{9,8},{10,11... | collective-permute-start | bytes 1572872 | tf_op jit(solution)/shard_map/w_query_1/ppermute | solution.py:20
  48.1 5.0 %project.1 = (f32[128,1024]{1,0:T(8,128)S(1)}, bf16[128,1024]{1,0:T(8,128)(2,1)}, bf16[128,1024]{1,0:T(8,128)(2,1)}, bf16[128,1024]{1,0:T(8,128)(2,1)}, bf16[256,256]{1,0:T(8,128)(2,1)S(1)}) custom-call(bf16[128,2048]{1,0:T(8,128)(2,1)S(1)} %copy-done, bf16[128,2048]{1,0:T(8,128)(2,1)S(1)} %collective-permute-done.refs_2_.refs_1_, ...), custom_call_target="tpu_custom_call" | custom-call | tf_op jit(solution)/shard_map/project/pallas_call | solution.py:119
  53.9 1.5 collective-permute-start.10
  55.4 1.5 collective-permute-start.11
  57.8 5.6 %collective-permute-done.10.refs_0_ = bf16[128,1024]{1,0:T(8,128)(2,1)} collective-permute-done((bf16[128,1024]{1,0:T(8,128)(2,1)}, bf16[128,1024]{1,0:T(8,128)(2,1)}, u32[]{:S(2)}, u32[]{:S(2)}) %collective-permute-start.10) | collective-permute-done | bytes 262176 | tf_op jit(solution)/shard_map/attn_4/ppermute | solution.py:20
  63.4 5.8 %collective-permute-done.11.refs_1_ = bf16[128,1024]{1,0:T(8,128)(2,1)} collective-permute-done((bf16[128,1024]{1,0:T(8,128)(2,1)}, bf16[128,1024]{1,0:T(8,128)(2,1)}, u32[]{:S(2)}, u32[]{:S(2)}) %collective-permute-start.11) | collective-permute-done | bytes 262176 | tf_op jit(solution)/shard_map/attn_1/ppermute | solution.py:20
  69.2 2.2 %add_up.1 = (bf16[128,256]{1,0:T(8,128)(2,1)}, bf16[128,256]{1,0:T(8,128)(2,1)}, bf16[128,256]{1,0:T(8,128)(2,1)}, bf16[128,256]{1,0:T(8,128)(2,1)}, bf16[128,25...) custom-call(s32[3]{0:T(128)} %pad_add_fusion.4.ranks_ref, ...), custom_call_target="tpu_custom_call" | custom-call | tf_op jit(solution)/shard_map/add_up/pallas_call | solution.py:166
  71.7 1.3 collective-permute-start.14
  73.1 2.8 %collective-permute-start.15 = (bf16[128,256]{1,0:T(8,128)(2,1)}, bf16[128,256]{1,0:T(8,128)(2,1)S(1)}, u32[]{:S(2)}, u32[]{:S(2)}) collective-permute-start(bf16[128,256]{1,0:T(8,128)(2,1)} %get-tuple-element.81), channel_id=1, source_target_pairs={{0,3},{1,2},{2,1},{3,0},{4,7},{5,6},{6,5},{7,4},{8,11},{9,10},{10,... | collective-permute-start | bytes 196616 | tf_op jit(solution)/shard_map/dout_3/ppermute | solution.py:20
  75.9 1.6 collective-permute-start.20
  77.5 2.3 %collective-permute-done.13.refs_0_ = bf16[128,256]{1,0:T(8,128)(2,1)S(1)} collective-permute-done((bf16[128,256]{1,0:T(8,128)(2,1)}, bf16[128,256]{1,0:T(8,128)(2,1)S(1)}, u32[]{:S(2)}, u32[]{:S(2)}) %collective-permute-start.13) | collective-permute-done | bytes 65568 | tf_op jit(solution)/shard_map/dout_2/ppermute | solution.py:20
  81.0 3.0 %attention.1 = (bf16[128,256]{1,0:T(8,128)(2,1)S(1)}, bf16[128,256]{1,0:T(8,128)(2,1)S(1)}, bf16[128,256]{1,0:T(8,128)(2,1)S(1)}, bf16[128,256]{1,0:T(8,128)(2,1...) custom-call(s32[3]{0:T(128)S(1)} %copy-done.12, s32[512,1]{1,0:T(8,128)S(1)} %copy.44.seg_query_ref, ...), custom_call_target="tpu_custom_call" | custom-call | tf_op jit(solution)/shard_map/attention/pallas_call | solution.py:488
  84.1 1.5 collective-permute-start.18
  85.5 2.4 %collective-permute-start.22 = (bf16[128,256]{1,0:T(8,128)(2,1)S(1)}, bf16[128,256]{1,0:T(8,128)(2,1)S(1)}, u32[]{:S(2)}, u32[]{:S(2)}) collective-permute-start(bf16[128,256]{1,0:T(8,128)(2,1)S(1)} %get-tuple-element.97), channel_id=1, source_target_pairs={{0,2},{1,3},{2,0},{3,1},{4,6},{5,7},{6,4},{7,5},{8,10},{9,11},{10,... | collective-permute-start | bytes 196616 | tf_op jit(solution)/shard_map/dquery_2/ppermute | solution.py:20
  88.8 1.7 %collective-permute-start.24 = (bf16[128,256]{1,0:T(8,128)(2,1)S(1)}, bf16[128,256]{1,0:T(8,128)(2,1)S(1)}, u32[]{:S(2)}, u32[]{:S(2)}) collective-permute-start(bf16[128,256]{1,0:T(8,128)(2,1)S(1)} %get-tuple-element.99), channel_id=1, source_target_pairs={{0,3},{1,2},{2,1},{3,0},{4,7},{5,6},{6,5},{7,4},{8,11},{9,10},{10,... | collective-permute-start | bytes 196616 | tf_op jit(solution)/shard_map/dquery_3/ppermute | solution.py:20
  90.7 1.5 collective-permute-done.23.refs_6_.refs_2_
  92.3 3.2 %collective-permute-done.24.refs_7_.refs_3_ = bf16[128,256]{1,0:T(8,128)(2,1)S(1)} collective-permute-done((bf16[128,256]{1,0:T(8,128)(2,1)S(1)}, bf16[128,256]{1,0:T(8,128)(2,1)S(1)}, u32[]{:S(2)}, u32[]{:S(2)}) %collective-permute-start.24) | collective-permute-done | bytes 65568 | tf_op jit(solution)/shard_map/dquery_3/ppermute | solution.py:20
  96.1 1.7 %collective-permute-start.25 = (bf16[256,256]{1,0:T(8,128)(2,1)S(1)}, bf16[256,256]{1,0:T(8,128)(2,1)S(1)}, u32[]{:S(2)}, u32[]{:S(2)}) collective-permute-start(bf16[256,256]{1,0:T(8,128)(2,1)S(1)} %get-tuple-element.101), channel_id=1, source_target_pairs={{0,2},{1,3},{2,0},{3,1},{4,6},{5,7},{6,4},{7,5},{8,10},{9,11},{10,... | collective-permute-start | bytes 393224 | tf_op jit(solution)/shard_map/kv_2/ppermute | solution.py:20
  98.9 1.4 collective-permute-start.32
  101.3 2.2 %collective-permute-done.25.got_ref = bf16[256,256]{1,0:T(8,128)(2,1)S(1)} collective-permute-done((bf16[256,256]{1,0:T(8,128)(2,1)S(1)}, bf16[256,256]{1,0:T(8,128)(2,1)S(1)}, u32[]{:S(2)}, u32[]{:S(2)}) %collective-permute-start.25) | collective-permute-done | bytes 131104 | tf_op jit(solution)/shard_map/kv_2/ppermute | solution.py:20
  104.0 4.7 %collective-permute-done.26.next_ref = bf16[128,256]{1,0:T(8,128)(2,1)S(1)} collective-permute-done((bf16[128,256]{1,0:T(8,128)(2,1)S(1)}, bf16[128,256]{1,0:T(8,128)(2,1)S(1)}, u32[]{:S(2)}, u32[]{:S(2)}) %collective-permute-start.26) | collective-permute-done | bytes 65568 | tf_op jit(solution)/shard_map/kv_1/ppermute | solution.py:20
  109.4 1.5 collective-permute-start.28
  110.8 1.8 %collective-permute-start.29 = (bf16[128,1280]{1,0:T(8,128)(2,1)S(1)}, bf16[128,1280]{1,0:T(8,128)(2,1)S(1)}, u32[]{:S(2)}, u32[]{:S(2)}) collective-permute-start(bf16[128,1280]{1,0:T(8,128)(2,1)S(1)} %get-tuple-element.104.refs_11_.refs_0_), channel_id=1, source_target_pairs={{0,20},{4,16},{8,28},{12,24},{16,4},{20,0},{24,12},{28,8},{1,21},{... | collective-permute-start | bytes 983048 | tf_op jit(solution)/shard_map/inner_5/ppermute | solution.py:20
  112.6 3.7 %outer.1 = (f32[1024,256]{1,0:T(8,128)S(1)}, f32[1024,256]{1,0:T(8,128)S(1)}, f32[1024,256]{1,0:T(8,128)S(1)}, f32[1024,256]{1,0:T(8,128)S(1)}, bf16[1024,1024]{...) custom-call(bf16[128,2048]{1,0:T(8,128)(2,1)S(1)} %copy-done, bf16[128,2048]{1,0:T(8,128)(2,1)S(1)} %collective-permute-done.refs_2_.refs_1_, ...), custom_call_target="tpu_custom_call" | custom-call | tf_op jit(solution)/shard_map/outer/pallas_call | solution.py:275
  117.6 4.5 %collective-permute-done.28.refs_1_ = bf16[128,1280]{1,0:T(8,128)(2,1)S(1)} collective-permute-done((bf16[128,1280]{1,0:T(8,128)(2,1)S(1)}, bf16[128,1280]{1,0:T(8,128)(2,1)S(1)}, u32[]{:S(2)}, u32[]{:S(2)}) %collective-permute-start.28) | collective-permute-done | bytes 327712 | tf_op jit(solution)/shard_map/inner_1/ppermute | solution.py:20
  124.8 3.8 %feed.1 = (bf16[128,2048]{1,0:T(8,128)(2,1)S(1)}, bf16[128,2048]{1,0:T(8,128)(2,1)S(1)}, bf16[128,2048]{1,0:T(8,128)(2,1)S(1)}, bf16[128,2048]{1,0:T(8,128)(2,1)S(1)}) custom-call(s32[3]{0:T(128)S(1)} %copy-done.12, bf16[128,1280]{1,0:T(8,128)(2,1)S(1)} %get-tuple-element.104.refs_11_.refs_0_, bf16[128,1280]{1,0:T(8,128)(2,1)S(1)} %get-tuple-element.115.refs_1_, ...), custom_call_target="tpu_custom_call" | custom-call | tf_op jit(solution)/shard_map/feed/pallas_call | solution.py:358
  128.7 1.4 collective-permute-start.39
  130.8 1.4 collective-permute-start.37
  132.2 1.8 %collective-permute-start.40 = (bf16[1024,256]{1,0:T(8,128)(2,1)S(1)}, bf16[1024,256]{1,0:T(8,128)(2,1)S(1)}, u32[]{:S(2)}, u32[]{:S(2)}) collective-permute-start(bf16[1024,256]{1,0:T(8,128)(2,1)S(1)} %add_pair.5.refs_11_), channel_id=1, source_target_pairs={{0,1},{1,0},{2,3},{3,2},{4,5},{5,4},{6,7},{7,6},{8,9},{9,8},{10,11... | collective-permute-start | bytes 1572872 | tf_op jit(solution)/shard_map/out_proj_1/ppermute | solution.py:20
  134.0 3.1 %collective-permute-done.41.refs_2_ = bf16[1024,256]{1,0:T(8,128)(2,1)S(1)} collective-permute-done((bf16[1024,256]{1,0:T(8,128)(2,1)S(1)}, bf16[1024,256]{1,0:T(8,128)(2,1)S(1)}, u32[]{:S(2)}, u32[]{:S(2)}) %collective-permute-start.41) | collective-permute-done | bytes 524320 | tf_op jit(solution)/shard_map/out_proj_3_1/ppermute | solution.py:20
  138.1 1.3 place.4.refs_1_
  139.5 4.0 %collective-permute-done.39.refs_0_ = bf16[128,2048]{1,0:T(8,128)(2,1)S(1)} collective-permute-done((bf16[128,2048]{1,0:T(8,128)(2,1)S(1)}, bf16[128,2048]{1,0:T(8,128)(2,1)S(1)}, u32[]{:S(2)}, u32[]{:S(2)}) %collective-permute-start.39) | collective-permute-done | bytes 524320 | tf_op jit(solution)/shard_map/grads_4/ppermute | solution.py:20
  143.5 1.4 place.5.refs_1_
  144.8 10.3 %collective-permute-done.38.refs_0_ = bf16[128,2048]{1,0:T(8,128)(2,1)S(1)} collective-permute-done((bf16[128,2048]{1,0:T(8,128)(2,1)S(1)}, bf16[128,2048]{1,0:T(8,128)(2,1)S(1)}, u32[]{:S(2)}, u32[]{:S(2)}) %collective-permute-start.38) | collective-permute-done | bytes 524320 | tf_op jit(solution)/shard_map/grads_1/ppermute | solution.py:20
  155.1 1.4 place.6.refs_1_
  156.5 1.4 place.7.refs_0_
  157.9 4.8 %collective-permute-done.42.refs_3_ = bf16[1024,256]{1,0:T(8,128)(2,1)S(1)} collective-permute-done((bf16[1024,256]{1,0:T(8,128)(2,1)S(1)}, bf16[1024,256]{1,0:T(8,128)(2,1)S(1)}, u32[]{:S(2)}, u32[]{:S(2)}) %collective-permute-start.42) | collective-permute-done | bytes 524320 | tf_op jit(solution)/shard_map/out_proj_2/ppermute | solution.py:20
  (107 shorter events, 18.8 us)
Async XLA Ops:
  0.6 27.6 %collective-permute-start.3 = (bf16[1024,256]{1,0:T(8,128)(2,1)}, bf16[1024,256]{1,0:T(8,128)(2,1)S(1)}, u32[]{:S(2)}, u32[]{:S(2)}) collective-permute-start(bf16[1024,256]{1,0:T(8,128)(2,1)} %weight_ref.1), channel_id=1, source_target_pairs={{0,2},{1,3},{2,0},{3,1},{4,6},{5,7},{6,4},{7,5},{8,10},{9,11},{10,... | collective-permute-start | bytes 1572872 | tf_op jit(solution)/shard_map/w_out_2/ppermute | solution.py:20
  4.7 23.8 %collective-permute-start.4 = (bf16[1024,256]{1,0:T(8,128)(2,1)}, bf16[1024,256]{1,0:T(8,128)(2,1)}, u32[]{:S(2)}, u32[]{:S(2)}) collective-permute-start(bf16[1024,256]{1,0:T(8,128)(2,1)} %weight_ref.1), channel_id=1, source_target_pairs={{0,1},{1,0},{2,3},{3,2},{4,5},{5,4},{6,7},{7,6},{8,9},{9,8},{10,11... | collective-permute-start | bytes 1572872 | tf_op jit(solution)/shard_map/w_out_1/ppermute | solution.py:20
  10.9 27.4 %collective-permute-start.1 = (bf16[128,2560]{1,0:T(8,128)(2,1)}, bf16[128,2560]{1,0:T(8,128)(2,1)S(1)}, u32[]{:S(2)}, u32[]{:S(2)}) collective-permute-start(bf16[128,2560]{1,0:T(8,128)(2,1)} %get-tuple-element.67), channel_id=1, source_target_pairs={{0,4},{4,0},{8,12},{12,8},{16,20},{20,16},{24,28},{28,24},{1,5},{5... | collective-permute-start | bytes 1966088 | tf_op jit(solution)/shard_map/tokens_1/ppermute | solution.py:20
  12.5 16.0 %collective-permute-start = (bf16[128,2048]{1,0:T(8,128)(2,1)}, bf16[128,2048]{1,0:T(8,128)(2,1)S(1)}, u32[]{:S(2)}, u32[]{:S(2)}) collective-permute-start(bf16[128,2048]{1,0:T(8,128)(2,1)} %get-tuple-element.66), channel_id=1, source_target_pairs={{0,16},{4,20},{8,24},{12,28},{16,0},{20,4},{24,8},{28,12},{1,17},{... | collective-permute-start | bytes 1572872 | tf_op jit(solution)/shard_map/tokens_4/ppermute | solution.py:20
  14.0 22.8 %collective-permute-start.2 = (bf16[128,2048]{1,0:T(8,128)(2,1)}, bf16[128,2048]{1,0:T(8,128)(2,1)S(1)}, u32[]{:S(2)}, u32[]{:S(2)}) collective-permute-start(bf16[128,2048]{1,0:T(8,128)(2,1)} %get-tuple-element.68), channel_id=1, source_target_pairs={{0,20},{4,16},{8,28},{12,24},{16,4},{20,0},{24,12},{28,8},{1,21},{... | collective-permute-start | bytes 1572872 | tf_op jit(solution)/shard_map/tokens_5/ppermute | solution.py:20
  28.5 12.9 %collective-permute-start.5 = (bf16[1024,256]{1,0:T(8,128)(2,1)S(1)}, bf16[1024,256]{1,0:T(8,128)(2,1)}, u32[]{:S(2)}, u32[]{:S(2)}) collective-permute-start(bf16[1024,256]{1,0:T(8,128)(2,1)S(1)} %get-tuple-element.72.refs_5_), channel_id=1, source_target_pairs={{0,1},{1,0},{2,3},{3,2},{4,5},{5,4},{6,7},{7,6},{8,9},{9,8},{10,11... | collective-permute-start | bytes 1572872 | tf_op jit(solution)/shard_map/w_out_on_1/ppermute | solution.py:20
  30.0 14.5 %collective-permute-start.7 = (bf16[1024,256]{1,0:T(8,128)(2,1)S(1)}, bf16[1024,256]{1,0:T(8,128)(2,1)S(1)}, u32[]{:S(2)}, u32[]{:S(2)}) collective-permute-start(bf16[1024,256]{1,0:T(8,128)(2,1)S(1)} %get-tuple-element.72.refs_5_), channel_id=1, source_target_pairs={{0,8},{4,12},{8,0},{12,4},{16,24},{20,28},{24,16},{28,20},{1,9},{5... | collective-permute-start | bytes 1572872 | tf_op jit(solution)/shard_map/w_out_pair_1/ppermute | solution.py:20
  30.0 17.0 %collective-permute-start.6 = (bf16[1024,256]{1,0:T(8,128)(2,1)}, bf16[1024,256]{1,0:T(8,128)(2,1)}, u32[]{:S(2)}, u32[]{:S(2)}) collective-permute-start(bf16[1024,256]{1,0:T(8,128)(2,1)} %get-tuple-element.71.refs_4_), channel_id=1, source_target_pairs={{0,8},{4,12},{8,0},{12,4},{16,24},{20,28},{24,16},{28,20},{1,9},{5... | collective-permute-start | bytes 1572872 | tf_op jit(solution)/shard_map/w_out_pair_0/ppermute | solution.py:20
  38.3 8.7 %copy-start = (bf16[128,2048]{1,0:T(8,128)(2,1)S(1)}, bf16[128,2048]{1,0:T(8,128)(2,1)}, u32[]{:S(2)}) copy-start(bf16[128,2048]{1,0:T(8,128)(2,1)} %get-tuple-element.65.refs_0_) | copy-start | bytes 1572868
  38.3 8.7 %collective-permute-start.8 = (bf16[1024,256]{1,0:T(8,128)(2,1)}, bf16[1024,256]{1,0:T(8,128)(2,1)}, u32[]{:S(2)}, u32[]{:S(2)}) collective-permute-start(bf16[1024,256]{1,0:T(8,128)(2,1)} %hand_on.12.refs_6_), channel_id=1, source_target_pairs={{0,8},{4,12},{8,0},{12,4},{16,24},{20,28},{24,16},{28,20},{1,9},{5... | collective-permute-start | bytes 1572872 | tf_op jit(solution)/shard_map/w_out_pair_2/ppermute | solution.py:20
  41.4 5.6 %collective-permute-start.9 = (bf16[1024,256]{1,0:T(8,128)(2,1)}, bf16[1024,256]{1,0:T(8,128)(2,1)}, u32[]{:S(2)}, u32[]{:S(2)}) collective-permute-start(bf16[1024,256]{1,0:T(8,128)(2,1)} %collective-permute-done.5.refs_7_), channel_id=1, source_target_pairs={{0,8},{4,12},{8,0},{12,4},{16,24},{20,28},{24,16},{28,20},{1,9},{5... | collective-permute-start | bytes 1572872 | tf_op jit(solution)/shard_map/w_out_pair_3/ppermute | solution.py:20
  41.4 34.4 %collective-permute-start.16 = (bf16[256,1024]{1,0:T(8,128)(2,1)}, bf16[256,1024]{1,0:T(8,128)(2,1)S(1)}, u32[]{:S(2)}, u32[]{:S(2)}) collective-permute-start(bf16[256,1024]{1,0:T(8,128)(2,1)} %refs_8_.2), channel_id=1, source_target_pairs={{0,2},{1,3},{2,0},{3,1},{4,6},{5,7},{6,4},{7,5},{8,10},{9,11},{10,... | collective-permute-start | bytes 1572872 | tf_op jit(solution)/shard_map/w_query_2/ppermute | solution.py:20
  45.3 30.5 %collective-permute-start.17 = (bf16[256,1024]{1,0:T(8,128)(2,1)}, bf16[256,1024]{1,0:T(8,128)(2,1)}, u32[]{:S(2)}, u32[]{:S(2)}) collective-permute-start(bf16[256,1024]{1,0:T(8,128)(2,1)} %refs_8_.2), channel_id=1, source_target_pairs={{0,1},{1,0},{2,3},{3,2},{4,5},{5,4},{6,7},{7,6},{8,9},{9,8},{10,11... | collective-permute-start | bytes 1572872 | tf_op jit(solution)/shard_map/w_query_1/ppermute | solution.py:20
  48.1 9.3 %copy-start.14 = (s32[1,1024]{1,0:T(1,128)S(1)}, s32[1,1024]{1,0:T(1,128)}, u32[]{:S(2)}) copy-start(s32[1,1024]{1,0:T(1,128)} %param.17) | copy-start | bytes 12292
  48.1 9.5 %copy-start.13 = (f32[2,512]{1,0:T(2,128)S(1)}, f32[2,512]{1,0:T(2,128)}, u32[]{:S(2)}) copy-start(f32[2,512]{1,0:T(2,128)} %param.16) | copy-start | bytes 12292
  53.9 9.5 %collective-permute-start.10 = (bf16[128,1024]{1,0:T(8,128)(2,1)}, bf16[128,1024]{1,0:T(8,128)(2,1)}, u32[]{:S(2)}, u32[]{:S(2)}) collective-permute-start(bf16[128,1024]{1,0:T(8,128)(2,1)} %get-tuple-element.75), channel_id=1, source_target_pairs={{0,16},{4,20},{8,24},{12,28},{16,0},{20,4},{24,8},{28,12},{1,17},{... | collective-permute-start | bytes 786440 | tf_op jit(solution)/shard_map/attn_4/ppermute | solution.py:20
  55.4 13.8 %collective-permute-start.11 = (bf16[128,1024]{1,0:T(8,128)(2,1)}, bf16[128,1024]{1,0:T(8,128)(2,1)}, u32[]{:S(2)}, u32[]{:S(2)}) collective-permute-start(bf16[128,1024]{1,0:T(8,128)(2,1)} %get-tuple-element.76), channel_id=1, source_target_pairs={{0,4},{4,0},{8,12},{12,8},{16,20},{20,16},{24,28},{28,24},{1,5},{5... | collective-permute-start | bytes 786440 | tf_op jit(solution)/shard_map/attn_1/ppermute | solution.py:20
  56.9 12.3 %collective-permute-start.12 = (bf16[128,1024]{1,0:T(8,128)(2,1)}, bf16[128,1024]{1,0:T(8,128)(2,1)}, u32[]{:S(2)}, u32[]{:S(2)}) collective-permute-start(bf16[128,1024]{1,0:T(8,128)(2,1)} %get-tuple-element.77), channel_id=1, source_target_pairs={{0,20},{4,16},{8,28},{12,24},{16,4},{20,0},{24,12},{28,8},{1,21},{... | collective-permute-start | bytes 786440 | tf_op jit(solution)/shard_map/attn_5/ppermute | solution.py:20
  71.4 8.5 %collective-permute-start.13 = (bf16[128,256]{1,0:T(8,128)(2,1)}, bf16[128,256]{1,0:T(8,128)(2,1)S(1)}, u32[]{:S(2)}, u32[]{:S(2)}) collective-permute-start(bf16[128,256]{1,0:T(8,128)(2,1)} %get-tuple-element.79), channel_id=1, source_target_pairs={{0,2},{1,3},{2,0},{3,1},{4,6},{5,7},{6,4},{7,5},{8,10},{9,11},{10,... | collective-permute-start | bytes 196616 | tf_op jit(solution)/shard_map/dout_2/ppermute | solution.py:20
  71.7 8.7 %collective-permute-start.14 = (bf16[128,256]{1,0:T(8,128)(2,1)}, bf16[128,256]{1,0:T(8,128)(2,1)S(1)}, u32[]{:S(2)}, u32[]{:S(2)}) collective-permute-start(bf16[128,256]{1,0:T(8,128)(2,1)} %get-tuple-element.80), channel_id=1, source_target_pairs={{0,1},{1,0},{2,3},{3,2},{4,5},{5,4},{6,7},{7,6},{8,9},{9,8},{10,11... | collective-permute-start | bytes 196616 | tf_op jit(solution)/shard_map/dout_1/ppermute | solution.py:20
  73.1 6.8 %copy-start.15 = (bf16[128,256]{1,0:T(8,128)(2,1)S(1)}, bf16[128,256]{1,0:T(8,128)(2,1)}, u32[]{:S(2)}) copy-start(bf16[128,256]{1,0:T(8,128)(2,1)} %get-tuple-element.93) | copy-start | bytes 196612
  73.1 7.4 %collective-permute-start.15 = (bf16[128,256]{1,0:T(8,128)(2,1)}, bf16[128,256]{1,0:T(8,128)(2,1)S(1)}, u32[]{:S(2)}, u32[]{:S(2)}) collective-permute-start(bf16[128,256]{1,0:T(8,128)(2,1)} %get-tuple-element.81), channel_id=1, source_target_pairs={{0,3},{1,2},{2,1},{3,0},{4,7},{5,6},{6,5},{7,4},{8,11},{9,10},{10,... | collective-permute-start | bytes 196616 | tf_op jit(solution)/shard_map/dout_3/ppermute | solution.py:20
  75.8 12.1 %collective-permute-start.19 = (bf16[128,256]{1,0:T(8,128)(2,1)S(1)}, bf16[128,256]{1,0:T(8,128)(2,1)S(1)}, u32[]{:S(2)}, u32[]{:S(2)}) collective-permute-start(bf16[128,256]{1,0:T(8,128)(2,1)S(1)} %copy-done.17), channel_id=1, source_target_pairs={{0,2},{1,3},{2,0},{3,1},{4,6},{5,7},{6,4},{7,5},{8,10},{9,11},{10,... | collective-permute-start | bytes 196616 | tf_op jit(solution)/shard_map/attended_2/ppermute | solution.py:20
  75.9 12.9 %collective-permute-start.20 = (bf16[128,256]{1,0:T(8,128)(2,1)S(1)}, bf16[128,256]{1,0:T(8,128)(2,1)S(1)}, u32[]{:S(2)}, u32[]{:S(2)}) collective-permute-start(bf16[128,256]{1,0:T(8,128)(2,1)S(1)} %copy-done.16), channel_id=1, source_target_pairs={{0,1},{1,0},{2,3},{3,2},{4,5},{5,4},{6,7},{7,6},{8,9},{9,8},{10,11... | collective-permute-start | bytes 196616 | tf_op jit(solution)/shard_map/attended_1/ppermute | solution.py:20
  79.9 10.6 %collective-permute-start.21 = (bf16[128,256]{1,0:T(8,128)(2,1)S(1)}, bf16[128,256]{1,0:T(8,128)(2,1)S(1)}, u32[]{:S(2)}, u32[]{:S(2)}) collective-permute-start(bf16[128,256]{1,0:T(8,128)(2,1)S(1)} %copy-done.15), channel_id=1, source_target_pairs={{0,3},{1,2},{2,1},{3,0},{4,7},{5,6},{6,5},{7,4},{8,11},{9,10},{10,... | collective-permute-start | bytes 196616 | tf_op jit(solution)/shard_map/attended_3/ppermute | solution.py:20
  84.1 11.4 %collective-permute-start.18 = (bf16[256,256]{1,0:T(8,128)(2,1)S(1)}, bf16[256,256]{1,0:T(8,128)(2,1)S(1)}, u32[]{:S(2)}, u32[]{:S(2)}) collective-permute-start(bf16[256,256]{1,0:T(8,128)(2,1)S(1)} %get-tuple-element.89), channel_id=1, source_target_pairs={{0,4},{4,0},{1,5},{5,1},{2,6},{6,2},{3,7},{7,3},{8,12},{12,8},{9,1... | collective-permute-start | bytes 393224 | tf_op jit(solution)/shard_map/kv_back/ppermute | solution.py:20
  85.5 5.2 %collective-permute-start.22 = (bf16[128,256]{1,0:T(8,128)(2,1)S(1)}, bf16[128,256]{1,0:T(8,128)(2,1)S(1)}, u32[]{:S(2)}, u32[]{:S(2)}) collective-permute-start(bf16[128,256]{1,0:T(8,128)(2,1)S(1)} %get-tuple-element.97), channel_id=1, source_target_pairs={{0,2},{1,3},{2,0},{3,1},{4,6},{5,7},{6,4},{7,5},{8,10},{9,11},{10,... | collective-permute-start | bytes 196616 | tf_op jit(solution)/shard_map/dquery_2/ppermute | solution.py:20
  88.0 4.3 %collective-permute-start.23 = (bf16[128,256]{1,0:T(8,128)(2,1)S(1)}, bf16[128,256]{1,0:T(8,128)(2,1)S(1)}, u32[]{:S(2)}, u32[]{:S(2)}) collective-permute-start(bf16[128,256]{1,0:T(8,128)(2,1)S(1)} %get-tuple-element.98), channel_id=1, source_target_pairs={{0,1},{1,0},{2,3},{3,2},{4,5},{5,4},{6,7},{7,6},{8,9},{9,8},{10,11... | collective-permute-start | bytes 196616 | tf_op jit(solution)/shard_map/dquery_1/ppermute | solution.py:20
  88.8 6.7 %copy-start.10 = (bf16[128,256]{1,0:T(8,128)(2,1)S(1)}, bf16[128,256]{1,0:T(8,128)(2,1)}, u32[]{:S(2)}) copy-start(bf16[128,256]{1,0:T(8,128)(2,1)} %get-tuple-element.90.refs_1_) | copy-start | bytes 196612
  88.8 6.6 %collective-permute-start.24 = (bf16[128,256]{1,0:T(8,128)(2,1)S(1)}, bf16[128,256]{1,0:T(8,128)(2,1)S(1)}, u32[]{:S(2)}, u32[]{:S(2)}) collective-permute-start(bf16[128,256]{1,0:T(8,128)(2,1)S(1)} %get-tuple-element.99), channel_id=1, source_target_pairs={{0,3},{1,2},{2,1},{3,0},{4,7},{5,6},{6,5},{7,4},{8,11},{9,10},{10,... | collective-permute-start | bytes 196616 | tf_op jit(solution)/shard_map/dquery_3/ppermute | solution.py:20
  96.1 7.4 %collective-permute-start.25 = (bf16[256,256]{1,0:T(8,128)(2,1)S(1)}, bf16[256,256]{1,0:T(8,128)(2,1)S(1)}, u32[]{:S(2)}, u32[]{:S(2)}) collective-permute-start(bf16[256,256]{1,0:T(8,128)(2,1)S(1)} %get-tuple-element.101), channel_id=1, source_target_pairs={{0,2},{1,3},{2,0},{3,1},{4,6},{5,7},{6,4},{7,5},{8,10},{9,11},{10,... | collective-permute-start | bytes 393224 | tf_op jit(solution)/shard_map/kv_2/ppermute | solution.py:20
  97.8 11.5 %collective-permute-start.31 = (bf16[128,1024]{1,0:T(8,128)(2,1)S(1)}, bf16[128,1024]{1,0:T(8,128)(2,1)S(1)}, u32[]{:S(2)}, u32[]{:S(2)}) collective-permute-start(bf16[128,1024]{1,0:T(8,128)(2,1)S(1)} %get-tuple-element.110.refs_4_), channel_id=1, source_target_pairs={{0,16},{4,20},{8,24},{12,28},{16,0},{20,4},{24,8},{28,12},{1,17},{... | collective-permute-start | bytes 786440 | tf_op jit(solution)/shard_map/attended_4/ppermute | solution.py:20
  98.9 12.0 %collective-permute-start.32 = (bf16[128,1024]{1,0:T(8,128)(2,1)S(1)}, bf16[128,1024]{1,0:T(8,128)(2,1)S(1)}, u32[]{:S(2)}, u32[]{:S(2)}) collective-permute-start(bf16[128,1024]{1,0:T(8,128)(2,1)S(1)} %get-tuple-element.110.refs_4_), channel_id=1, source_target_pairs={{0,4},{4,0},{8,12},{12,8},{16,20},{20,16},{24,28},{28,24},{1,5},{5... | collective-permute-start | bytes 786440 | tf_op jit(solution)/shard_map/attended_1/ppermute | solution.py:20
  100.3 12.3 %collective-permute-start.33 = (bf16[128,1024]{1,0:T(8,128)(2,1)S(1)}, bf16[128,1024]{1,0:T(8,128)(2,1)S(1)}, u32[]{:S(2)}, u32[]{:S(2)}) collective-permute-start(bf16[128,1024]{1,0:T(8,128)(2,1)S(1)} %get-tuple-element.110.refs_4_), channel_id=1, source_target_pairs={{0,20},{4,16},{8,28},{12,24},{16,4},{20,0},{24,12},{28,8},{1,21},{... | collective-permute-start | bytes 786440 | tf_op jit(solution)/shard_map/attended_5/ppermute | solution.py:20
  103.6 5.1 %collective-permute-start.26 = (bf16[128,256]{1,0:T(8,128)(2,1)S(1)}, bf16[128,256]{1,0:T(8,128)(2,1)S(1)}, u32[]{:S(2)}, u32[]{:S(2)}) collective-permute-start(bf16[128,256]{1,0:T(8,128)(2,1)S(1)} %add_convert_fusion), channel_id=1, source_target_pairs={{0,1},{1,0},{2,3},{3,2},{4,5},{5,4},{6,7},{7,6},{8,9},{9,8},{10,11... | collective-permute-start | bytes 196616 | tf_op jit(solution)/shard_map/kv_1/ppermute | solution.py:20
  108.7 13.4 %collective-permute-start.30 = (bf16[256,1024]{1,0:T(8,128)(2,1)S(1)}, bf16[256,1024]{1,0:T(8,128)(2,1)S(1)}, u32[]{:S(2)}, u32[]{:S(2)}) collective-permute-start(bf16[256,1024]{1,0:T(8,128)(2,1)S(1)} %get-tuple-element.105.refs_9_), channel_id=1, source_target_pairs={{0,1},{1,0},{2,3},{3,2},{4,5},{5,4},{6,7},{7,6},{8,9},{9,8},{10,11... | collective-permute-start | bytes 1572872 | tf_op jit(solution)/shard_map/w_query_on_1/ppermute | solution.py:20
  109.1 8.5 %collective-permute-start.27 = (bf16[128,1280]{1,0:T(8,128)(2,1)S(1)}, bf16[128,1280]{1,0:T(8,128)(2,1)S(1)}, u32[]{:S(2)}, u32[]{:S(2)}) collective-permute-start(bf16[128,1280]{1,0:T(8,128)(2,1)S(1)} %get-tuple-element.104.refs_11_.refs_0_), channel_id=1, source_target_pairs={{0,16},{4,20},{8,24},{12,28},{16,0},{20,4},{24,8},{28,12},{1,17},{... | collective-permute-start | bytes 983048 | tf_op jit(solution)/shard_map/inner_4/ppermute | solution.py:20
  109.4 12.7 %collective-permute-start.28 = (bf16[128,1280]{1,0:T(8,128)(2,1)S(1)}, bf16[128,1280]{1,0:T(8,128)(2,1)S(1)}, u32[]{:S(2)}, u32[]{:S(2)}) collective-permute-start(bf16[128,1280]{1,0:T(8,128)(2,1)S(1)} %get-tuple-element.104.refs_11_.refs_0_), channel_id=1, source_target_pairs={{0,4},{4,0},{8,12},{12,8},{16,20},{20,16},{24,28},{28,24},{1,5},{5... | collective-permute-start | bytes 983048 | tf_op jit(solution)/shard_map/inner_1/ppermute | solution.py:20
  110.8 11.3 %collective-permute-start.29 = (bf16[128,1280]{1,0:T(8,128)(2,1)S(1)}, bf16[128,1280]{1,0:T(8,128)(2,1)S(1)}, u32[]{:S(2)}, u32[]{:S(2)}) collective-permute-start(bf16[128,1280]{1,0:T(8,128)(2,1)S(1)} %get-tuple-element.104.refs_11_.refs_0_), channel_id=1, source_target_pairs={{0,20},{4,16},{8,28},{12,24},{16,4},{20,0},{24,12},{28,8},{1,21},{... | collective-permute-start | bytes 983048 | tf_op jit(solution)/shard_map/inner_5/ppermute | solution.py:20
  116.3 5.8 %collective-permute-start.34 = (bf16[1024,1024]{1,0:T(8,128)(2,1)S(1)}, bf16[1024,1024]{1,0:T(8,128)(2,1)S(1)}, u32[]{:S(2)}, u32[]{:S(2)}) collective-permute-start(bf16[1024,1024]{1,0:T(8,128)(2,1)S(1)} %get-tuple-element.114), channel_id=1, source_target_pairs={{0,8},{4,12},{8,0},{12,4},{16,24},{20,28},{24,16},{28,20},{1,9},{5... | collective-permute-start | bytes 6291464 | tf_op jit(solution)/shard_map/out_proj_pair/ppermute | solution.py:20
  117.6 5.2 %collective-permute-start.35 = (bf16[768,1024]{1,0:T(8,128)(2,1)S(1)}, bf16[768,1024]{1,0:T(8,128)(2,1)S(1)}, u32[]{:S(2)}, u32[]{:S(2)}) collective-permute-start(bf16[768,1024]{1,0:T(8,128)(2,1)S(1)} %get-tuple-element.118.refs_4_), channel_id=1, source_target_pairs={{0,8},{4,12},{8,0},{12,4},{16,24},{20,28},{24,16},{28,20},{1,9},{5... | collective-permute-start | bytes 4718600 | tf_op jit(solution)/shard_map/w_query_pair_0/ppermute | solution.py:20
  122.1 2.0 %collective-permute-start.36 = (bf16[256,1024]{1,0:T(8,128)(2,1)S(1)}, bf16[256,1024]{1,0:T(8,128)(2,1)S(1)}, u32[]{:S(2)}, u32[]{:S(2)}) collective-permute-start(bf16[256,1024]{1,0:T(8,128)(2,1)S(1)} %get-tuple-element.119.refs_5_), channel_id=1, source_target_pairs={{0,8},{4,12},{8,0},{12,4},{16,24},{20,28},{24,16},{28,20},{1,9},{5... | collective-permute-start | bytes 1572872 | tf_op jit(solution)/shard_map/w_query_pair_1/ppermute | solution.py:20
  122.3 14.8 %collective-permute-start.41 = (bf16[1024,256]{1,0:T(8,128)(2,1)S(1)}, bf16[1024,256]{1,0:T(8,128)(2,1)S(1)}, u32[]{:S(2)}, u32[]{:S(2)}) collective-permute-start(bf16[1024,256]{1,0:T(8,128)(2,1)S(1)} %add_pair.4.refs_2_.refs_10_), channel_id=1, source_target_pairs={{0,1},{1,0},{2,3},{3,2},{4,5},{5,4},{6,7},{7,6},{8,9},{9,8},{10,11... | collective-permute-start | bytes 1572872 | tf_op jit(solution)/shard_map/out_proj_3_1/ppermute | solution.py:20
  128.7 14.8 %collective-permute-start.39 = (bf16[128,2048]{1,0:T(8,128)(2,1)S(1)}, bf16[128,2048]{1,0:T(8,128)(2,1)S(1)}, u32[]{:S(2)}, u32[]{:S(2)}) collective-permute-start(bf16[128,2048]{1,0:T(8,128)(2,1)S(1)} %get-tuple-element.124.refs_3_), channel_id=1, source_target_pairs={{0,16},{4,20},{8,24},{12,28},{16,0},{20,4},{24,8},{28,12},{1,17},{... | collective-permute-start | bytes 1572872 | tf_op jit(solution)/shard_map/grads_4/ppermute | solution.py:20
  130.0 25.1 %collective-permute-start.38 = (bf16[128,2048]{1,0:T(8,128)(2,1)S(1)}, bf16[128,2048]{1,0:T(8,128)(2,1)S(1)}, u32[]{:S(2)}, u32[]{:S(2)}) collective-permute-start(bf16[128,2048]{1,0:T(8,128)(2,1)S(1)} %get-tuple-element.123), channel_id=1, source_target_pairs={{0,4},{4,0},{8,12},{12,8},{16,20},{20,16},{24,28},{28,24},{1,5},{5... | collective-permute-start | bytes 1572872 | tf_op jit(solution)/shard_map/grads_1/ppermute | solution.py:20
  130.8 25.7 %collective-permute-start.37 = (bf16[128,2048]{1,0:T(8,128)(2,1)S(1)}, bf16[128,2048]{1,0:T(8,128)(2,1)S(1)}, u32[]{:S(2)}, u32[]{:S(2)}) collective-permute-start(bf16[128,2048]{1,0:T(8,128)(2,1)S(1)} %get-tuple-element.122), channel_id=1, source_target_pairs={{0,20},{4,16},{8,28},{12,24},{16,4},{20,0},{24,12},{28,8},{1,21},{... | collective-permute-start | bytes 1572872 | tf_op jit(solution)/shard_map/grads_5/ppermute | solution.py:20
  132.2 25.6 %collective-permute-start.40 = (bf16[1024,256]{1,0:T(8,128)(2,1)S(1)}, bf16[1024,256]{1,0:T(8,128)(2,1)S(1)}, u32[]{:S(2)}, u32[]{:S(2)}) collective-permute-start(bf16[1024,256]{1,0:T(8,128)(2,1)S(1)} %add_pair.5.refs_11_), channel_id=1, source_target_pairs={{0,1},{1,0},{2,3},{3,2},{4,5},{5,4},{6,7},{7,6},{8,9},{9,8},{10,11... | collective-permute-start | bytes 1572872 | tf_op jit(solution)/shard_map/out_proj_1/ppermute | solution.py:20
  137.3 25.4 %collective-permute-start.42 = (bf16[1024,256]{1,0:T(8,128)(2,1)S(1)}, bf16[1024,256]{1,0:T(8,128)(2,1)S(1)}, u32[]{:S(2)}, u32[]{:S(2)}) collective-permute-start(bf16[1024,256]{1,0:T(8,128)(2,1)S(1)} %add_pair.6), channel_id=1, source_target_pairs={{0,2},{1,3},{2,0},{3,1},{4,6},{5,7},{6,4},{7,5},{8,10},{9,11},{10,... | collective-permute-start | bytes 1572872 | tf_op jit(solution)/shard_map/out_proj_2/ppermute | solution.py:20
  (13 other events, 18.5 us)
